TPU v7x, 32 devices: a whole 2x2x4 slice. The times are simulated.
32 devices in a mesh: slab: 8 (over y, x, core), grp: 4 (over z).
Axes of the slice: x: 2, y: 2, z: 4, core: 2. Of those that a mesh axis runs over, the one named last changes fastest.
Arguments:
- cloud_states: float32 [2, 16, 4, 64, 1024], P(None, 'grp', None, 'slab'), may hold values from -6 to 6
- cloud_shift: int32 [2], replicated, may hold values from 9 to 15, as said below
- boost_wave: int32 [2], replicated, may hold values from -6 to 6, as said below
Outputs:
- evolved: float32 [2, 16, 4, 64, 1024], P(None, 'grp', None, 'slab')
Inputs may be any that keep to these rules, and one draw needn't show every extreme that they name: `cloud_shift`: one of the two entries equals 15. `boost_wave`: the first entry is 6; the second is negative.
All inputs are finite; a program needn't handle non-finite values.
Results may differ from a plain program's by a relative error of at most 0.00002.
Values sent between devices are 32-bit elements; how exact they have to be, the bound alone decides.
No kernel may reach another device: no remote copies, remote signals or barrier semaphores. Data moves between devices by JAX's collectives and lax.ppermute only.
A program may use at most 64 MiB of HBM per device.

v0:
```python
import math

import jax
import jax.numpy as jnp
from jax import lax
from jax.sharding import PartitionSpec as P

NY = 32


stencil = (-49.0 / 18.0, 1.5, -0.15, 1.0 / 90.0)
coupling = 3.0
xi_factor = 1.2
chemical = 1.0
time_step = 0.1


def padded_2(x, sides, width):
    for axis, dim in sides:
        peers, length = (lax.axis_size(axis), x.shape[dim])
        up = [(i, (i + 1) % peers) for i in range(peers)]
        down = [(j, i) for i, j in up]
        last = lax.slice_in_dim(x, length - width, length, axis=dim)
        initial = lax.slice_in_dim(x, 0, width, axis=dim)
        before = lax.ppermute(last, axis, up)
        after = lax.ppermute(initial, axis, down)
        x = jnp.concatenate([before, x, after], axis=dim)
    return x


def shifted(x, axis, by):
    peers = lax.axis_size(axis)
    return lax.ppermute(x, axis, [(i, (i + by) % peers) for i in range(peers)])


def transverse(volume, row_width):
    cell_count = volume.shape[-1]
    column = lax.broadcasted_iota(jnp.int32, (cell_count,), 0) % row_width
    pad_spec = [(0, 0)] * (volume.ndim - 1) + [(3 * row_width, 3 * row_width)]
    padded = jnp.pad(volume, pad_spec)
    running = 2.0 * stencil[0] * volume
    base = 3 * row_width
    for offset in range(1, 4):
        for signed in (offset, -offset):
            across_rows = padded[
                ..., base + signed * row_width : base + signed * row_width + cell_count
            ]
            across_columns = padded[..., base + signed : base + signed + cell_count]
            inside = ((column + signed >= 0) & (column + signed < row_width)).astype(jnp.float32)
            running = running + stencil[offset] * (across_rows + across_columns * inside)
    return running


def along_depth(extended, planes):
    running = stencil[0] * extended[..., 3 : 3 + planes, :]
    for offset in range(1, 4):
        for signed in (offset, -offset):
            running = running + stencil[offset] * extended[..., 3 + signed : 3 + signed + planes, :]
    return running


def fields_of(totals):
    potential = xi_factor * jnp.square(jnp.cbrt(totals[0])) - chemical
    return jnp.stack([potential, -coupling * totals[1], -coupling * totals[2]])


def local_terms(states):
    particle_real = states[:, :, 0]
    particle_imag = states[:, :, 1]
    hole_real = states[:, :, 2]
    hole_imag = states[:, :, 3]
    density = jnp.sum(hole_real * hole_real + hole_imag * hole_imag, axis=(0, 1))
    pair_real = jnp.sum(particle_real * hole_real + particle_imag * hole_imag, axis=(0, 1))
    pair_imag = jnp.sum(particle_imag * hole_real - particle_real * hole_imag, axis=(0, 1))
    return jnp.stack([density, pair_real, pair_imag])


def potentials(states, total_states):
    partial_value = local_terms(states)
    totals = lax.psum(partial_value, "grp") / total_states
    return fields_of(totals)


def hamiltonian(states, fields):
    planes = states.shape[3]
    extended = padded_2(states, (("slab", 3),), 3)
    kinetic = -0.5 * (along_depth(extended, planes) + transverse(states, NY))
    potential = fields[0]
    gap_real = fields[1]
    gap_imag = fields[2]
    particle_real = states[:, :, 0]
    particle_imag = states[:, :, 1]
    hole_real = states[:, :, 2]
    hole_imag = states[:, :, 3]
    out_pr = (
        kinetic[:, :, 0] + potential * particle_real + gap_real * hole_real - gap_imag * hole_imag
    )
    out_pi = (
        kinetic[:, :, 1] + potential * particle_imag + gap_real * hole_imag + gap_imag * hole_real
    )
    out_hr = (
        gap_real * particle_real
        + gap_imag * particle_imag
        - kinetic[:, :, 2]
        - potential * hole_real
    )
    out_hi = (
        gap_real * particle_imag
        - gap_imag * particle_real
        - kinetic[:, :, 3]
        - potential * hole_imag
    )
    return jnp.stack([out_pr, out_pi, out_hr, out_hi], axis=2)


def advance(states, change, factor):
    return jnp.stack(
        [
            states[:, :, 0] + factor * change[:, :, 1],
            states[:, :, 1] - factor * change[:, :, 0],
            states[:, :, 2] + factor * change[:, :, 3],
            states[:, :, 3] - factor * change[:, :, 2],
        ],
        axis=2,
    )


def local(cloud_states, cloud_shift, boost_wave):
    slab_count = lax.axis_size("slab")
    slab_index = lax.axis_index("slab")
    _, per_group, _, planes, cell_count = cloud_states.shape
    total_states = per_group * lax.axis_size("grp")
    depth = planes * slab_count
    first_source = cloud_states[0]
    second_source = cloud_states[1]
    upper_one = shifted(first_source, "slab", 1)
    upper_two = shifted(first_source, "slab", 2)
    lower_one = shifted(second_source, "slab", -1)
    lower_two = shifted(second_source, "slab", -2)
    first_blocks = jnp.concatenate([upper_two, upper_one, first_source], axis=2)
    first_cloud = lax.dynamic_slice_in_dim(first_blocks, 2 * planes - cloud_shift[0], planes, 2)
    second_blocks = jnp.concatenate([second_source, lower_one, lower_two], axis=2)
    second_cloud = lax.dynamic_slice_in_dim(second_blocks, cloud_shift[1], planes, 2)
    placed = jnp.stack([first_cloud, second_cloud])
    global_plane = slab_index * planes + lax.broadcasted_iota(jnp.int32, (planes,), 0)
    phase_index = jnp.mod(boost_wave[:, None] * global_plane[None, :], depth)
    phases = 2.0 * math.pi / depth * phase_index.astype(jnp.float32)
    cosine_table = jnp.cos(phases)[:, None, :, None]
    sine_table = jnp.sin(phases)[:, None, :, None]
    particle_real = placed[:, :, 0]
    particle_imag = placed[:, :, 1]
    hole_real = placed[:, :, 2]
    hole_imag = placed[:, :, 3]
    boosted = jnp.stack(
        [
            particle_real * cosine_table - particle_imag * sine_table,
            particle_real * sine_table + particle_imag * cosine_table,
            hole_real * cosine_table + hole_imag * sine_table,
            hole_imag * cosine_table - hole_real * sine_table,
        ],
        axis=2,
    )
    change_now = hamiltonian(boosted, potentials(boosted, total_states))
    predicted = advance(boosted, change_now, time_step)
    change_next = hamiltonian(predicted, potentials(predicted, total_states))
    return advance(boosted, change_now + change_next, time_step / 2.0)


def solution(mesh):
    in_specs = (P(None, "grp", None, "slab", None), P(), P())
    out_specs = P(None, "grp", None, "slab", None)
    return jax.shard_map(local, mesh=mesh, in_specs=in_specs, out_specs=out_specs, check_vma=False)
```

profile of v0, /device:TPU:0, one launch (start us, length us, event | category | flops | bytes accessed | tf_op | source)
XLA Modules:
  0.0 140.7 jit_solution(12605973654560415989)
XLA Ops:
  6.5 1.3 slice_bitcast_fusion.1
  8.4 2.6 %collective-permute-start = (f32[4,4,8,1024]{3,2,1,0:T(8,128)S(1)}, f32[4,4,8,1024]{3,2,1,0:T(8,128)S(1)}, u32[]{:S(2)}, u32[]{:S(2)}) collective-permute-start(f32[4,4,8,1024]{3,2,1,0:T(8,128)S(1)} %get-tuple-element.52), channel_id=1, source_target_pairs={{0,8},{4,12},{8,16},{12,20},{16,24},{20,28},{24,0},{28,4},{1,9},{5... | collective-permute-start | bytes 1572872 | tf_op jit(solution)/shard_map/ppermute | solution.py:33
  10.9 1.0 collective-permute-start.3
  12.0 1.3 collective-permute-start.2
  13.3 0.7 fusion.168
  17.5 5.3 %collective-permute-done.1 = f32[4,4,8,1024]{3,2,1,0:T(8,128)S(1)} collective-permute-done((f32[4,4,8,1024]{3,2,1,0:T(8,128)S(1)}, f32[4,4,8,1024]{3,2,1,0:T(8,128)S(1)}, u32[]{:S(2)}, u32[]{:S(2)}) %collective-permute-start.1) | collective-permute-done | bytes 524320 | tf_op jit(solution)/shard_map/ppermute | solution.py:33
  22.8 1.8 %collective-permute-done = f32[4,4,8,1024]{3,2,1,0:T(8,128)S(1)} collective-permute-done((f32[4,4,8,1024]{3,2,1,0:T(8,128)S(1)}, f32[4,4,8,1024]{3,2,1,0:T(8,128)S(1)}, u32[]{:S(2)}, u32[]{:S(2)}) %collective-permute-start) | collective-permute-done | bytes 524320 | tf_op jit(solution)/shard_map/ppermute | solution.py:33
  24.9 11.5 %collective-permute-done.3 = f32[4,4,8,1024]{3,2,1,0:T(8,128)S(1)} collective-permute-done((f32[4,4,8,1024]{3,2,1,0:T(8,128)S(1)}, f32[4,4,8,1024]{3,2,1,0:T(8,128)S(1)}, u32[]{:S(2)}, u32[]{:S(2)}) %collective-permute-start.3) | collective-permute-done | bytes 524320 | tf_op jit(solution)/shard_map/ppermute | solution.py:33
  36.4 8.7 %collective-permute-done.2 = f32[4,4,8,1024]{3,2,1,0:T(8,128)S(1)} collective-permute-done((f32[4,4,8,1024]{3,2,1,0:T(8,128)S(1)}, f32[4,4,8,1024]{3,2,1,0:T(8,128)S(1)}, u32[]{:S(2)}, u32[]{:S(2)}) %collective-permute-start.2) | collective-permute-done | bytes 524320 | tf_op jit(solution)/shard_map/ppermute | solution.py:33
  45.3 1.2 add_reduce_fusion.2
  47.7 1.2 fusion.167
  48.9 2.8 %collective-permute-start.4 = (f32[2,4,4,3,1024]{4,3,1,0,2:T(4,128)}, f32[2,4,4,3,1024]{4,3,1,0,2:T(4,128)S(1)}, u32[]{:S(2)}, u32[]{:S(2)}) collective-permute-start(f32[2,4,4,3,1024]{4,3,1,0,2:T(4,128)} %get-tuple-element.50), channel_id=1, source_target_pairs={{4,0},{8,4},{12,8},{16,12},{20,16},{24,20},{28,24},{0,28},{5,1},{9... | collective-permute-start | bytes 1179656 | tf_op jit(solution)/shard_map/ppermute | solution.py:26
  51.7 31.9 %all-reduce.5.cloned.1.call-done = f32[3,8,1024]{2,1,0:T(8,128)} async-done(((f32[3,8,1024]{2,1,0:T(8,128)}), f32[3,8,1024]{2,1,0:T(8,128)}) %all-reduce.5.cloned.1.call-update) | async-done | bytes 98320 | tf_op jit(solution)/shard_map/psum | solution.py:80
  83.7 0.9 broadcast_multiply_fusion.1
  85.2 3.4 %copy_multiply_fusion.1 = f32[2,4,4,8,1024]{4,3,2,1,0:T(8,128)S(1)} fusion(f32[2,4,4,8,1024]{4,3,1,0,2:T(8,128)S(1)} %pad_maximum_fusion.2, f32[2,4,4,11,1024]{4,3,1,0,2:T(8,128)S(1)} %get-tuple-element.49, f32[2,4,4,11,1024]{4,3,1,0,2:T(8,128)S(1)} %get-tuple-element.48, f32[1024]{0:T(1024)S(1)} %get-tuple-element.68, f32[1024]{0:T(1024)S(1)} %get-tuple-element.69, ...), kind=kLoop, calls=%fused_computation.120 | loop fusion | flops 10485760 | bytes 8413184 | tf_op jit(solution)/shard_map/mul | solution.py:87
  88.7 1.2 bitcast_add_fusion.5
  90.4 0.7 pad_maximum_fusion.8
  91.1 1.3 fusion.166
  92.9 32.2 %all-reduce.7.cloned.1.call-done = f32[3,8,1024]{2,1,0:T(8,128)} async-done(((f32[3,8,1024]{2,1,0:T(8,128)}), f32[3,8,1024]{2,1,0:T(8,128)}) %all-reduce.7.cloned.1.call-update) | async-done | bytes 98320 | tf_op jit(solution)/shard_map/psum | solution.py:80
  125.1 0.9 broadcast_multiply_fusion
  126.1 1.8 %pad_maximum_fusion.1 = (f32[2,4,4,11,1024]{4,3,1,0,2:T(8,128)S(1)}, f32[2,4,4,11,1024]{4,3,1,0,2:T(8,128)S(1)}) fusion(f32[2,4,4,3,1024]{4,3,1,0,2:T(4,128)} %collective-permute-done.6, f32[2,4,1,8,1024]{4,3,1,0,2:T(8,128)S(1)} %bitcast.188, f32[2,4,1,8,1024]{4,3,1,0,2:T(8,128)S(1)} %bitcast.186, f32[2,4,1,8,1024]{4,3,1,0,2:T(8,128)S(1)} %bitcast.190, ...), kind=kLoop, calls=%fused_computation.2 | loop fusion | flops 2883584 | bytes 4718592 | tf_op jit(solution)/shard_map/concatenate | solution.py:27
  127.9 3.4 %copy_multiply_fusion = f32[2,4,4,8,1024]{4,3,2,1,0:T(8,128)S(1)} fusion(f32[2,4,4,8,1024]{4,3,1,0,2:T(8,128)S(1)} %pad_maximum_fusion.4, f32[2,4,4,11,1024]{4,3,1,0,2:T(8,128)S(1)} %get-tuple-element.45, f32[2,4,4,11,1024]{4,3,1,0,2:T(8,128)S(1)} %get-tuple-element.44, f32[1024]{0:T(1024)S(1)} %get-tuple-element.68, f32[1024]{0:T(1024)S(1)} %get-tuple-element.69, ...), kind=kLoop, calls=%fused_computation.119 | loop fusion | flops 10485760 | bytes 8413184 | tf_op jit(solution)/shard_map/mul | solution.py:87
  131.6 0.7 copy-done
  132.7 1.1 pad_maximum_fusion.5
  (50 shorter events, 4.7 us)
Async XLA Ops:
  6.5 6.8 %copy-start.7 = (s32[2]{0:T(128)S(1)}, s32[2]{0:T(128)}, u32[]{:S(2)}) copy-start(s32[2]{0:T(128)} %param.4) | copy-start | bytes 28
  6.5 10.8 %copy-start.8 = (s32[2]{0:T(128)S(1)}, s32[2]{0:T(128)}, u32[]{:S(2)}) copy-start(s32[2]{0:T(128)} %param.5) | copy-start | bytes 28
  6.5 77.1 %all-reduce.5.cloned.1.call-start = ((), (), s32[]{:S(2)}) async-start(), calls=%async_computation | async-start | bytes 196608 | tf_op jit(solution)/shard_map/psum | solution.py:80
  7.9 15.0 %collective-permute-start.1 = (f32[4,4,8,1024]{3,2,1,0:T(8,128)S(1)}, f32[4,4,8,1024]{3,2,1,0:T(8,128)S(1)}, u32[]{:S(2)}, u32[]{:S(2)}) collective-permute-start(f32[4,4,8,1024]{3,2,1,0:T(8,128)S(1)} %get-tuple-element.52), channel_id=1, source_target_pairs={{0,4},{4,8},{8,12},{12,16},{16,20},{20,24},{24,28},{28,0},{1,5},{5... | collective-permute-start | bytes 1572872 | tf_op jit(solution)/shard_map/ppermute | solution.py:33
  8.4 16.3 %collective-permute-start = (f32[4,4,8,1024]{3,2,1,0:T(8,128)S(1)}, f32[4,4,8,1024]{3,2,1,0:T(8,128)S(1)}, u32[]{:S(2)}, u32[]{:S(2)}) collective-permute-start(f32[4,4,8,1024]{3,2,1,0:T(8,128)S(1)} %get-tuple-element.52), channel_id=1, source_target_pairs={{0,8},{4,12},{8,16},{12,20},{16,24},{20,28},{24,0},{28,4},{1,9},{5... | collective-permute-start | bytes 1572872 | tf_op jit(solution)/shard_map/ppermute | solution.py:33
  10.9 25.4 %collective-permute-start.3 = (f32[4,4,8,1024]{3,2,1,0:T(8,128)S(1)}, f32[4,4,8,1024]{3,2,1,0:T(8,128)S(1)}, u32[]{:S(2)}, u32[]{:S(2)}) collective-permute-start(f32[4,4,8,1024]{3,2,1,0:T(8,128)S(1)} %get-tuple-element.53), channel_id=1, source_target_pairs={{0,24},{4,28},{8,0},{12,4},{16,8},{20,12},{24,16},{28,20},{1,25},{... | collective-permute-start | bytes 1572872 | tf_op jit(solution)/shard_map/ppermute | solution.py:33
  12.0 33.1 %collective-permute-start.2 = (f32[4,4,8,1024]{3,2,1,0:T(8,128)S(1)}, f32[4,4,8,1024]{3,2,1,0:T(8,128)S(1)}, u32[]{:S(2)}, u32[]{:S(2)}) collective-permute-start(f32[4,4,8,1024]{3,2,1,0:T(8,128)S(1)} %get-tuple-element.53), channel_id=1, source_target_pairs={{0,28},{4,0},{8,4},{12,8},{16,12},{20,16},{24,20},{28,24},{1,29},{... | collective-permute-start | bytes 1572872 | tf_op jit(solution)/shard_map/ppermute | solution.py:33
  47.5 77.6 %all-reduce.7.cloned.1.call-start = ((), (), s32[]{:S(2)}) async-start(), calls=%async_computation.1 | async-start | bytes 196608 | tf_op jit(solution)/shard_map/psum | solution.py:80
  48.9 35.7 %collective-permute-start.4 = (f32[2,4,4,3,1024]{4,3,1,0,2:T(4,128)}, f32[2,4,4,3,1024]{4,3,1,0,2:T(4,128)S(1)}, u32[]{:S(2)}, u32[]{:S(2)}) collective-permute-start(f32[2,4,4,3,1024]{4,3,1,0,2:T(4,128)} %get-tuple-element.50), channel_id=1, source_target_pairs={{4,0},{8,4},{12,8},{16,12},{20,16},{24,20},{28,24},{0,28},{5,1},{9... | collective-permute-start | bytes 1179656 | tf_op jit(solution)/shard_map/ppermute | solution.py:26
  51.7 32.9 %collective-permute-start.5 = (f32[2,4,4,3,1024]{4,3,1,0,2:T(4,128)}, f32[2,4,4,3,1024]{4,3,1,0,2:T(4,128)S(1)}, u32[]{:S(2)}, u32[]{:S(2)}) collective-permute-start(f32[2,4,4,3,1024]{4,3,1,0,2:T(4,128)} %get-tuple-element.51), channel_id=1, source_target_pairs={{0,4},{4,8},{8,12},{12,16},{16,20},{20,24},{24,28},{28,0},{1,5},{5... | collective-permute-start | bytes 1179656 | tf_op jit(solution)/shard_map/ppermute | solution.py:25
  88.6 1.2 copy-start.3
  88.6 1.2 copy-start.4
  88.6 1.2 copy-start.5
  88.6 1.3 copy-start.6
  92.4 33.7 %collective-permute-start.6 = (f32[2,4,4,3,1024]{4,3,1,0,2:T(4,128)}, f32[2,4,4,3,1024]{4,3,1,0,2:T(4,128)}, u32[]{:S(2)}, u32[]{:S(2)}) collective-permute-start(f32[2,4,4,3,1024]{4,3,1,0,2:T(4,128)} %get-tuple-element.46), channel_id=1, source_target_pairs={{4,0},{8,4},{12,8},{16,12},{20,16},{24,20},{28,24},{0,28},{5,1},{9... | collective-permute-start | bytes 1179656 | tf_op jit(solution)/shard_map/ppermute | solution.py:26
  92.4 33.7 %collective-permute-start.7 = (f32[2,4,4,3,1024]{4,3,1,0,2:T(4,128)}, f32[2,4,4,3,1024]{4,3,1,0,2:T(4,128)}, u32[]{:S(2)}, u32[]{:S(2)}) collective-permute-start(f32[2,4,4,3,1024]{4,3,1,0,2:T(4,128)} %get-tuple-element.47), channel_id=1, source_target_pairs={{0,4},{4,8},{8,12},{12,16},{16,20},{20,24},{24,28},{28,0},{1,5},{5... | collective-permute-start | bytes 1179656 | tf_op jit(solution)/shard_map/ppermute | solution.py:25
  131.3 1.0 copy-start
  131.3 1.0 copy-start.1
  131.3 1.1 copy-start.2
Sparse Core Ops, SparseCore 0:
  47.7 35.9 all-reduce.4
  91.1 33.9 all-reduce.6
where the time goes:
time: 141 us
  waiting for transfers between devices  91.6 us (65%)
  other arithmetic  17.9 us (13%)
  between operations  17 us (12%)
  starting transfers between devices  8.78 us (6%)
  local copies, waits for them, and re-layouts  5.4 us (4%)
    psum x2, waiting for transfers between devices, potentials(): totals = lax.psum(partial_value, 'grp') / total_states  64.2 us
    ppermute x4, waiting for transfers between devices, shifted(): return lax.ppermute(x, axis, [(i, (i + by) % peers) for i in range(peers)])  27.3 us
    mul x2, other arithmetic, hamiltonian(): kinetic = -0.5 * (along_depth(extended, planes) + transverse(states, NY))  6.85 us
    ppermute x4, starting transfers between devices, shifted(): return lax.ppermute(x, axis, [(i, (i + by) % peers) for i in range(peers)])  5.41 us
  transfers between devices with their start and end apart: 10, of which 6 were waited for; matrix products, arithmetic and copies ran while one was open for 4% of the time, Pallas kernels for 0%

commit v1 on v0

v1 whole, which is shorter than its diff:
```python
import functools
import math

import jax
import jax.numpy as jnp
import numpy as np
from jax import lax
from jax.experimental import pallas as pl
from jax.experimental.pallas import tpu as pltpu
from jax.sharding import PartitionSpec as P

NY = 32
LANES = 128
SUBS = 8
HALO = 3
REACH = 2 * HALO
CHUNKS = 2
VMEM_BYTES = 40 * 1024 * 1024

stencil = (-49.0 / 18.0, 1.5, -0.15, 1.0 / 90.0)
coupling = 3.0
xi_factor = 1.2
chemical = 1.0
time_step = 0.1

VMEM = pl.BlockSpec(memory_space=pltpu.VMEM)
SMEM = pl.BlockSpec(memory_space=pltpu.SMEM)


def params():
    return pltpu.CompilerParams(vmem_limit_bytes=VMEM_BYTES)


def moved(x, axis, by):
    peers = lax.axis_size(axis)
    return lax.ppermute(x, axis, [(i, (i + by) % peers) for i in range(peers)])


def swapped(x):
    peers = lax.axis_size("slab")
    return lax.ppermute(x, "slab", [(i, i ^ 1) for i in range(peers)])


def transverse_weights():
    whole = {0: -980.0, 1: 270.0, 2: -27.0, 3: 2.0}
    rows = LANES // NY
    weights = np.zeros((LANES, 3 * LANES), np.float32)
    for a in range(LANES):
        xa, ya = divmod(a, NY)
        for b in range(LANES):
            xb, yb = divmod(b, NY)
            for part, distance in ((0, xb + rows - xa), (1, xb - xa), (2, xb - rows - xa)):
                if ya == yb and abs(distance) <= HALO:
                    weights[a, part * LANES + b] += whole[abs(distance)]
            if xa == xb and 0 < abs(ya - yb) <= HALO:
                weights[a, LANES + b] += whole[abs(ya - yb)]
    return np.concatenate([weights, weights]).astype(jnp.bfloat16)


def phase(wave, first, depth):
    z = first + lax.broadcasted_iota(jnp.int32, (SUBS, LANES), 0)
    index = jnp.bitwise_and(wave * z, depth - 1)
    angle = (2.0 * math.pi / depth) * index.astype(jnp.float32)
    return jnp.cos(angle), jnp.sin(angle)


def densities(ur, ui, vr, vi):
    return vr * vr + vi * vi, ur * vr + ui * vi, ui * vr - ur * vi


def fields_of(n, kr, ki, scale):
    n = n * scale
    safe = jnp.where(n > 0.0, n, 1.0)
    power = jnp.where(n > 0.0, jnp.exp((2.0 / 3.0) * jnp.log(safe)), 0.0)
    return xi_factor * power - chemical, (-coupling * scale) * kr, (-coupling * scale) * ki


def local_part(field, ur, ui, vr, vi):
    potential, gap_real, gap_imag = field
    return (
        potential * ur + gap_real * vr - gap_imag * vi,
        potential * ui + gap_real * vi + gap_imag * vr,
        gap_real * ur + gap_imag * ui - potential * vr,
        gap_real * ui - gap_imag * ur - potential * vi,
    )


def raw_density_kernel(parts, me_ref, x_ref, *refs):
    outs, total = refs[:-1], refs[-1]
    clouds, states, _, planes, cells = x_ref.shape
    for j in range(clouds):
        for t in range(cells // LANES):
            lanes = pl.ds(t * LANES, LANES)
            sums = [jnp.zeros((planes, LANES), jnp.float32)] * 3
            for s in range(states):
                terms = densities(*[x_ref[j, s, k, :, lanes] for k in range(4)])
                sums = [a + b for a, b in zip(sums, terms)]
            for f in range(3):
                total[j, f, :, lanes] = sums[f]
    width = cells // parts
    for d in range(parts):
        first = pl.multiple_of(lax.rem(me_ref[0] + d, parts) * width, width)
        outs[d][...] = total[:, :, :, pl.ds(first, width)]


def raw_density(x, me, parts):
    clouds, _, _, planes, cells = x.shape
    shape = jax.ShapeDtypeStruct((clouds, 3, planes, cells // parts), jnp.float32)
    return pl.pallas_call(
        functools.partial(raw_density_kernel, parts),
        out_shape=[shape] * parts,
        in_specs=[SMEM, VMEM],
        out_specs=[VMEM] * parts,
        scratch_shapes=[pltpu.VMEM((clouds, 3, planes, cells), jnp.float32)],
        compiler_params=params(),
        name="raw_density",
    )(me, x)


def placed_fields_kernel(depth, scale, where_ref, shift_ref, wave_ref, *refs):
    first_refs, second_refs = refs[0:4], refs[4:8]
    out_ref, held = refs[8], refs[9]
    planes = first_refs[0].shape[1]
    width = first_refs[0].shape[2]
    slab = where_ref[0]
    for j, slots in enumerate((first_refs, second_refs)):
        for q, slot in enumerate(slots):
            first = (slab - 3 + q) * planes + shift_ref[0] if j == 0 else (slab + q) * planes - shift_ref[1]
            cos, sin = phase(2 * wave_ref[j], first, depth)
            for t in range(width // LANES):
                lanes = pl.ds(t * LANES, LANES)
                kr, ki = slot[1, :, lanes], slot[2, :, lanes]
                layers = pl.ds(q * planes, planes)
                held[j, 0, layers, lanes] = slot[0, :, lanes]
                held[j, 1, layers, lanes] = kr * cos - ki * sin
                held[j, 2, layers, lanes] = kr * sin + ki * cos
    count = out_ref.shape[1]
    start_first = 3 * planes - HALO - shift_ref[0]
    start_second = shift_ref[1] - HALO
    rows = held.shape[2]
    totals = [
        pltpu.roll(held[0, f], rows - start_first, 0)[:count] + pltpu.roll(held[1, f], rows - start_second, 0)[:count] for f in range(3)
    ]
    for f, field in enumerate(fields_of(*totals, scale)):
        out_ref[f] = field


def placed_fields(where, shift, wave, first, second, depth, scale):
    planes, width = first[0].shape[1:]
    return pl.pallas_call(
        functools.partial(placed_fields_kernel, depth, scale),
        out_shape=jax.ShapeDtypeStruct((3, planes + 8, width), jnp.float32),
        in_specs=[SMEM] * 3 + [VMEM] * 8,
        out_specs=VMEM,
        scratch_shapes=[pltpu.VMEM((2, 3, 4 * planes, width), jnp.float32)],
        compiler_params=params(),
        name="placed_fields",
    )(where, shift, wave, *first, *second)


def transverse(x, weights):
    rows = x.shape[0]
    flat = x.reshape(rows * SUBS, LANES)
    high = flat.astype(jnp.bfloat16)
    low = (flat - high.astype(jnp.float32)).astype(jnp.bfloat16)
    product = jnp.dot(jnp.concatenate([high, low], axis=1), weights, preferred_element_type=jnp.float32)
    sub = lax.broadcasted_iota(jnp.int32, (rows * SUBS, LANES), 0) % SUBS
    up = pltpu.roll(product[:, :LANES].reshape(rows, SUBS, LANES), 1, 1).reshape(rows * SUBS, LANES)
    down = pltpu.roll(product[:, 2 * LANES :].reshape(rows, SUBS, LANES), SUBS - 1, 1).reshape(rows * SUBS, LANES)
    result = product[:, LANES : 2 * LANES] + jnp.where(sub > 0, up, 0.0) + jnp.where(sub < SUBS - 1, down, 0.0)
    return result.reshape(rows, SUBS, LANES)


def kinetic(layers, weights):
    count = layers.shape[0] - 2 * HALO
    inner = layers[HALO : HALO + count]
    along = stencil[0] * inner
    for j in range(1, HALO + 1):
        along = along + stencil[j] * (layers[HALO - j : HALO - j + count] + layers[HALO + j : HALO + j + count])
    return -0.5 * along + (-0.5 / 180.0) * transverse(inner, weights)


def gather_kernel(depth, where_ref, shift_ref, wave_ref, weights_ref, own_ref, partner_ref, extra_ref, recv_first, recv_second,
                  precv_first, precv_second, boosted_ref, base_ref, window):
    slab = where_ref[0]
    even = lax.rem(slab, 2) == 0
    planes = own_ref.shape[3]
    states = own_ref.shape[1]
    tiles = own_ref.shape[4] // LANES
    count = boosted_ref.shape[3]

    def turned(u_re, u_im, v_re, v_im, cos, sin):
        return u_re * cos - u_im * sin, u_re * sin + u_im * cos, v_re * cos + v_im * sin, v_im * cos - v_re * sin

    for j in range(2):
        phases = []
        for q in range(4):
            first = (slab - 3 + q) * planes + shift_ref[0] if j == 0 else (slab + q) * planes - shift_ref[1]
            phases.append(phase(wave_ref[j], first, depth))
        start = 3 * planes - REACH - shift_ref[0] if j == 0 else shift_ref[1] - REACH

        def one_state(s, _):
            def fill(q, read):
                cos, sin = phases[q]
                for t in range(tiles):
                    lanes = pl.ds(t * LANES, LANES)
                    for k, value in enumerate(turned(*[read(k, lanes) for k in range(4)], cos, sin)):
                        window[k, pl.ds(q * planes, planes), t, :] = value

            def fill_extra(q, layer):
                cos, sin = phases[q]
                for n in range(extra_ref.shape[2]):
                    inside = layer % planes + n
                    c = jnp.broadcast_to(cos[inside : inside + 1], (SUBS, LANES))
                    d = jnp.broadcast_to(sin[inside : inside + 1], (SUBS, LANES))
                    for k, value in enumerate(turned(*[extra_ref[s, k, n] for k in range(4)], c, d)):
                        window[k, layer + n] = value

            own = lambda k, lanes: own_ref[j, s, k, :, lanes]
            partner = lambda k, lanes: partner_ref[j, s, k, :, lanes]
            recv = lambda k, lanes: (recv_first if j == 0 else recv_second)[s, k, :, lanes]
            precv = lambda k, lanes: (precv_first if j == 0 else precv_second)[s, k, :, lanes]
            far = 0 if j == 0 else 3
            near = 2 if j == 0 else 1
            fill(3 - far, own)
            fill(3 - near, recv)

            @pl.when(even if j == 0 else jnp.logical_not(even))
            def _():
                fill(near, precv)
                fill_extra(far, planes - extra_ref.shape[2] if j == 0 else 3 * planes)

            @pl.when(jnp.logical_not(even) if j == 0 else even)
            def _():
                fill(near, partner)
                fill(far, precv)

            kin = []
            values = []
            for k in range(4):
                layers = window[k, pl.ds(start, count + 2 * HALO)]
                values.append(layers[HALO : HALO + count])
                kin.append(kinetic(layers, weights_ref[...]))
            for k in range(4):
                boosted_ref[j, s, k] = values[k]
            base_ref[j, s, 0] = values[0] + time_step * kin[1]
            base_ref[j, s, 1] = values[1] - time_step * kin[0]
            base_ref[j, s, 2] = values[2] - time_step * kin[3]
            base_ref[j, s, 3] = values[3] + time_step * kin[2]
            return 0

        lax.fori_loop(0, states, one_state, 0)


def gather(where, shift, wave, weights, x, partner, extra, received, exchanged, chunk, depth):
    _, per_group, _, planes, cells = x.shape
    states = per_group // CHUNKS
    count = planes + 2 * HALO
    shape = jax.ShapeDtypeStruct((2, states, 4, count, SUBS, LANES), jnp.float32)
    five = lambda block: pl.BlockSpec(block, lambda i: (0, chunk, 0, 0, 0))
    whole = lambda a: pl.BlockSpec(a.shape, lambda i: (0,) * a.ndim)
    extra_spec = pl.BlockSpec((states, *extra.shape[1:]), lambda i: (chunk, 0, 0, 0, 0))
    operands = (*received, *exchanged)
    return pl.pallas_call(
        functools.partial(gather_kernel, depth),
        out_shape=[shape] * 2,
        grid=(1,),
        in_specs=[SMEM] * 3 + [whole(weights), five((2, states, 4, planes, cells)), five((2, states, 4, planes, cells)), extra_spec]
        + [whole(a) for a in operands],
        out_specs=[pl.BlockSpec(shape.shape, lambda i: (0,) * 6)] * 2,
        scratch_shapes=[pltpu.VMEM((4, 4 * planes, SUBS, LANES), jnp.float32)],
        compiler_params=params(),
        name="gather",
    )(where, shift, wave, weights, x, partner, extra, *operands)


def spread_fields(me_ref, parts, field_refs, fields):
    count = fields.shape[1]
    width = field_refs[0].shape[2]
    tiles = width // LANES
    for d, ref in enumerate(field_refs):
        part = lax.rem(me_ref[0] + parts - d, parts)
        for own in range(parts):
            @pl.when(part == own)
            def _():
                for f in range(3):
                    for t in range(tiles):
                        fields[f, :, own * tiles + t, :] = ref[f, 0:count, t * LANES : (t + 1) * LANES]


def density_kernel(parts, chunks, me_ref, *refs):
    field_refs = refs[:parts]
    boosted_refs = refs[parts : parts + chunks]
    base_refs = refs[parts + chunks : parts + 2 * chunks]
    out_ref, fields, sums = refs[parts + 2 * chunks :]
    spread_fields(me_ref, parts, field_refs, fields)
    planes = sums.shape[1]
    states = boosted_refs[0].shape[1]
    for z in range(planes):
        field = [fields[f, HALO + z] for f in range(3)]
        total = [jnp.zeros((SUBS, LANES), jnp.float32)] * 3
        for boosted, base in zip(boosted_refs, base_refs):
            for j in range(2):
                for s in range(states):
                    part = local_part(field, *[boosted[j, s, k, HALO + z] for k in range(4)])
                    pr = base[j, s, 0, HALO + z] + time_step * part[1]
                    pi = base[j, s, 1, HALO + z] - time_step * part[0]
                    hr = base[j, s, 2, HALO + z] + time_step * part[3]
                    hi = base[j, s, 3, HALO + z] - time_step * part[2]
                    total = [a + b for a, b in zip(total, densities(pr, pi, hr, hi))]
        for f in range(3):
            sums[f, z] = total[f]
    for f in range(3):
        for t in range(SUBS):
            out_ref[f, :, t * LANES : (t + 1) * LANES] = sums[f, :, t, :]


def density(me, fields, boosted, base, planes):
    parts, chunks = len(fields), len(boosted)
    return pl.pallas_call(
        functools.partial(density_kernel, parts, chunks),
        out_shape=jax.ShapeDtypeStruct((3, planes, SUBS * LANES), jnp.float32),
        in_specs=[SMEM] + [VMEM] * (parts + 2 * chunks),
        out_specs=VMEM,
        scratch_shapes=[
            pltpu.VMEM((3, planes + 2 * HALO, SUBS, LANES), jnp.float32),
            pltpu.VMEM((3, planes, SUBS, LANES), jnp.float32),
        ],
        compiler_params=params(),
        name="density",
    )(me, *fields, *boosted, *base)


def free_kernel(parts, chunks, me_ref, weights_ref, *refs):
    field_refs = refs[:parts]
    boosted_refs = refs[parts : parts + chunks]
    base_refs = refs[parts + chunks : parts + 2 * chunks]
    free_ref, predicted_ref, fields, window, turned = refs[parts + 2 * chunks :]
    spread_fields(me_ref, parts, field_refs, fields)
    planes = free_ref.shape[3]
    states = boosted_refs[0].shape[1]
    inner = pl.ds(HALO, planes)
    for c, (boosted, base) in enumerate(zip(boosted_refs, base_refs)):
        for j in range(2):
            def one_state(s, _):
                for z in range(planes + 2 * HALO):
                    field = [fields[f, z] for f in range(3)]
                    part = local_part(field, *[boosted[j, s, k, z] for k in range(4)])
                    window[0, z] = base[j, s, 0, z] + time_step * part[1]
                    window[1, z] = base[j, s, 1, z] - time_step * part[0]
                    window[2, z] = base[j, s, 2, z] + time_step * part[3]
                    window[3, z] = base[j, s, 3, z] - time_step * part[2]
                kin = [kinetic(window[k], weights_ref[...]) for k in range(4)]
                mean = [0.5 * (boosted[j, s, k, inner] + window[k, inner]) for k in range(4)]
                half = 0.5 * time_step
                turned[0] = mean[0] + half * kin[1]
                turned[1] = mean[1] - half * kin[0]
                turned[2] = mean[2] - half * kin[3]
                turned[3] = mean[3] + half * kin[2]
                for k in range(4):
                    for t in range(SUBS):
                        lanes = pl.ds(t * LANES, LANES)
                        free_ref[j, c * states + s, k, :, lanes] = turned[k, :, t, :]
                        predicted_ref[j, c * states + s, k, :, lanes] = window[k, inner, t, :]
                return 0

            lax.fori_loop(0, states, one_state, 0)


def free_part(me, weights, fields, boosted, base, shape, planes):
    parts, chunks = len(fields), len(boosted)
    out = jax.ShapeDtypeStruct(shape, jnp.float32)
    return pl.pallas_call(
        functools.partial(free_kernel, parts, chunks),
        out_shape=[out] * 2,
        in_specs=[SMEM] + [VMEM] * (1 + parts + 2 * chunks),
        out_specs=[VMEM] * 2,
        scratch_shapes=[
            pltpu.VMEM((3, planes + 2 * HALO, SUBS, LANES), jnp.float32),
            pltpu.VMEM((4, planes + 2 * HALO, SUBS, LANES), jnp.float32),
            pltpu.VMEM((4, planes, SUBS, LANES), jnp.float32),
        ],
        compiler_params=params(),
        name="free_part",
    )(me, weights, *fields, *boosted, *base)


def last_kernel(scale, *refs):
    partial_refs = refs[:-4]
    free_ref, predicted_ref, out_ref, fields = refs[-4:]

    @pl.when(pl.program_id(0) == 0)
    def _():
        totals = []
        for f in range(3):
            total = partial_refs[0][f]
            for ref in partial_refs[1:]:
                total = total + ref[f]
            totals.append(total)
        for f, field in enumerate(fields_of(*totals, scale)):
            fields[f] = field

    half = 0.5 * time_step
    for t in range(free_ref.shape[-1] // LANES):
        lanes = pl.ds(t * LANES, LANES)
        field = [fields[f, :, lanes] for f in range(3)]
        for s in range(free_ref.shape[1]):
            part = local_part(field, *[predicted_ref[0, s, k, :, lanes] for k in range(4)])
            out_ref[0, s, 0, :, lanes] = free_ref[0, s, 0, :, lanes] + half * part[1]
            out_ref[0, s, 1, :, lanes] = free_ref[0, s, 1, :, lanes] - half * part[0]
            out_ref[0, s, 2, :, lanes] = free_ref[0, s, 2, :, lanes] + half * part[3]
            out_ref[0, s, 3, :, lanes] = free_ref[0, s, 3, :, lanes] - half * part[2]


def last_part(partials, free, predicted, scale):
    shape = free.shape
    whole = pl.BlockSpec(partials[0].shape, lambda i: (0, 0, 0))
    block = pl.BlockSpec((1, *shape[1:]), lambda i: (i, 0, 0, 0, 0))
    return pl.pallas_call(
        functools.partial(last_kernel, scale),
        out_shape=jax.ShapeDtypeStruct(shape, jnp.float32),
        grid=(shape[0],),
        in_specs=[whole] * len(partials) + [block] * 2,
        out_specs=block,
        scratch_shapes=[pltpu.VMEM(partials[0].shape, jnp.float32)],
        compiler_params=params(),
        name="last_part",
    )(*partials, free, predicted)


def local(weights, cloud_states, cloud_shift, boost_wave):
    slab_count, group_count = lax.axis_size("slab"), lax.axis_size("grp")
    _, per_group, _, planes, cells = cloud_states.shape
    depth = planes * slab_count
    scale = 1.0 / (per_group * group_count)
    few = group_count <= 4 and cells % (group_count * LANES) == 0
    parts = group_count if few else 1
    slab = lax.axis_index("slab")
    where = slab.astype(jnp.int32).reshape(1)
    me = lax.axis_index("grp").astype(jnp.int32).reshape(1)

    own = raw_density(cloud_states, me, parts)
    if few:
        summed = own[0]
        for d in range(1, parts):
            summed = summed + moved(own[d], "grp", d)
    else:
        summed = lax.psum(own[0], "grp")

    per_chunk = per_group // CHUNKS
    received = []
    for c in range(CHUNKS):
        states = slice(c * per_chunk, (c + 1) * per_chunk)
        received.append((moved(cloud_states[0, states], "slab", 2), moved(cloud_states[1, states], "slab", -2)))
    partner = swapped(cloud_states)
    odd = lax.rem(slab, 2) == 1
    extra_layers = REACH - 1
    leaving = jnp.where(odd, cloud_states[0, :, :, planes - extra_layers :], cloud_states[1, :, :, :extra_layers])
    leaving = leaving.reshape(per_group, 4, extra_layers, SUBS, LANES)
    extra = lax.ppermute(leaving, "slab", [(i, (i + 3) % slab_count if i % 2 else (i - 3) % slab_count) for i in range(slab_count)])

    first = [moved(summed[0], "slab", d) for d in (3, 2, 1)] + [summed[0]]
    second = [summed[1]] + [moved(summed[1], "slab", -d) for d in (1, 2, 3)]
    piece = placed_fields(where, cloud_shift, boost_wave, first, second, depth, scale)
    fields = [piece] + [moved(piece, "grp", d) for d in range(1, parts)]

    boosted, base = [], []
    for c in range(CHUNKS):
        exchanged = [swapped(r) for r in received[c]]
        b, a = gather(where, cloud_shift, boost_wave, weights, cloud_states, partner, extra, received[c], exchanged, c, depth)
        boosted.append(b)
        base.append(a)
    partial = density(me, fields, boosted, base, planes)
    if few:
        partials = [partial] + [moved(partial, "grp", d) for d in range(1, parts)]
    else:
        partials = [lax.psum(partial, "grp")]
    free, predicted = free_part(me, weights, fields, boosted, base, cloud_states.shape, planes)
    return last_part(partials, free, predicted, scale)


def solution(mesh):
    states = P(None, "grp", None, "slab", None)
    weights = transverse_weights()
    step = jax.shard_map(local, mesh=mesh, in_specs=(P(), states, P(), P()), out_specs=states, check_vma=False)
    return lambda cloud_states, cloud_shift, boost_wave: step(weights, cloud_states, cloud_shift, boost_wave)
```

time: 141 us -> 69.3 us (0.49)
  waiting for transfers between devices: 91.6 us -> 21.8 us
  starting transfers between devices: 8.78 us -> 29.5 us
  between operations: 17 us -> 0.18 us
  other arithmetic: 17.9 us -> 1.28 us
  Pallas kernels: 0 us -> 14.7 us
  local copies, waits for them, and re-layouts: 5.4 us -> 1.37 us
    psum x2 -> x0, waiting for transfers between devices: 64.2 us -> none  [potentials(): totals = lax.psum(partial_value, 'grp') / total_states]
    ppermute x8 -> x25, starting transfers between devices: 8.73 us -> 29.5 us  [the longest x19 25.9 us: moved(): return lax.ppermute(x, axis, [(i, (i + by) % peers) for i in range(peers)])]
    pallas_call x0 -> x7, Pallas kernels: none -> 14.7 us  [the longest x2 7.19 us: gather(): pl.pallas_call(functools.partial(gather_kernel, depth), out_shape=[shape]...]
    mul x3 -> x0, other arithmetic: 6.9 us -> none  [the longest x2 6.85 us: hamiltonian(): kinetic = -0.5 * (along_depth(extended, planes) + transverse(states, NY))]
    ppermute x8 -> x25, waiting for transfers between devices: 27.4 us -> 21.8 us  [the longest x19 21.8 us: moved(): return lax.ppermute(x, axis, [(i, (i + by) % peers) for i in range(peers)])]
    slice x3 -> x0, local copies, waits for them, and re-layouts: 3.16 us -> none  [the longest x2 2.5 us: padded_2(): initial = lax.slice_in_dim(x, 0, width, axis=dim)]
    another operation x7 -> x0, other arithmetic: 3.01 us -> none  [the longest x2 1.29 us: local_terms(): return jnp.stack([density, pair_real, pair_imag])]
    concatenate x2 -> x0, other arithmetic: 2.31 us -> none  [padded_2(): x = jnp.concatenate([before, x, after], axis=dim)]
  transfers between devices with their start and end apart: 10 -> 25, of which waited for: 6 -> 9; matrix products, arithmetic and copies ran while one was open for 4% -> 4% of each run, Pallas kernels for 0% -> 17%
where the time goes in v1:
time: 69.3 us; the launch traced here: 68.9 us
  starting transfers between devices  29.5 us (43%)
  waiting for transfers between devices  21.8 us (31%)
  Pallas kernels  14.7 us (21%)
  local copies, waits for them, and re-layouts  1.37 us (2%)
  other arithmetic  1.28 us (2%)
    ppermute x19, starting transfers between devices, moved(): return lax.ppermute(x, axis, [(i, (i + by) % peers) for i in range(peers)])  25.9 us
    ppermute x19, waiting for transfers between devices, moved(): return lax.ppermute(x, axis, [(i, (i + by) % peers) for i in range(peers)])  21.8 us
    pallas_call x2, Pallas kernels, gather(): pl.pallas_call(functools.partial(gather_kernel, depth), out_shape=[shape]...  7.19 us
    pallas_call x1, Pallas kernels, free_part(): pl.pallas_call(functools.partial(free_kernel, parts, chunks), out_shape=[...  3.76 us
    ppermute x1, starting transfers between devices, local(): lax.ppermute(leaving, 'slab', [(i, (i + 3) % slab_count if i % 2 else (i...  3.07 us
  transfers between devices with their start and end apart: 25, of which 9 were waited for; matrix products, arithmetic and copies ran while one was open for 4% of the time, Pallas kernels for 17%

profile of v1, /device:TPU:0, one launch (start us, length us, event | category | flops | bytes accessed | tf_op | source)
XLA Modules:
  0.0 68.9 jit_solution(3480529079182051293)
XLA Ops:
  0.0 1.3 %raw_density.1 = (f32[2,3,8,256]{3,2,1,0:T(8,128)S(1)}, f32[2,3,8,256]{3,2,1,0:T(8,128)S(1)}, f32[2,3,8,256]{3,2,1,0:T(8,128)S(1)}, f32[2,3,8,256]{3,2,1,0:T(8,128)S(1)}) custom-call(s32[1]{0:T(128)} %bitcast.me_ref, f32[2,4,4,8,1024]{4,3,2,1,0:T(8,128)} %own_ref.3), custom_call_target="tpu_custom_call" | custom-call | tf_op jit(solution)/shard_map/raw_density/pallas_call | solution.py:109
  1.3 3.1 %collective-permute-start = (f32[2,3,8,256]{3,2,1,0:T(8,128)S(1)}, f32[2,3,8,256]{3,2,1,0:T(8,128)S(1)}, u32[]{:S(2)}, u32[]{:S(2)}) collective-permute-start(f32[2,3,8,256]{3,2,1,0:T(8,128)S(1)} %get-tuple-element.16), channel_id=1, source_target_pairs={{0,1},{1,2},{2,3},{3,0},{4,5},{5,6},{6,7},{7,4},{8,9},{9,10},{10,1... | collective-permute-start | bytes 147464 | tf_op jit(solution)/shard_map/ppermute | solution.py:36
  4.4 2.6 %collective-permute-start.1 = (f32[2,3,8,256]{3,2,1,0:T(8,128)S(1)}, f32[2,3,8,256]{3,2,1,0:T(8,128)S(1)}, u32[]{:S(2)}, u32[]{:S(2)}) collective-permute-start(f32[2,3,8,256]{3,2,1,0:T(8,128)S(1)} %get-tuple-element.17), channel_id=1, source_target_pairs={{0,2},{1,3},{2,0},{3,1},{4,6},{5,7},{6,4},{7,5},{8,10},{9,11},{10,... | collective-permute-start | bytes 147464 | tf_op jit(solution)/shard_map/ppermute | solution.py:36
  7.0 1.4 %collective-permute-start.2 = (f32[2,3,8,256]{3,2,1,0:T(8,128)S(1)}, f32[2,3,8,256]{3,2,1,0:T(8,128)S(1)}, u32[]{:S(2)}, u32[]{:S(2)}) collective-permute-start(f32[2,3,8,256]{3,2,1,0:T(8,128)S(1)} %get-tuple-element.18), channel_id=1, source_target_pairs={{0,3},{1,0},{2,1},{3,2},{4,7},{5,4},{6,5},{7,6},{8,11},{9,8},{10,9... | collective-permute-start | bytes 147464 | tf_op jit(solution)/shard_map/ppermute | solution.py:36
  8.6 2.0 %collective-permute-done.1 = f32[2,3,8,256]{3,2,1,0:T(8,128)S(1)} collective-permute-done((f32[2,3,8,256]{3,2,1,0:T(8,128)S(1)}, f32[2,3,8,256]{3,2,1,0:T(8,128)S(1)}, u32[]{:S(2)}, u32[]{:S(2)}) %collective-permute-start.1) | collective-permute-done | bytes 49184 | tf_op jit(solution)/shard_map/ppermute | solution.py:36
  11.2 1.7 %collective-permute-start.4 = (f32[3,8,256]{2,1,0:T(8,128)S(1)}, f32[3,8,256]{2,1,0:T(8,128)S(1)}, u32[]{:S(2)}, u32[]{:S(2)}) collective-permute-start(f32[3,8,256]{2,1,0:T(8,128)S(1)} %get-tuple-element.30.refs_3_), channel_id=1, source_target_pairs={{0,8},{4,12},{8,16},{12,20},{16,24},{20,28},{24,0},{28,4},{1,9},{5... | collective-permute-start | bytes 73736 | tf_op jit(solution)/shard_map/ppermute | solution.py:36
  12.9 1.3 %collective-permute-start.5 = (f32[3,8,256]{2,1,0:T(8,128)S(1)}, f32[3,8,256]{2,1,0:T(8,128)S(1)}, u32[]{:S(2)}, u32[]{:S(2)}) collective-permute-start(f32[3,8,256]{2,1,0:T(8,128)S(1)} %get-tuple-element.30.refs_3_), channel_id=1, source_target_pairs={{0,4},{4,8},{8,12},{12,16},{16,20},{20,24},{24,28},{28,0},{1,5},{5... | collective-permute-start | bytes 73736 | tf_op jit(solution)/shard_map/ppermute | solution.py:36
  14.2 1.3 %slice_bitcast_fusion = (f32[2,4,8,1024]{3,2,1,0:T(8,128)S(1)}, f32[2,4,8,1024]{3,2,1,0:T(8,128)S(1)}, f32[2,4,8,1024]{3,2,1,0:T(8,128)S(1)}, f32[2,4,8,1024]{3,2,1,0:T(8,128)S(1)}) fusion(f32[2,4,4,8,1024]{4,3,2,1,0:T(8,128)} %own_ref.3), kind=kLoop, calls=%fused_computation.1 | loop fusion | bytes 2097152 | tf_op jit(solution)/shard_map/squeeze | solution.py:454
  15.8 2.2 %collective-permute-start.6 = (f32[3,8,256]{2,1,0:T(8,128)S(1)}, f32[3,8,256]{2,1,0:T(8,128)S(1)}, u32[]{:S(2)}, u32[]{:S(2)}) collective-permute-start(f32[3,8,256]{2,1,0:T(8,128)S(1)} %get-tuple-element.29.refs_4_), channel_id=1, source_target_pairs={{0,28},{4,0},{8,4},{12,8},{16,12},{20,16},{24,20},{28,24},{1,29},{... | collective-permute-start | bytes 73736 | tf_op jit(solution)/shard_map/ppermute | solution.py:36
  18.8 1.3 %slice_select_fusion = f32[1,4,4,5,1024]{4,3,2,1,0:T(8,128)S(1)} fusion(f32[2,4,4,8,1024]{4,3,2,1,0:T(8,128)} %own_ref.3, pred[]{:T(512)S(6)} %eq.3), kind=kLoop, calls=%fused_computation | loop fusion | flops 81920 | bytes 983041 | tf_op jit(solution)/shard_map/jit(_where)/select_n | solution.py:458
  20.2 2.5 %collective-permute-done.6.refs_5_ = f32[3,8,256]{2,1,0:T(8,128)S(1)} collective-permute-done((f32[3,8,256]{2,1,0:T(8,128)S(1)}, f32[3,8,256]{2,1,0:T(8,128)S(1)}, u32[]{:S(2)}, u32[]{:S(2)}) %collective-permute-start.6) | collective-permute-done | bytes 24608 | tf_op jit(solution)/shard_map/ppermute | solution.py:36
  22.7 3.1 %collective-permute-start.13 = (f32[4,4,5,8,128]{4,3,2,1,0:T(8,128)S(1)}, f32[4,4,5,8,128]{4,3,2,1,0:T(8,128)S(1)}, u32[]{:S(2)}, u32[]{:S(2)}) collective-permute-start(f32[4,4,5,8,128]{4,3,2,1,0:T(8,128)S(1)} %select_n.14), channel_id=1, source_target_pairs={{0,20},{4,16},{8,28},{12,24},{16,4},{20,0},{24,12},{28,8},{1,21},{... | collective-permute-start | bytes 983048 | tf_op jit(solution)/shard_map/ppermute | solution.py:460
  25.7 1.4 %collective-permute-start.19 = (f32[2,4,8,1024]{3,2,1,0:T(8,128)S(1)}, f32[2,4,8,1024]{3,2,1,0:T(8,128)S(1)}, u32[]{:S(2)}, u32[]{:S(2)}) collective-permute-start(f32[2,4,8,1024]{3,2,1,0:T(8,128)S(1)} %get-tuple-element.25), channel_id=1, source_target_pairs={{0,24},{4,28},{8,0},{12,4},{16,8},{20,12},{24,16},{28,20},{1,25},{... | collective-permute-start | bytes 786440 | tf_op jit(solution)/shard_map/ppermute | solution.py:36
  27.8 2.3 %collective-permute-start.15 = (f32[2,4,8,1024]{3,2,1,0:T(8,128)S(1)}, f32[2,4,8,1024]{3,2,1,0:T(8,128)S(1)}, u32[]{:S(2)}, u32[]{:S(2)}) collective-permute-start(f32[2,4,8,1024]{3,2,1,0:T(8,128)S(1)} %get-tuple-element.26), channel_id=1, source_target_pairs={{0,24},{4,28},{8,0},{12,4},{16,8},{20,12},{24,16},{28,20},{1,25},{... | collective-permute-start | bytes 786440 | tf_op jit(solution)/shard_map/ppermute | solution.py:36
  30.1 4.9 %collective-permute-done.19.recv_second = f32[2,4,8,1024]{3,2,1,0:T(8,128)S(1)} collective-permute-done((f32[2,4,8,1024]{3,2,1,0:T(8,128)S(1)}, f32[2,4,8,1024]{3,2,1,0:T(8,128)S(1)}, u32[]{:S(2)}, u32[]{:S(2)}) %collective-permute-start.19) | collective-permute-done | bytes 262176 | tf_op jit(solution)/shard_map/ppermute | solution.py:36
  35.0 5.9 %collective-permute-done.14.recv_first = f32[2,4,8,1024]{3,2,1,0:T(8,128)S(1)} collective-permute-done((f32[2,4,8,1024]{3,2,1,0:T(8,128)S(1)}, f32[2,4,8,1024]{3,2,1,0:T(8,128)S(1)}, u32[]{:S(2)}, u32[]{:S(2)}) %collective-permute-start.14) | collective-permute-done | bytes 262176 | tf_op jit(solution)/shard_map/ppermute | solution.py:36
  40.9 3.4 %collective-permute-done.15.recv_second = f32[2,4,8,1024]{3,2,1,0:T(8,128)S(1)} collective-permute-done((f32[2,4,8,1024]{3,2,1,0:T(8,128)S(1)}, f32[2,4,8,1024]{3,2,1,0:T(8,128)S(1)}, u32[]{:S(2)}, u32[]{:S(2)}) %collective-permute-start.15) | collective-permute-done | bytes 262176 | tf_op jit(solution)/shard_map/ppermute | solution.py:36
  46.7 2.4 %collective-permute-start.11 = (f32[3,16,256]{2,1,0:T(8,128)S(1)}, f32[3,16,256]{2,1,0:T(8,128)S(1)}, u32[]{:S(2)}, u32[]{:S(2)}) collective-permute-start(f32[3,16,256]{2,1,0:T(8,128)S(1)} %placed_fields.1.refs_0_), channel_id=1, source_target_pairs={{0,3},{1,0},{2,1},{3,2},{4,7},{5,4},{6,5},{7,6},{8,11},{9,8},{10,9... | collective-permute-start | bytes 147464 | tf_op jit(solution)/shard_map/ppermute | solution.py:36
  49.4 3.6 %gather.3 = (f32[2,2,4,14,8,128]{5,4,3,2,1,0:T(8,128)S(1)}, f32[2,2,4,14,8,128]{5,4,3,2,1,0:T(8,128)S(1)}) custom-call(s32[1]{0:T(128)} %bitcast.1.where_ref, s32[2]{0:T(128)S(1)} %copy-done.1, s32[2]{0:T(128)S(1)} %copy-done.2, bf16[256,384]{1,0:T(8,128)(2,1)S(1)} %copy-done, f32[2,4,4,8,1024]{4,3,2,1,0:T(8,128)} %own_ref.3, ...), custom_call_target="tpu_custom_call" | custom-call | tf_op jit(solution)/shard_map/gather/pallas_call | solution.py:264
  53.0 3.6 %gather.2 = (f32[2,2,4,14,8,128]{5,4,3,2,1,0:T(8,128)S(1)}, f32[2,2,4,14,8,128]{5,4,3,2,1,0:T(8,128)S(1)}) custom-call(s32[1]{0:T(128)} %bitcast.1.where_ref, s32[2]{0:T(128)S(1)} %copy-done.1, s32[2]{0:T(128)S(1)} %copy-done.2, bf16[256,384]{1,0:T(8,128)(2,1)S(1)} %copy-done, f32[2,4,4,8,1024]{4,3,2,1,0:T(8,128)} %own_ref.3, ...), custom_call_target="tpu_custom_call" | custom-call | tf_op jit(solution)/shard_map/gather/pallas_call | solution.py:264
  57.2 2.0 %collective-permute-start.22 = (f32[3,8,1024]{2,1,0:T(8,128)S(1)}, f32[3,8,1024]{2,1,0:T(8,128)S(1)}, u32[]{:S(2)}, u32[]{:S(2)}) collective-permute-start(f32[3,8,1024]{2,1,0:T(8,128)S(1)} %density.1.refs_0_), channel_id=1, source_target_pairs={{0,1},{1,2},{2,3},{3,0},{4,5},{5,6},{6,7},{7,4},{8,9},{9,10},{10,1... | collective-permute-start | bytes 294920 | tf_op jit(solution)/shard_map/ppermute | solution.py:36
  59.2 2.1 %collective-permute-start.23 = (f32[3,8,1024]{2,1,0:T(8,128)S(1)}, f32[3,8,1024]{2,1,0:T(8,128)S(1)}, u32[]{:S(2)}, u32[]{:S(2)}) collective-permute-start(f32[3,8,1024]{2,1,0:T(8,128)S(1)} %density.1.refs_0_), channel_id=1, source_target_pairs={{0,2},{1,3},{2,0},{3,1},{4,6},{5,7},{6,4},{7,5},{8,10},{9,11},{10,... | collective-permute-start | bytes 294920 | tf_op jit(solution)/shard_map/ppermute | solution.py:36
  61.6 3.8 %free_part.1 = (f32[2,4,4,8,1024]{4,3,2,1,0:T(8,128)S(1)}, f32[2,4,4,8,1024]{4,3,2,1,0:T(8,128)S(1)}) custom-call(s32[1]{0:T(128)} %bitcast.me_ref, bf16[256,384]{1,0:T(8,128)(2,1)S(1)} %copy-done, f32[3,16,256]{2,1,0:T(8,128)S(1)} %placed_fields.1.refs_0_, f32[3,16,256]{2,1,0:T(8,128)S(1)} %collective-permute-done.9.refs_1_, ...), custom_call_target="tpu_custom_call" | custom-call | tf_op jit(solution)/shard_map/free_part/pallas_call | solution.py:373
  65.4 2.1 %collective-permute-done.23.refs_2_ = f32[3,8,1024]{2,1,0:T(8,128)S(1)} collective-permute-done((f32[3,8,1024]{2,1,0:T(8,128)S(1)}, f32[3,8,1024]{2,1,0:T(8,128)S(1)}, u32[]{:S(2)}, u32[]{:S(2)}) %collective-permute-start.23) | collective-permute-done | bytes 98336 | tf_op jit(solution)/shard_map/ppermute | solution.py:36
  (44 shorter events, 7.5 us)
Async XLA Ops:
  1.3 7.3 %collective-permute-start = (f32[2,3,8,256]{3,2,1,0:T(8,128)S(1)}, f32[2,3,8,256]{3,2,1,0:T(8,128)S(1)}, u32[]{:S(2)}, u32[]{:S(2)}) collective-permute-start(f32[2,3,8,256]{3,2,1,0:T(8,128)S(1)} %get-tuple-element.16), channel_id=1, source_target_pairs={{0,1},{1,2},{2,3},{3,0},{4,5},{5,6},{6,7},{7,4},{8,9},{9,10},{10,1... | collective-permute-start | bytes 147464 | tf_op jit(solution)/shard_map/ppermute | solution.py:36
  4.4 6.2 %collective-permute-start.1 = (f32[2,3,8,256]{3,2,1,0:T(8,128)S(1)}, f32[2,3,8,256]{3,2,1,0:T(8,128)S(1)}, u32[]{:S(2)}, u32[]{:S(2)}) collective-permute-start(f32[2,3,8,256]{3,2,1,0:T(8,128)S(1)} %get-tuple-element.17), channel_id=1, source_target_pairs={{0,2},{1,3},{2,0},{3,1},{4,6},{5,7},{6,4},{7,5},{8,10},{9,11},{10,... | collective-permute-start | bytes 147464 | tf_op jit(solution)/shard_map/ppermute | solution.py:36
  8.4 40.7 %collective-permute-start.12 = (f32[2,4,4,8,1024]{4,3,2,1,0:T(8,128)}, f32[2,4,4,8,1024]{4,3,2,1,0:T(8,128)S(1)}, u32[]{:S(2)}, u32[]{:S(2)}) collective-permute-start(f32[2,4,4,8,1024]{4,3,2,1,0:T(8,128)} %own_ref.3), channel_id=1, source_target_pairs={{0,4},{4,0},{8,12},{12,8},{16,20},{20,16},{24,28},{28,24},{1,5},{5... | collective-permute-start | bytes 3145736 | tf_op jit(solution)/shard_map/ppermute | solution.py:41
  11.2 4.7 %collective-permute-start.3 = (f32[3,8,256]{2,1,0:T(8,128)S(1)}, f32[3,8,256]{2,1,0:T(8,128)S(1)}, u32[]{:S(2)}, u32[]{:S(2)}) collective-permute-start(f32[3,8,256]{2,1,0:T(8,128)S(1)} %get-tuple-element.30.refs_3_), channel_id=1, source_target_pairs={{0,12},{4,16},{8,20},{12,24},{16,28},{20,0},{24,4},{28,8},{1,13},{... | collective-permute-start | bytes 73736 | tf_op jit(solution)/shard_map/ppermute | solution.py:36
  11.2 6.8 %collective-permute-start.4 = (f32[3,8,256]{2,1,0:T(8,128)S(1)}, f32[3,8,256]{2,1,0:T(8,128)S(1)}, u32[]{:S(2)}, u32[]{:S(2)}) collective-permute-start(f32[3,8,256]{2,1,0:T(8,128)S(1)} %get-tuple-element.30.refs_3_), channel_id=1, source_target_pairs={{0,8},{4,12},{8,16},{12,20},{16,24},{20,28},{24,0},{28,4},{1,9},{5... | collective-permute-start | bytes 73736 | tf_op jit(solution)/shard_map/ppermute | solution.py:36
  12.9 5.7 %collective-permute-start.5 = (f32[3,8,256]{2,1,0:T(8,128)S(1)}, f32[3,8,256]{2,1,0:T(8,128)S(1)}, u32[]{:S(2)}, u32[]{:S(2)}) collective-permute-start(f32[3,8,256]{2,1,0:T(8,128)S(1)} %get-tuple-element.30.refs_3_), channel_id=1, source_target_pairs={{0,4},{4,8},{8,12},{12,16},{16,20},{20,24},{24,28},{28,0},{1,5},{5... | collective-permute-start | bytes 73736 | tf_op jit(solution)/shard_map/ppermute | solution.py:36
  15.4 12.3 %collective-permute-start.18 = (f32[2,4,8,1024]{3,2,1,0:T(8,128)S(1)}, f32[2,4,8,1024]{3,2,1,0:T(8,128)S(1)}, u32[]{:S(2)}, u32[]{:S(2)}) collective-permute-start(f32[2,4,8,1024]{3,2,1,0:T(8,128)S(1)} %get-tuple-element.28), channel_id=1, source_target_pairs={{0,8},{4,12},{8,16},{12,20},{16,24},{20,28},{24,0},{28,4},{1,9},{5... | collective-permute-start | bytes 786440 | tf_op jit(solution)/shard_map/ppermute | solution.py:36
  15.8 6.8 %collective-permute-start.6 = (f32[3,8,256]{2,1,0:T(8,128)S(1)}, f32[3,8,256]{2,1,0:T(8,128)S(1)}, u32[]{:S(2)}, u32[]{:S(2)}) collective-permute-start(f32[3,8,256]{2,1,0:T(8,128)S(1)} %get-tuple-element.29.refs_4_), channel_id=1, source_target_pairs={{0,28},{4,0},{8,4},{12,8},{16,12},{20,16},{24,20},{28,24},{1,29},{... | collective-permute-start | bytes 73736 | tf_op jit(solution)/shard_map/ppermute | solution.py:36
  18.1 7.7 %collective-permute-start.7 = (f32[3,8,256]{2,1,0:T(8,128)S(1)}, f32[3,8,256]{2,1,0:T(8,128)S(1)}, u32[]{:S(2)}, u32[]{:S(2)}) collective-permute-start(f32[3,8,256]{2,1,0:T(8,128)S(1)} %get-tuple-element.29.refs_4_), channel_id=1, source_target_pairs={{0,24},{4,28},{8,0},{12,4},{16,8},{20,12},{24,16},{28,20},{1,25},{... | collective-permute-start | bytes 73736 | tf_op jit(solution)/shard_map/ppermute | solution.py:36
  18.6 8.5 %collective-permute-start.8 = (f32[3,8,256]{2,1,0:T(8,128)S(1)}, f32[3,8,256]{2,1,0:T(8,128)S(1)}, u32[]{:S(2)}, u32[]{:S(2)}) collective-permute-start(f32[3,8,256]{2,1,0:T(8,128)S(1)} %get-tuple-element.29.refs_4_), channel_id=1, source_target_pairs={{0,20},{4,24},{8,28},{12,0},{16,4},{20,8},{24,12},{28,16},{1,21},{... | collective-permute-start | bytes 73736 | tf_op jit(solution)/shard_map/ppermute | solution.py:36
  22.7 21.6 %collective-permute-start.13 = (f32[4,4,5,8,128]{4,3,2,1,0:T(8,128)S(1)}, f32[4,4,5,8,128]{4,3,2,1,0:T(8,128)S(1)}, u32[]{:S(2)}, u32[]{:S(2)}) collective-permute-start(f32[4,4,5,8,128]{4,3,2,1,0:T(8,128)S(1)} %select_n.14), channel_id=1, source_target_pairs={{0,20},{4,16},{8,28},{12,24},{16,4},{20,0},{24,12},{28,8},{1,21},{... | collective-permute-start | bytes 983048 | tf_op jit(solution)/shard_map/ppermute | solution.py:460
  25.7 9.2 %collective-permute-start.19 = (f32[2,4,8,1024]{3,2,1,0:T(8,128)S(1)}, f32[2,4,8,1024]{3,2,1,0:T(8,128)S(1)}, u32[]{:S(2)}, u32[]{:S(2)}) collective-permute-start(f32[2,4,8,1024]{3,2,1,0:T(8,128)S(1)} %get-tuple-element.25), channel_id=1, source_target_pairs={{0,24},{4,28},{8,0},{12,4},{16,8},{20,12},{24,16},{28,20},{1,25},{... | collective-permute-start | bytes 786440 | tf_op jit(solution)/shard_map/ppermute | solution.py:36
  27.1 13.8 %collective-permute-start.14 = (f32[2,4,8,1024]{3,2,1,0:T(8,128)S(1)}, f32[2,4,8,1024]{3,2,1,0:T(8,128)S(1)}, u32[]{:S(2)}, u32[]{:S(2)}) collective-permute-start(f32[2,4,8,1024]{3,2,1,0:T(8,128)S(1)} %get-tuple-element.27), channel_id=1, source_target_pairs={{0,8},{4,12},{8,16},{12,20},{16,24},{20,28},{24,0},{28,4},{1,9},{5... | collective-permute-start | bytes 786440 | tf_op jit(solution)/shard_map/ppermute | solution.py:36
  27.8 16.5 %collective-permute-start.15 = (f32[2,4,8,1024]{3,2,1,0:T(8,128)S(1)}, f32[2,4,8,1024]{3,2,1,0:T(8,128)S(1)}, u32[]{:S(2)}, u32[]{:S(2)}) collective-permute-start(f32[2,4,8,1024]{3,2,1,0:T(8,128)S(1)} %get-tuple-element.26), channel_id=1, source_target_pairs={{0,24},{4,28},{8,0},{12,4},{16,8},{20,12},{24,16},{28,20},{1,25},{... | collective-permute-start | bytes 786440 | tf_op jit(solution)/shard_map/ppermute | solution.py:36
  35.0 10.6 %collective-permute-start.20 = (f32[2,4,8,1024]{3,2,1,0:T(8,128)S(1)}, f32[2,4,8,1024]{3,2,1,0:T(8,128)S(1)}, u32[]{:S(2)}, u32[]{:S(2)}) collective-permute-start(f32[2,4,8,1024]{3,2,1,0:T(8,128)S(1)} %collective-permute-done.18.recv_first), channel_id=1, source_target_pairs={{0,4},{4,0},{8,12},{12,8},{16,20},{20,16},{24,28},{28,24},{1,5},{5... | collective-permute-start | bytes 786440 | tf_op jit(solution)/shard_map/ppermute | solution.py:41
  40.9 5.8 %collective-permute-start.21 = (f32[2,4,8,1024]{3,2,1,0:T(8,128)S(1)}, f32[2,4,8,1024]{3,2,1,0:T(8,128)S(1)}, u32[]{:S(2)}, u32[]{:S(2)}) collective-permute-start(f32[2,4,8,1024]{3,2,1,0:T(8,128)S(1)} %collective-permute-done.19.recv_second), channel_id=1, source_target_pairs={{0,4},{4,0},{8,12},{12,8},{16,20},{20,16},{24,28},{28,24},{1,5},{5... | collective-permute-start | bytes 786440 | tf_op jit(solution)/shard_map/ppermute | solution.py:41
  44.3 8.7 %collective-permute-start.16 = (f32[2,4,8,1024]{3,2,1,0:T(8,128)S(1)}, f32[2,4,8,1024]{3,2,1,0:T(8,128)S(1)}, u32[]{:S(2)}, u32[]{:S(2)}) collective-permute-start(f32[2,4,8,1024]{3,2,1,0:T(8,128)S(1)} %collective-permute-done.14.recv_first), channel_id=1, source_target_pairs={{0,4},{4,0},{8,12},{12,8},{16,20},{20,16},{24,28},{28,24},{1,5},{5... | collective-permute-start | bytes 786440 | tf_op jit(solution)/shard_map/ppermute | solution.py:41
  44.3 8.7 %collective-permute-start.17 = (f32[2,4,8,1024]{3,2,1,0:T(8,128)S(1)}, f32[2,4,8,1024]{3,2,1,0:T(8,128)S(1)}, u32[]{:S(2)}, u32[]{:S(2)}) collective-permute-start(f32[2,4,8,1024]{3,2,1,0:T(8,128)S(1)} %collective-permute-done.15.recv_second), channel_id=1, source_target_pairs={{0,4},{4,0},{8,12},{12,8},{16,20},{20,16},{24,28},{28,24},{1,5},{5... | collective-permute-start | bytes 786440 | tf_op jit(solution)/shard_map/ppermute | solution.py:41
  45.5 11.1 %collective-permute-start.10 = (f32[3,16,256]{2,1,0:T(8,128)S(1)}, f32[3,16,256]{2,1,0:T(8,128)S(1)}, u32[]{:S(2)}, u32[]{:S(2)}) collective-permute-start(f32[3,16,256]{2,1,0:T(8,128)S(1)} %placed_fields.1.refs_0_), channel_id=1, source_target_pairs={{0,2},{1,3},{2,0},{3,1},{4,6},{5,7},{6,4},{7,5},{8,10},{9,11},{10,... | collective-permute-start | bytes 147464 | tf_op jit(solution)/shard_map/ppermute | solution.py:36
  46.7 9.9 %collective-permute-start.11 = (f32[3,16,256]{2,1,0:T(8,128)S(1)}, f32[3,16,256]{2,1,0:T(8,128)S(1)}, u32[]{:S(2)}, u32[]{:S(2)}) collective-permute-start(f32[3,16,256]{2,1,0:T(8,128)S(1)} %placed_fields.1.refs_0_), channel_id=1, source_target_pairs={{0,3},{1,0},{2,1},{3,2},{4,7},{5,4},{6,5},{7,6},{8,11},{9,8},{10,9... | collective-permute-start | bytes 147464 | tf_op jit(solution)/shard_map/ppermute | solution.py:36
  49.1 7.5 %collective-permute-start.9 = (f32[3,16,256]{2,1,0:T(8,128)S(1)}, f32[3,16,256]{2,1,0:T(8,128)S(1)}, u32[]{:S(2)}, u32[]{:S(2)}) collective-permute-start(f32[3,16,256]{2,1,0:T(8,128)S(1)} %placed_fields.1.refs_0_), channel_id=1, source_target_pairs={{0,1},{1,2},{2,3},{3,0},{4,5},{5,6},{6,7},{7,4},{8,9},{9,10},{10,1... | collective-permute-start | bytes 147464 | tf_op jit(solution)/shard_map/ppermute | solution.py:36
  57.2 8.2 %collective-permute-start.22 = (f32[3,8,1024]{2,1,0:T(8,128)S(1)}, f32[3,8,1024]{2,1,0:T(8,128)S(1)}, u32[]{:S(2)}, u32[]{:S(2)}) collective-permute-start(f32[3,8,1024]{2,1,0:T(8,128)S(1)} %density.1.refs_0_), channel_id=1, source_target_pairs={{0,1},{1,2},{2,3},{3,0},{4,5},{5,6},{6,7},{7,4},{8,9},{9,10},{10,1... | collective-permute-start | bytes 294920 | tf_op jit(solution)/shard_map/ppermute | solution.py:36
  59.2 8.4 %collective-permute-start.23 = (f32[3,8,1024]{2,1,0:T(8,128)S(1)}, f32[3,8,1024]{2,1,0:T(8,128)S(1)}, u32[]{:S(2)}, u32[]{:S(2)}) collective-permute-start(f32[3,8,1024]{2,1,0:T(8,128)S(1)} %density.1.refs_0_), channel_id=1, source_target_pairs={{0,2},{1,3},{2,0},{3,1},{4,6},{5,7},{6,4},{7,5},{8,10},{9,11},{10,... | collective-permute-start | bytes 294920 | tf_op jit(solution)/shard_map/ppermute | solution.py:36
  61.4 6.4 %collective-permute-start.24 = (f32[3,8,1024]{2,1,0:T(8,128)S(1)}, f32[3,8,1024]{2,1,0:T(8,128)S(1)}, u32[]{:S(2)}, u32[]{:S(2)}) collective-permute-start(f32[3,8,1024]{2,1,0:T(8,128)S(1)} %density.1.refs_0_), channel_id=1, source_target_pairs={{0,3},{1,0},{2,1},{3,2},{4,7},{5,4},{6,5},{7,6},{8,11},{9,8},{10,9... | collective-permute-start | bytes 294920 | tf_op jit(solution)/shard_map/ppermute | solution.py:36
  (4 other events, 82.9 us)

commit v2 on v1

v2 whole, which is shorter than its diff:
```python
import functools
import math

import jax
import jax.numpy as jnp
import numpy as np
from jax import lax
from jax.experimental import pallas as pl
from jax.experimental.pallas import tpu as pltpu
from jax.sharding import PartitionSpec as P

NY = 32
LANES = 128
SUBS = 8
HALO = 3
REACH = 2 * HALO
VMEM_BYTES = 40 * 1024 * 1024

stencil = (-49.0 / 18.0, 1.5, -0.15, 1.0 / 90.0)
coupling = 3.0
xi_factor = 1.2
chemical = 1.0
time_step = 0.1

VMEM = pl.BlockSpec(memory_space=pltpu.VMEM)
SMEM = pl.BlockSpec(memory_space=pltpu.SMEM)
ANYWHERE = pl.BlockSpec(memory_space=pl.ANY)


def params():
    return pltpu.CompilerParams(vmem_limit_bytes=VMEM_BYTES)


def moved(x, axis, by):
    peers = lax.axis_size(axis)
    return lax.ppermute(x, axis, [(i, (i + by) % peers) for i in range(peers)])


def swapped(x):
    peers = lax.axis_size("slab")
    return lax.ppermute(x, "slab", [(i, i ^ 1) for i in range(peers)])


def transverse_weights():
    whole = {0: -980.0, 1: 270.0, 2: -27.0, 3: 2.0}
    rows = LANES // NY
    weights = np.zeros((LANES, 3 * LANES), np.float32)
    for a in range(LANES):
        xa, ya = divmod(a, NY)
        for b in range(LANES):
            xb, yb = divmod(b, NY)
            for part, distance in ((0, xb + rows - xa), (1, xb - xa), (2, xb - rows - xa)):
                if ya == yb and abs(distance) <= HALO:
                    weights[a, part * LANES + b] += whole[abs(distance)]
            if xa == xb and 0 < abs(ya - yb) <= HALO:
                weights[a, LANES + b] += whole[abs(ya - yb)]
    return np.concatenate([weights, weights]).astype(jnp.bfloat16)


def phase(wave, first, depth):
    z = first + lax.broadcasted_iota(jnp.int32, (SUBS, LANES), 0)
    index = jnp.bitwise_and(wave * z, depth - 1)
    angle = (2.0 * math.pi / depth) * index.astype(jnp.float32)
    return jnp.cos(angle), jnp.sin(angle)


def densities(ur, ui, vr, vi):
    return vr * vr + vi * vi, ur * vr + ui * vi, ui * vr - ur * vi


def fields_of(n, kr, ki, scale):
    n = n * scale
    safe = jnp.where(n > 0.0, n, 1.0)
    power = jnp.where(n > 0.0, jnp.exp((2.0 / 3.0) * jnp.log(safe)), 0.0)
    return xi_factor * power - chemical, (-coupling * scale) * kr, (-coupling * scale) * ki


def local_part(field, ur, ui, vr, vi):
    potential, gap_real, gap_imag = field
    return (
        potential * ur + gap_real * vr - gap_imag * vi,
        potential * ui + gap_real * vi + gap_imag * vr,
        gap_real * ur + gap_imag * ui - potential * vr,
        gap_real * ui - gap_imag * ur - potential * vi,
    )


def copy_rows(x_ref, cloud, state, out_ref, first_row):
    planes, cells = x_ref.shape[3:]
    for k in range(4):
        rows = pl.ds(first_row + k * planes, planes)
        for t in range(cells // LANES):
            out_ref[rows, t, :] = x_ref[cloud, state, k, :, t * LANES : (t + 1) * LANES]


def take_kernel(mine, first, count, where_ref, x_ref, *refs):
    odd = lax.rem(where_ref[0], 2)
    out_ref = refs[-1]
    for s in range(count):
        copy_rows(x_ref, odd if mine else 1 - odd, first + s, out_ref, s * 4 * x_ref.shape[3])


def take(where, x, mine, first, count, *after):
    return pl.pallas_call(
        functools.partial(take_kernel, mine, first, count),
        out_shape=jax.ShapeDtypeStruct((count * 4 * x.shape[3], SUBS, LANES), x.dtype),
        in_specs=[SMEM, VMEM] + [ANYWHERE] * len(after),
        out_specs=VMEM,
        compiler_params=params(),
        name="take",
    )(where, x, *after)


def take_extra_kernel(where_ref, x_ref, *refs):
    out_ref, turned = refs[-2:]
    odd = lax.rem(where_ref[0], 2)
    per_group, _, planes, cells = x_ref.shape[1:]
    layers = REACH - 1

    def fill(cloud, lowest):
        for s in range(per_group):
            copy_rows(x_ref, cloud, s, turned, 0)
            for k in range(4):
                out_ref[(4 * s + k) * layers : (4 * s + k + 1) * layers] = turned[k * planes + lowest : k * planes + lowest + layers]

    @pl.when(odd == 1)
    def _():
        fill(0, planes - layers)

    @pl.when(odd == 0)
    def _():
        fill(1, 0)


def take_extra(where, x, *after):
    per_group, _, planes, _ = x.shape[1:]
    return pl.pallas_call(
        take_extra_kernel,
        out_shape=jax.ShapeDtypeStruct((per_group * 4 * (REACH - 1), SUBS, LANES), x.dtype),
        in_specs=[SMEM, VMEM] + [ANYWHERE] * len(after),
        out_specs=VMEM,
        scratch_shapes=[pltpu.VMEM((4 * planes, SUBS, LANES), x.dtype)],
        compiler_params=params(),
        name="take_extra",
    )(where, x, *after)


def join_kernel(count, *refs):
    out_ref = refs[-1]
    first = 0
    for ref in refs[:count]:
        out_ref[first : first + ref.shape[0]] = ref[...]
        first += ref.shape[0]


def join(pieces, *after):
    rows = sum(piece.shape[0] for piece in pieces)
    return pl.pallas_call(
        functools.partial(join_kernel, len(pieces)),
        out_shape=jax.ShapeDtypeStruct((rows, *pieces[0].shape[1:]), pieces[0].dtype),
        in_specs=[VMEM] * len(pieces) + [ANYWHERE] * len(after),
        out_specs=VMEM,
        compiler_params=params(),
        name="join",
    )(*pieces, *after)


def total_kernel(count, where_ref, *refs):
    odd = lax.rem(where_ref[0], 2)
    mine_ref, other_ref = refs[-2:]
    total = refs[0][...]
    for ref in refs[1:count]:
        total = total + ref[...]
    mine_ref[...] = jnp.where(odd == 1, total[1], total[0])
    other_ref[...] = jnp.where(odd == 1, total[0], total[1])


def total_of(where, terms, *after):
    return pl.pallas_call(
        functools.partial(total_kernel, len(terms)),
        out_shape=[jax.ShapeDtypeStruct(terms[0].shape[1:], terms[0].dtype)] * 2,
        in_specs=[SMEM] + [VMEM] * len(terms) + [ANYWHERE] * len(after),
        out_specs=[VMEM] * 2,
        compiler_params=params(),
        name="total",
    )(where, *terms, *after)


def raw_density_kernel(x_ref, *refs):
    out_ref = refs[-1]
    clouds, states, _, planes, cells = x_ref.shape
    for j in range(clouds):
        for t in range(cells // LANES):
            lanes = pl.ds(t * LANES, LANES)
            sums = [jnp.zeros((planes, LANES), jnp.float32)] * 3
            for s in range(states):
                terms = densities(*[x_ref[j, s, k, :, lanes] for k in range(4)])
                sums = [a + b for a, b in zip(sums, terms)]
            for f in range(3):
                out_ref[j, f, :, lanes] = sums[f]


def raw_density(x, *after):
    clouds, _, _, planes, cells = x.shape
    return pl.pallas_call(
        raw_density_kernel,
        out_shape=jax.ShapeDtypeStruct((clouds, 3, planes, cells), jnp.float32),
        in_specs=[VMEM] + [ANYWHERE] * len(after),
        out_specs=VMEM,
        compiler_params=params(),
        name="raw_density",
    )(x, *after)


def slots_of(cloud):
    return [jnp.where(cloud == 0, q, 3 - q) for q in range(4)]


def first_layer(cloud, slot, slab, planes, shift_ref):
    return jnp.where(cloud == 0, (slab - 3 + slot) * planes + shift_ref[0], (slab + slot) * planes - shift_ref[1])


def window_start(cloud, planes, reach, shift_ref):
    return jnp.where(cloud == 0, 3 * planes - reach - shift_ref[0], shift_ref[1] - reach)


def placed_fields_kernel(depth, scale, where_ref, shift_ref, wave_ref, *refs):
    mine_refs, other_refs = refs[0:4], refs[4:8]
    out_ref, held = refs[-2:]
    planes, cells = mine_refs[0].shape[1:]
    slab = where_ref[0]
    odd = lax.rem(slab, 2)
    count = out_ref.shape[1]
    totals = [jnp.zeros((count, SUBS, LANES), jnp.float32)] * 3
    for cloud, slot_refs in ((odd, mine_refs), (1 - odd, other_refs)):
        for slot, ref in zip(slots_of(cloud), slot_refs):
            cos, sin = phase(2 * wave_ref[cloud], first_layer(cloud, slot, slab, planes, shift_ref), depth)
            layers = pl.ds(slot * planes, planes)
            for t in range(cells // LANES):
                lanes = pl.ds(t * LANES, LANES)
                kr, ki = ref[1, :, lanes], ref[2, :, lanes]
                held[0, layers, t, :] = ref[0, :, lanes]
                held[1, layers, t, :] = kr * cos - ki * sin
                held[2, layers, t, :] = kr * sin + ki * cos
        start = window_start(cloud, planes, HALO, shift_ref)
        totals = [total + held[f, pl.ds(start, count)] for f, total in enumerate(totals)]
    for f, field in enumerate(fields_of(*totals, scale)):
        out_ref[f] = field


def placed_fields(where, shift, wave, mine, other, depth, scale, *after):
    planes = mine[0].shape[1]
    return pl.pallas_call(
        functools.partial(placed_fields_kernel, depth, scale),
        out_shape=jax.ShapeDtypeStruct((3, planes + 2 * HALO, SUBS, LANES), jnp.float32),
        in_specs=[SMEM] * 3 + [VMEM] * 8 + [ANYWHERE] * len(after),
        out_specs=VMEM,
        scratch_shapes=[pltpu.VMEM((3, 4 * planes, SUBS, LANES), jnp.float32)],
        compiler_params=params(),
        name="placed_fields",
    )(where, shift, wave, *mine, *other, *after)


def transverse(x, weights):
    rows = x.shape[0]
    flat = x.reshape(rows * SUBS, LANES)
    high = flat.astype(jnp.bfloat16)
    low = (flat - high.astype(jnp.float32)).astype(jnp.bfloat16)
    product = jnp.dot(jnp.concatenate([high, low], axis=1), weights, preferred_element_type=jnp.float32)
    sub = lax.broadcasted_iota(jnp.int32, (rows * SUBS, LANES), 0) % SUBS
    up = pltpu.roll(product[:, :LANES].reshape(rows, SUBS, LANES), 1, 1).reshape(rows * SUBS, LANES)
    down = pltpu.roll(product[:, 2 * LANES :].reshape(rows, SUBS, LANES), SUBS - 1, 1).reshape(rows * SUBS, LANES)
    result = product[:, LANES : 2 * LANES] + jnp.where(sub > 0, up, 0.0) + jnp.where(sub < SUBS - 1, down, 0.0)
    return result.reshape(rows, SUBS, LANES)


def kinetic(layers, weights):
    count = layers.shape[1] - 2 * HALO
    inner = layers[:, HALO : HALO + count]
    along = stencil[0] * inner
    for j in range(1, HALO + 1):
        along = along + stencil[j] * (layers[:, HALO - j : HALO - j + count] + layers[:, HALO + j : HALO + j + count])
    across = transverse(inner.reshape(4 * count, SUBS, LANES), weights).reshape(inner.shape)
    return -0.5 * along + (-0.5 / 180.0) * across


def gather_kernel(depth, planes, mine, starts, where_ref, shift_ref, wave_ref, weights_ref, far_ref, second_ref, next_ref, own_ref, *refs):
    boosted_ref, base_ref, turns, window = refs[-4:]
    slab = where_ref[0]
    odd = lax.rem(slab, 2)
    cloud = odd if mine else 1 - odd
    states, _, count = boosted_ref.shape[:3]
    layers = REACH - 1
    far_edge = jnp.where(cloud == 0, planes - layers, 0)
    own_edge = jnp.where(cloud == 0, 0, planes - layers)
    slots = slots_of(cloud)
    for slot in slots:
        for n, part in enumerate(phase(wave_ref[cloud], first_layer(cloud, slot, slab, planes, shift_ref), depth)):
            for z in range(planes):
                turns[n, slot * planes + z] = jnp.broadcast_to(part[z : z + 1], (SUBS, LANES))
    start = window_start(cloud, planes, REACH, shift_ref)

    def one_state(s, _):
        def fill(place, ref, row, pitch, number):
            for n in range(number):
                cos, sin = turns[0, place + n], turns[1, place + n]
                u_re, u_im, v_re, v_im = [ref[row + k * pitch + n] for k in range(4)]
                window[0, place + n] = u_re * cos - u_im * sin
                window[1, place + n] = u_re * sin + u_im * cos
                window[2, place + n] = v_re * cos + v_im * sin
                window[3, place + n] = v_im * cos - v_re * sin

        rows = [(start + s) * 4 * planes for start in starts]
        if mine:
            fill(slots[0] * planes + far_edge, far_ref, (starts[0] + s) * 4 * layers, layers, layers)
        else:
            fill(slots[0] * planes + far_edge, far_ref, rows[0] + far_edge, planes, layers)
        fill(slots[1] * planes, second_ref, rows[1], planes, planes)
        fill(slots[2] * planes, next_ref, rows[2], planes, planes)
        fill(slots[3] * planes + own_edge, own_ref, rows[3] + own_edge, planes, layers)

        whole = window[:, pl.ds(start, count + 2 * HALO)]
        values = whole[:, HALO : HALO + count]
        kin = kinetic(whole, weights_ref[...])
        boosted_ref[s] = values
        base_ref[s, 0] = values[0] + time_step * kin[1]
        base_ref[s, 1] = values[1] - time_step * kin[0]
        base_ref[s, 2] = values[2] - time_step * kin[3]
        base_ref[s, 3] = values[3] + time_step * kin[2]
        return 0

    lax.fori_loop(0, states, one_state, 0)


def gather(where, shift, wave, weights, mine, pieces, count, planes, depth, *after):
    arrays, starts = zip(*pieces)
    shape = jax.ShapeDtypeStruct((count, 4, planes + 2 * HALO, SUBS, LANES), jnp.float32)
    return pl.pallas_call(
        functools.partial(gather_kernel, depth, planes, mine, starts),
        out_shape=[shape] * 2,
        in_specs=[SMEM] * 3 + [VMEM] * 5 + [ANYWHERE] * len(after),
        out_specs=[VMEM] * 2,
        scratch_shapes=[pltpu.VMEM((2, 4 * planes, SUBS, LANES), jnp.float32), pltpu.VMEM((4, 4 * planes, SUBS, LANES), jnp.float32)],
        compiler_params=params(),
        name="gather",
    )(where, shift, wave, weights, *arrays, *after)


def density_kernel(pieces, fields, *refs):
    boosted_refs, base_refs = refs[:pieces], refs[pieces : 2 * pieces]
    out_ref, sums = refs[2 * pieces :]
    planes = sums.shape[1]
    for z in range(planes):
        field = [fields[f, HALO + z] for f in range(3)]
        total = [jnp.zeros((SUBS, LANES), jnp.float32)] * 3
        for boosted, base in zip(boosted_refs, base_refs):
            for s in range(boosted.shape[0]):
                part = local_part(field, *[boosted[s, k, HALO + z] for k in range(4)])
                pr = base[s, 0, HALO + z] + time_step * part[1]
                pi = base[s, 1, HALO + z] - time_step * part[0]
                hr = base[s, 2, HALO + z] + time_step * part[3]
                hi = base[s, 3, HALO + z] - time_step * part[2]
                total = [a + b for a, b in zip(total, densities(pr, pi, hr, hi))]
        for f in range(3):
            sums[f, z] = total[f]
    for f in range(3):
        for t in range(SUBS):
            out_ref[f, :, t * LANES : (t + 1) * LANES] = sums[f, :, t, :]


def density(fields, boosted, base, planes):
    pieces = len(boosted)
    return pl.pallas_call(
        functools.partial(density_kernel, pieces),
        out_shape=jax.ShapeDtypeStruct((3, planes, SUBS * LANES), jnp.float32),
        in_specs=[VMEM] * (1 + 2 * pieces),
        out_specs=VMEM,
        scratch_shapes=[pltpu.VMEM((3, planes, SUBS, LANES), jnp.float32)],
        compiler_params=params(),
        name="density",
    )(fields, *boosted, *base)


def free_kernel(places, where_ref, weights_ref, fields, *refs):
    pieces = len(places)
    boosted_refs, base_refs = refs[:pieces], refs[pieces : 2 * pieces]
    free_ref, predicted_ref, window, turned = refs[2 * pieces :]
    planes = free_ref.shape[3]
    inner = pl.ds(HALO, planes)
    odd = lax.rem(where_ref[0], 2)
    for (mine, first, count), boosted, base in zip(places, boosted_refs, base_refs):
        j = odd if mine else 1 - odd

        def one_state(s, _):
            for z in range(planes + 2 * HALO):
                field = [fields[f, z] for f in range(3)]
                part = local_part(field, *[boosted[s, k, z] for k in range(4)])
                window[0, z] = base[s, 0, z] + time_step * part[1]
                window[1, z] = base[s, 1, z] - time_step * part[0]
                window[2, z] = base[s, 2, z] + time_step * part[3]
                window[3, z] = base[s, 3, z] - time_step * part[2]
            kin = kinetic(window[...], weights_ref[...])
            mean = [0.5 * (boosted[s, k, inner] + window[k, inner]) for k in range(4)]
            half = 0.5 * time_step
            turned[0] = mean[0] + half * kin[1]
            turned[1] = mean[1] - half * kin[0]
            turned[2] = mean[2] - half * kin[3]
            turned[3] = mean[3] + half * kin[2]
            for k in range(4):
                for t in range(SUBS):
                    lanes = pl.ds(t * LANES, LANES)
                    free_ref[j, first + s, k, :, lanes] = turned[k, :, t, :]
                    predicted_ref[j, first + s, k, :, lanes] = window[k, inner, t, :]
            return 0

        lax.fori_loop(0, count, one_state, 0)


def free_part(where, weights, fields, boosted, base, places, shape, planes):
    pieces = len(places)
    out = jax.ShapeDtypeStruct(shape, jnp.float32)
    return pl.pallas_call(
        functools.partial(free_kernel, places),
        out_shape=[out] * 2,
        in_specs=[SMEM] + [VMEM] * (2 + 2 * pieces),
        out_specs=[VMEM] * 2,
        scratch_shapes=[
            pltpu.VMEM((4, planes + 2 * HALO, SUBS, LANES), jnp.float32),
            pltpu.VMEM((4, planes, SUBS, LANES), jnp.float32),
        ],
        compiler_params=params(),
        name="free_part",
    )(where, weights, fields, *boosted, *base)


def last_kernel(scale, *refs):
    partial_refs = refs[:-4]
    free_ref, predicted_ref, out_ref, fields = refs[-4:]

    @pl.when(pl.program_id(0) == 0)
    def _():
        totals = []
        for f in range(3):
            total = partial_refs[0][f]
            for ref in partial_refs[1:]:
                total = total + ref[f]
            totals.append(total)
        for f, field in enumerate(fields_of(*totals, scale)):
            fields[f] = field

    half = 0.5 * time_step
    for t in range(free_ref.shape[-1] // LANES):
        lanes = pl.ds(t * LANES, LANES)
        field = [fields[f, :, lanes] for f in range(3)]
        for s in range(free_ref.shape[1]):
            part = local_part(field, *[predicted_ref[0, s, k, :, lanes] for k in range(4)])
            out_ref[0, s, 0, :, lanes] = free_ref[0, s, 0, :, lanes] + half * part[1]
            out_ref[0, s, 1, :, lanes] = free_ref[0, s, 1, :, lanes] - half * part[0]
            out_ref[0, s, 2, :, lanes] = free_ref[0, s, 2, :, lanes] + half * part[3]
            out_ref[0, s, 3, :, lanes] = free_ref[0, s, 3, :, lanes] - half * part[2]


def last_part(partials, free, predicted, scale):
    shape = free.shape
    whole = pl.BlockSpec(partials[0].shape, lambda i: (0, 0, 0))
    block = pl.BlockSpec((1, *shape[1:]), lambda i: (i, 0, 0, 0, 0))
    return pl.pallas_call(
        functools.partial(last_kernel, scale),
        out_shape=jax.ShapeDtypeStruct(shape, jnp.float32),
        grid=(shape[0],),
        in_specs=[whole] * len(partials) + [block] * 2,
        out_specs=block,
        scratch_shapes=[pltpu.VMEM(partials[0].shape, jnp.float32)],
        compiler_params=params(),
        name="last_part",
    )(*partials, free, predicted)


def local(weights, cloud_states, cloud_shift, boost_wave):
    slab_count, group_count = lax.axis_size("slab"), lax.axis_size("grp")
    _, per_group, _, planes, cells = cloud_states.shape
    depth = planes * slab_count
    scale = 1.0 / (per_group * group_count)
    where = lax.axis_index("slab").astype(jnp.int32).reshape(1)

    even_on = lambda a: lax.ppermute(a, "slab", [(i, (i - 2 if i % 2 else i + 2) % slab_count) for i in range(slab_count)])
    odd_on = lambda a: lax.ppermute(a, "slab", [(i, (i + 2 if i % 2 else i - 2) % slab_count) for i in range(slab_count)])
    across = lambda a: lax.ppermute(a, "slab", [(i, (i + 3 if i % 2 else i - 3) % slab_count) for i in range(slab_count)])

    def group_terms(a):
        if group_count > 4:
            return [lax.psum(a, "grp")]
        return [a] + [moved(a, "grp", d) for d in range(1, group_count)]

    chunks = [(0, per_group)]
    mine = [take(where, cloud_states, True, *chunk) for chunk in chunks]
    mine_second = [even_on(piece) for piece in mine]
    other = [take(where, cloud_states, False, *chunk) for chunk in chunks]
    other_second = [odd_on(piece) for piece in other]
    terms = group_terms(raw_density(cloud_states, *mine, *other))
    mine_sums, other_sums = total_of(where, terms, *mine_second)
    extra = across(take_extra(where, cloud_states, mine[0]))

    mine_sums_second, other_sums_second, far_sums = even_on(mine_sums), odd_on(other_sums), across(other_sums)
    other_next = swapped(mine[0])
    other_far = swapped(mine_second[0])
    joined = join([mine_sums_second, other_sums_second, mine_sums], extra, far_sums)
    swapped_sums = swapped(joined)
    swapped_sums = [swapped_sums[3 * n : 3 * n + 3] for n in range(3)]
    mine_next = [swapped(piece) for piece in other_second]
    work = lambda *a: gather(where, cloud_shift, boost_wave, weights, *a, planes, depth)
    places, worked = [], []
    for n, (first, count) in enumerate(chunks):
        worked.append(work(False, [(other_far, first), (other_second[n], 0), (other_next, first), (other[n], 0)], count))
        places.append((False, first, count))
    fields = placed_fields(
        where, cloud_shift, boost_wave, [far_sums, mine_sums_second, swapped_sums[1], mine_sums],
        [swapped_sums[0], other_sums_second, swapped_sums[2], other_sums], depth, scale, *[piece[0] for piece in worked],
    )
    for n, (first, count) in enumerate(chunks):
        worked.append(work(True, [(extra, first), (mine_second[n], 0), (mine_next[n], 0), (mine[n], 0)], count))
        places.append((True, first, count))
    boosted, base = [list(part) for part in zip(*worked)]
    partials = group_terms(density(fields, boosted, base, planes))
    free, predicted = free_part(where, weights, fields, boosted, base, tuple(places), cloud_states.shape, planes)
    return last_part(partials, free, predicted, scale)


def solution(mesh):
    states = P(None, "grp", None, "slab", None)
    weights = transverse_weights()
    step = jax.shard_map(local, mesh=mesh, in_specs=(P(), states, P(), P()), out_specs=states, check_vma=False)
    return lambda cloud_states, cloud_shift, boost_wave: step(weights, cloud_states, cloud_shift, boost_wave)
```

time: 69.3 us -> 55 us (0.79)
  starting transfers between devices: 29.5 us -> 23.7 us
  Pallas kernels: 14.7 us -> 11.2 us
  waiting for transfers between devices: 21.8 us -> 18.4 us
  other arithmetic: 1.28 us -> 0 us
    ppermute x19 -> x6, starting transfers between devices: 25.9 us -> 14.1 us  [moved(): return lax.ppermute(x, axis, [(i, (i + by) % peers) for i in range(peers)])]
    ppermute x19 -> x6, waiting for transfers between devices: 21.8 us -> 11.6 us  [moved(): return lax.ppermute(x, axis, [(i, (i + by) % peers) for i in range(peers)])]
    ppermute x1 -> x6, waiting for transfers between devices: 0.01 us -> 5.46 us  [the longest x2 3.2 us: local(): lax.ppermute(a, 'slab', [(i, (i - 2 if i % 2 else i + 2) % slab_count) fo...]
    ppermute x1 -> x6, starting transfers between devices: 3.07 us -> 8.52 us  [the longest x2 6.33 us: local(): lax.ppermute(a, 'slab', [(i, (i - 2 if i % 2 else i + 2) % slab_count) fo...]
    pallas_call x5 -> x10, Pallas kernels: 12.8 us -> 8.91 us  [the longest x2 4.11 us: gather(): pl.pallas_call(functools.partial(gather_kernel, depth, planes, mine, star...]
    ppermute x5 -> x4, waiting for transfers between devices: 0.01 us -> 1.29 us  [swapped(): return lax.ppermute(x, 'slab', [(i, i ^ 1) for i in range(peers)])]
    select_n x1 -> x0, other arithmetic: 1.27 us -> none  [local(): jnp.where(odd, cloud_states[0, :, :, planes - extra_layers:], cloud_state...]
    squeeze x2 -> x0, local copies, waits for them, and re-layouts: 1.26 us -> none  [the longest x1 1.26 us: local(): cloud_states[1, states]]
  transfers between devices with their start and end apart: 25 -> 16, of which waited for: 9 -> 9; matrix products, arithmetic and copies ran while one was open for 4% -> 0% of each run, Pallas kernels for 17% -> 11%
where the time goes in v2:
time: 55 us; the launch traced here: 54.8 us
  starting transfers between devices  23.7 us (43%)
  waiting for transfers between devices  18.4 us (33%)
  Pallas kernels  11.2 us (20%)
  local copies, waits for them, and re-layouts  1.27 us (2%)
    ppermute x6, starting transfers between devices, moved(): return lax.ppermute(x, axis, [(i, (i + by) % peers) for i in range(peers)])  14.1 us
    ppermute x6, waiting for transfers between devices, moved(): return lax.ppermute(x, axis, [(i, (i + by) % peers) for i in range(peers)])  11.6 us
    ppermute x2, starting transfers between devices, local(): lax.ppermute(a, 'slab', [(i, (i - 2 if i % 2 else i + 2) % slab_count) fo...  6.33 us
    pallas_call x2, Pallas kernels, gather(): pl.pallas_call(functools.partial(gather_kernel, depth, planes, mine, star...  4.11 us
    pallas_call x1, Pallas kernels, free_part(): pl.pallas_call(functools.partial(free_kernel, places), out_shape=[out] *...  3.33 us
    ppermute x2, waiting for transfers between devices, local(): lax.ppermute(a, 'slab', [(i, (i - 2 if i % 2 else i + 2) % slab_count) fo...  3.2 us
    ppermute x2, starting transfers between devices, local(): lax.ppermute(a, 'slab', [(i, (i + 2 if i % 2 else i - 2) % slab_count) fo...  2.05 us
    ppermute x2, waiting for transfers between devices, local(): lax.ppermute(a, 'slab', [(i, (i + 2 if i % 2 else i - 2) % slab_count) fo...  2.01 us
  transfers between devices with their start and end apart: 16, of which 9 were waited for; matrix products, arithmetic and copies ran while one was open for 0% of the time, Pallas kernels for 11%

profile of v2, /device:TPU:0, one launch (start us, length us, event | category | flops | bytes accessed | tf_op | source)
XLA Modules:
  0.0 54.8 jit_solution(17505744413244193284)
XLA Ops:
  0.0 1.2 %copy-done = f32[2,4,4,8,1024]{4,3,2,1,0:T(8,128)S(1)} copy-done((f32[2,4,4,8,1024]{4,3,2,1,0:T(8,128)S(1)}, f32[2,4,4,8,1024]{4,3,2,1,0:T(8,128)}, u32[]{:S(2)}) %copy-start) | copy-done | bytes 1048600
  1.5 3.0 %collective-permute-start.3 = (f32[128,8,128]{2,1,0:T(8,128)S(1)}, f32[128,8,128]{2,1,0:T(8,128)S(1)}, u32[]{:S(2)}, u32[]{:S(2)}) collective-permute-start(f32[128,8,128]{2,1,0:T(8,128)S(1)} %take.2.refs_0_.own_ref), channel_id=1, source_target_pairs={{0,8},{4,28},{8,16},{12,4},{16,24},{20,12},{24,0},{28,20},{1,9},{5... | collective-permute-start | bytes 1572872 | tf_op jit(solution)/shard_map/ppermute | solution.py:486
  4.8 1.0 %collective-permute-start.10 = (f32[128,8,128]{2,1,0:T(8,128)S(1)}, f32[128,8,128]{2,1,0:T(8,128)S(1)}, u32[]{:S(2)}, u32[]{:S(2)}) collective-permute-start(f32[128,8,128]{2,1,0:T(8,128)S(1)} %take.3.refs_1_.own_ref), channel_id=1, source_target_pairs={{0,24},{4,12},{8,0},{12,20},{16,8},{20,28},{24,16},{28,4},{1,25},{... | collective-permute-start | bytes 1572872 | tf_op jit(solution)/shard_map/ppermute | solution.py:487
  6.0 2.1 %collective-permute-start = (f32[2,3,8,1024]{3,2,1,0:T(8,128)S(1)}, f32[2,3,8,1024]{3,2,1,0:T(8,128)S(1)}, u32[]{:S(2)}, u32[]{:S(2)}) collective-permute-start(f32[2,3,8,1024]{3,2,1,0:T(8,128)S(1)} %raw_density.1.refs_0_), channel_id=1, source_target_pairs={{0,1},{1,2},{2,3},{3,0},{4,5},{5,6},{6,7},{7,4},{8,9},{9,10},{10,1... | collective-permute-start | bytes 589832 | tf_op jit(solution)/shard_map/ppermute | solution.py:36
  8.5 2.7 %collective-permute-start.1 = (f32[2,3,8,1024]{3,2,1,0:T(8,128)S(1)}, f32[2,3,8,1024]{3,2,1,0:T(8,128)S(1)}, u32[]{:S(2)}, u32[]{:S(2)}) collective-permute-start(f32[2,3,8,1024]{3,2,1,0:T(8,128)S(1)} %raw_density.1.refs_0_), channel_id=1, source_target_pairs={{0,2},{1,3},{2,0},{3,1},{4,6},{5,7},{6,4},{7,5},{8,10},{9,11},{10,... | collective-permute-start | bytes 589832 | tf_op jit(solution)/shard_map/ppermute | solution.py:36
  11.1 3.2 %collective-permute-done.refs_1_ = f32[2,3,8,1024]{3,2,1,0:T(8,128)S(1)} collective-permute-done((f32[2,3,8,1024]{3,2,1,0:T(8,128)S(1)}, f32[2,3,8,1024]{3,2,1,0:T(8,128)S(1)}, u32[]{:S(2)}, u32[]{:S(2)}) %collective-permute-start) | collective-permute-done | bytes 196640 | tf_op jit(solution)/shard_map/ppermute | solution.py:36
  14.3 2.3 %collective-permute-start.2 = (f32[2,3,8,1024]{3,2,1,0:T(8,128)S(1)}, f32[2,3,8,1024]{3,2,1,0:T(8,128)S(1)}, u32[]{:S(2)}, u32[]{:S(2)}) collective-permute-start(f32[2,3,8,1024]{3,2,1,0:T(8,128)S(1)} %raw_density.1.refs_0_), channel_id=1, source_target_pairs={{0,3},{1,0},{2,1},{3,2},{4,7},{5,4},{6,5},{7,6},{8,11},{9,8},{10,9... | collective-permute-start | bytes 589832 | tf_op jit(solution)/shard_map/ppermute | solution.py:36
  16.7 6.0 %collective-permute-done.1.refs_2_ = f32[2,3,8,1024]{3,2,1,0:T(8,128)S(1)} collective-permute-done((f32[2,3,8,1024]{3,2,1,0:T(8,128)S(1)}, f32[2,3,8,1024]{3,2,1,0:T(8,128)S(1)}, u32[]{:S(2)}, u32[]{:S(2)}) %collective-permute-start.1) | collective-permute-done | bytes 196640 | tf_op jit(solution)/shard_map/ppermute | solution.py:36
  22.7 1.4 %collective-permute-done.2.refs_3_ = f32[2,3,8,1024]{3,2,1,0:T(8,128)S(1)} collective-permute-done((f32[2,3,8,1024]{3,2,1,0:T(8,128)S(1)}, f32[2,3,8,1024]{3,2,1,0:T(8,128)S(1)}, u32[]{:S(2)}, u32[]{:S(2)}) %collective-permute-start.2) | collective-permute-done | bytes 196640 | tf_op jit(solution)/shard_map/ppermute | solution.py:36
  24.2 3.3 %collective-permute-start.5 = (f32[3,8,1024]{2,1,0:T(8,128)S(1)}, f32[3,8,1024]{2,1,0:T(8,128)S(1)}, u32[]{:S(2)}, u32[]{:S(2)}) collective-permute-start(f32[3,8,1024]{2,1,0:T(8,128)S(1)} %get-tuple-element.14.refs_2_.refs_3_), channel_id=1, source_target_pairs={{0,8},{4,28},{8,16},{12,4},{16,24},{20,12},{24,0},{28,20},{1,9},{5... | collective-permute-start | bytes 294920 | tf_op jit(solution)/shard_map/ppermute | solution.py:486
  27.6 1.0 %collective-permute-start.6 = (f32[3,8,1024]{2,1,0:T(8,128)S(1)}, f32[3,8,1024]{2,1,0:T(8,128)S(1)}, u32[]{:S(2)}, u32[]{:S(2)}) collective-permute-start(f32[3,8,1024]{2,1,0:T(8,128)S(1)} %get-tuple-element.13.refs_7_), channel_id=1, source_target_pairs={{0,24},{4,12},{8,0},{12,20},{16,8},{20,28},{24,16},{28,4},{1,25},{... | collective-permute-start | bytes 294920 | tf_op jit(solution)/shard_map/ppermute | solution.py:487
  28.9 3.2 %collective-permute-done.5.refs_0_.refs_1_ = f32[3,8,1024]{2,1,0:T(8,128)S(1)} collective-permute-done((f32[3,8,1024]{2,1,0:T(8,128)S(1)}, f32[3,8,1024]{2,1,0:T(8,128)S(1)}, u32[]{:S(2)}, u32[]{:S(2)}) %collective-permute-start.5) | collective-permute-done | bytes 98336 | tf_op jit(solution)/shard_map/ppermute | solution.py:486
  32.0 2.0 %collective-permute-done.6.refs_1_.refs_5_ = f32[3,8,1024]{2,1,0:T(8,128)S(1)} collective-permute-done((f32[3,8,1024]{2,1,0:T(8,128)S(1)}, f32[3,8,1024]{2,1,0:T(8,128)S(1)}, u32[]{:S(2)}, u32[]{:S(2)}) %collective-permute-start.6) | collective-permute-done | bytes 98336 | tf_op jit(solution)/shard_map/ppermute | solution.py:487
  35.2 0.6 %collective-permute-done.8 = f32[9,8,1024]{2,1,0:T(8,128)S(1)} collective-permute-done((f32[9,8,1024]{2,1,0:T(8,128)S(1)}, f32[9,8,1024]{2,1,0:T(8,128)S(1)}, u32[]{:S(2)}, u32[]{:S(2)}) %collective-permute-start.8) | collective-permute-done | bytes 294944 | tf_op jit(solution)/shard_map/ppermute | solution.py:41
  35.8 0.7 %collective-permute-done.12.next_ref = f32[128,8,128]{2,1,0:T(8,128)S(1)} collective-permute-done((f32[128,8,128]{2,1,0:T(8,128)S(1)}, f32[128,8,128]{2,1,0:T(8,128)S(1)}, u32[]{:S(2)}, u32[]{:S(2)}) %collective-permute-start.12) | collective-permute-done | bytes 524320 | tf_op jit(solution)/shard_map/ppermute | solution.py:41
  36.5 2.1 %gather.3 = (f32[4,4,14,8,128]{4,3,2,1,0:T(8,128)S(1)}, f32[4,4,14,8,128]{4,3,2,1,0:T(8,128)S(1)}) custom-call(s32[1]{0:T(128)} %bitcast.where_ref, s32[2]{0:T(128)S(1)} %copy-done.3, s32[2]{0:T(128)S(1)} %copy-done.4, bf16[256,384]{1,0:T(8,128)(2,1)S(1)} %copy-done.2, f32[80,8,128]{2,1,0:T(8,128)S(1)} %collective-permute-done.7.refs_3_.far_ref, ...), custom_call_target="tpu_custom_call" | custom-call | tf_op jit(solution)/shard_map/gather/pallas_call | solution.py:338
  38.6 2.0 %gather.2 = (f32[4,4,14,8,128]{4,3,2,1,0:T(8,128)S(1)}, f32[4,4,14,8,128]{4,3,2,1,0:T(8,128)S(1)}) custom-call(s32[1]{0:T(128)} %bitcast.where_ref, s32[2]{0:T(128)S(1)} %copy-done.3, s32[2]{0:T(128)S(1)} %copy-done.4, bf16[256,384]{1,0:T(8,128)(2,1)S(1)} %copy-done.2, f32[128,8,128]{2,1,0:T(8,128)S(1)} %collective-permute-done.9.far_ref, ...), custom_call_target="tpu_custom_call" | custom-call | tf_op jit(solution)/shard_map/gather/pallas_call | solution.py:338
  40.7 1.2 %placed_fields.1.fields = f32[3,14,8,128]{3,2,1,0:T(8,128)S(1)} custom-call(s32[1]{0:T(128)} %bitcast.where_ref, s32[2]{0:T(128)S(1)} %copy-done.3, s32[2]{0:T(128)S(1)} %copy-done.4, f32[3,8,1024]{2,1,0:T(8,128)S(1)} %collective-permute-done.4.refs_4_.refs_0_, f32[3,8,1024]{2,1,0:T(8,128)S(1)} %collective-permute-done.5.refs_0_.refs_1_, ...), custom_call_target="tpu_custom_call" | custom-call | tf_op jit(solution)/shard_map/placed_fields/pallas_call | solution.py:253
  42.3 2.7 %collective-permute-start.13 = (f32[3,8,1024]{2,1,0:T(8,128)S(1)}, f32[3,8,1024]{2,1,0:T(8,128)S(1)}, u32[]{:S(2)}, u32[]{:S(2)}) collective-permute-start(f32[3,8,1024]{2,1,0:T(8,128)S(1)} %density.1.refs_0_), channel_id=1, source_target_pairs={{0,1},{1,2},{2,3},{3,0},{4,5},{5,6},{6,7},{7,4},{8,9},{9,10},{10,1... | collective-permute-start | bytes 294920 | tf_op jit(solution)/shard_map/ppermute | solution.py:36
  44.9 1.5 %collective-permute-start.14 = (f32[3,8,1024]{2,1,0:T(8,128)S(1)}, f32[3,8,1024]{2,1,0:T(8,128)S(1)}, u32[]{:S(2)}, u32[]{:S(2)}) collective-permute-start(f32[3,8,1024]{2,1,0:T(8,128)S(1)} %density.1.refs_0_), channel_id=1, source_target_pairs={{0,2},{1,3},{2,0},{3,1},{4,6},{5,7},{6,4},{7,5},{8,10},{9,11},{10,... | collective-permute-start | bytes 294920 | tf_op jit(solution)/shard_map/ppermute | solution.py:36
  46.5 2.8 %collective-permute-start.15 = (f32[3,8,1024]{2,1,0:T(8,128)S(1)}, f32[3,8,1024]{2,1,0:T(8,128)S(1)}, u32[]{:S(2)}, u32[]{:S(2)}) collective-permute-start(f32[3,8,1024]{2,1,0:T(8,128)S(1)} %density.1.refs_0_), channel_id=1, source_target_pairs={{0,3},{1,0},{2,1},{3,2},{4,7},{5,4},{6,5},{7,6},{8,11},{9,8},{10,9... | collective-permute-start | bytes 294920 | tf_op jit(solution)/shard_map/ppermute | solution.py:36
  49.3 3.3 %free_part.1 = (f32[2,4,4,8,1024]{4,3,2,1,0:T(8,128)S(1)}, f32[2,4,4,8,1024]{4,3,2,1,0:T(8,128)S(1)}) custom-call(s32[1]{0:T(128)} %bitcast.where_ref, bf16[256,384]{1,0:T(8,128)(2,1)S(1)} %copy-done.2, f32[3,14,8,128]{3,2,1,0:T(8,128)S(1)} %placed_fields.1.fields, f32[4,4,14,8,128]{4,3,2,1,0:T(8,128)S(1)} %get-tuple-element.15.refs_8_.refs_0_, ...), custom_call_target="tpu_custom_call" | custom-call | tf_op jit(solution)/shard_map/free_part/pallas_call | solution.py:422
  52.7 1.0 %collective-permute-done.14.refs_2_ = f32[3,8,1024]{2,1,0:T(8,128)S(1)} collective-permute-done((f32[3,8,1024]{2,1,0:T(8,128)S(1)}, f32[3,8,1024]{2,1,0:T(8,128)S(1)}, u32[]{:S(2)}, u32[]{:S(2)}) %collective-permute-start.14) | collective-permute-done | bytes 98336 | tf_op jit(solution)/shard_map/ppermute | solution.py:36
  53.6 1.1 %last_part.1 = f32[2,4,4,8,1024]{4,3,2,1,0:T(8,128)} custom-call(f32[3,8,1024]{2,1,0:T(8,128)S(1)} %density.1.refs_0_, f32[3,8,1024]{2,1,0:T(8,128)S(1)} %collective-permute-done.13.refs_1_, f32[3,8,1024]{2,1,0:T(8,128)S(1)} %collective-permute-done.14.refs_2_, f32[3,8,1024]{2,1,0:T(8,128)S(1)} %collective-permute-done.15.refs_3_, ...), custom_call_target="tpu_custom_call" | custom-call | tf_op jit(solution)/shard_map/last_part/pallas_call | solution.py:467
  (31 shorter events, 3.0 us)
Async XLA Ops:
  0.0 1.2 %copy-start = (f32[2,4,4,8,1024]{4,3,2,1,0:T(8,128)S(1)}, f32[2,4,4,8,1024]{4,3,2,1,0:T(8,128)}, u32[]{:S(2)}) copy-start(f32[2,4,4,8,1024]{4,3,2,1,0:T(8,128)} %x_ref.7) | copy-start | bytes 3145732
  1.5 4.3 %copy-start.1 = (f32[2,4,4,8,1024]{4,3,2,1,0:T(8,128)S(1)}, f32[2,4,4,8,1024]{4,3,2,1,0:T(8,128)}, u32[]{:S(2)}) copy-start(f32[2,4,4,8,1024]{4,3,2,1,0:T(8,128)} %x_ref.7) | copy-start | bytes 3145732
  1.5 22.6 %collective-permute-start.3 = (f32[128,8,128]{2,1,0:T(8,128)S(1)}, f32[128,8,128]{2,1,0:T(8,128)S(1)}, u32[]{:S(2)}, u32[]{:S(2)}) collective-permute-start(f32[128,8,128]{2,1,0:T(8,128)S(1)} %take.2.refs_0_.own_ref), channel_id=1, source_target_pairs={{0,8},{4,28},{8,16},{12,4},{16,24},{20,12},{24,0},{28,20},{1,9},{5... | collective-permute-start | bytes 1572872 | tf_op jit(solution)/shard_map/ppermute | solution.py:486
  4.8 29.4 %collective-permute-start.10 = (f32[128,8,128]{2,1,0:T(8,128)S(1)}, f32[128,8,128]{2,1,0:T(8,128)S(1)}, u32[]{:S(2)}, u32[]{:S(2)}) collective-permute-start(f32[128,8,128]{2,1,0:T(8,128)S(1)} %take.3.refs_1_.own_ref), channel_id=1, source_target_pairs={{0,24},{4,12},{8,0},{12,20},{16,8},{20,28},{24,16},{28,4},{1,25},{... | collective-permute-start | bytes 1572872 | tf_op jit(solution)/shard_map/ppermute | solution.py:487
  6.0 8.4 %collective-permute-start = (f32[2,3,8,1024]{3,2,1,0:T(8,128)S(1)}, f32[2,3,8,1024]{3,2,1,0:T(8,128)S(1)}, u32[]{:S(2)}, u32[]{:S(2)}) collective-permute-start(f32[2,3,8,1024]{3,2,1,0:T(8,128)S(1)} %raw_density.1.refs_0_), channel_id=1, source_target_pairs={{0,1},{1,2},{2,3},{3,0},{4,5},{5,6},{6,7},{7,4},{8,9},{9,10},{10,1... | collective-permute-start | bytes 589832 | tf_op jit(solution)/shard_map/ppermute | solution.py:36
  8.4 20.2 %collective-permute-start.7 = (f32[80,8,128]{2,1,0:T(8,128)S(1)}, f32[80,8,128]{2,1,0:T(8,128)S(1)}, u32[]{:S(2)}, u32[]{:S(2)}) collective-permute-start(f32[80,8,128]{2,1,0:T(8,128)S(1)} %take_extra.1), channel_id=1, source_target_pairs={{0,20},{4,16},{8,28},{12,24},{16,4},{20,0},{24,12},{28,8},{1,21},{... | collective-permute-start | bytes 983048 | tf_op jit(solution)/shard_map/ppermute | solution.py:488
  8.5 14.3 %collective-permute-start.1 = (f32[2,3,8,1024]{3,2,1,0:T(8,128)S(1)}, f32[2,3,8,1024]{3,2,1,0:T(8,128)S(1)}, u32[]{:S(2)}, u32[]{:S(2)}) collective-permute-start(f32[2,3,8,1024]{3,2,1,0:T(8,128)S(1)} %raw_density.1.refs_0_), channel_id=1, source_target_pairs={{0,2},{1,3},{2,0},{3,1},{4,6},{5,7},{6,4},{7,5},{8,10},{9,11},{10,... | collective-permute-start | bytes 589832 | tf_op jit(solution)/shard_map/ppermute | solution.py:36
  14.3 9.8 %collective-permute-start.2 = (f32[2,3,8,1024]{3,2,1,0:T(8,128)S(1)}, f32[2,3,8,1024]{3,2,1,0:T(8,128)S(1)}, u32[]{:S(2)}, u32[]{:S(2)}) collective-permute-start(f32[2,3,8,1024]{3,2,1,0:T(8,128)S(1)} %raw_density.1.refs_0_), channel_id=1, source_target_pairs={{0,3},{1,0},{2,1},{3,2},{4,7},{5,4},{6,5},{7,6},{8,11},{9,8},{10,9... | collective-permute-start | bytes 589832 | tf_op jit(solution)/shard_map/ppermute | solution.py:36
  24.2 4.7 %collective-permute-start.4 = (f32[3,8,1024]{2,1,0:T(8,128)S(1)}, f32[3,8,1024]{2,1,0:T(8,128)S(1)}, u32[]{:S(2)}, u32[]{:S(2)}) collective-permute-start(f32[3,8,1024]{2,1,0:T(8,128)S(1)} %get-tuple-element.13.refs_7_), channel_id=1, source_target_pairs={{0,20},{4,16},{8,28},{12,24},{16,4},{20,0},{24,12},{28,8},{1,21},{... | collective-permute-start | bytes 294920 | tf_op jit(solution)/shard_map/ppermute | solution.py:488
  24.2 7.8 %collective-permute-start.5 = (f32[3,8,1024]{2,1,0:T(8,128)S(1)}, f32[3,8,1024]{2,1,0:T(8,128)S(1)}, u32[]{:S(2)}, u32[]{:S(2)}) collective-permute-start(f32[3,8,1024]{2,1,0:T(8,128)S(1)} %get-tuple-element.14.refs_2_.refs_3_), channel_id=1, source_target_pairs={{0,8},{4,28},{8,16},{12,4},{16,24},{20,12},{24,0},{28,20},{1,9},{5... | collective-permute-start | bytes 294920 | tf_op jit(solution)/shard_map/ppermute | solution.py:486
  27.6 6.5 %collective-permute-start.6 = (f32[3,8,1024]{2,1,0:T(8,128)S(1)}, f32[3,8,1024]{2,1,0:T(8,128)S(1)}, u32[]{:S(2)}, u32[]{:S(2)}) collective-permute-start(f32[3,8,1024]{2,1,0:T(8,128)S(1)} %get-tuple-element.13.refs_7_), channel_id=1, source_target_pairs={{0,24},{4,12},{8,0},{12,20},{16,8},{20,28},{24,16},{28,4},{1,25},{... | collective-permute-start | bytes 294920 | tf_op jit(solution)/shard_map/ppermute | solution.py:487
  34.1 2.4 %copy-start.2 = (bf16[256,384]{1,0:T(8,128)(2,1)S(1)}, bf16[256,384]{1,0:T(8,128)(2,1)}, u32[]{:S(2)}) copy-start(bf16[256,384]{1,0:T(8,128)(2,1)} %constant.8.clone.weights_ref) | copy-start | bytes 589828
  34.1 2.4 %copy-start.3 = (s32[2]{0:T(128)S(1)}, s32[2]{0:T(128)}, u32[]{:S(2)}) copy-start(s32[2]{0:T(128)} %shift_ref.5) | copy-start | bytes 28
  34.1 2.4 %copy-start.4 = (s32[2]{0:T(128)S(1)}, s32[2]{0:T(128)}, u32[]{:S(2)}) copy-start(s32[2]{0:T(128)} %wave_ref.5) | copy-start | bytes 28
  34.1 1.6 %collective-permute-start.8 = (f32[9,8,1024]{2,1,0:T(8,128)S(1)}, f32[9,8,1024]{2,1,0:T(8,128)S(1)}, u32[]{:S(2)}, u32[]{:S(2)}) collective-permute-start(f32[9,8,1024]{2,1,0:T(8,128)S(1)} %join.1), channel_id=1, source_target_pairs={{0,4},{4,0},{8,12},{12,8},{16,20},{20,16},{24,28},{28,24},{1,5},{5... | collective-permute-start | bytes 884744 | tf_op jit(solution)/shard_map/ppermute | solution.py:41
  34.2 2.3 %collective-permute-start.12 = (f32[128,8,128]{2,1,0:T(8,128)S(1)}, f32[128,8,128]{2,1,0:T(8,128)S(1)}, u32[]{:S(2)}, u32[]{:S(2)}) collective-permute-start(f32[128,8,128]{2,1,0:T(8,128)S(1)} %collective-permute-done.10.second_ref), channel_id=1, source_target_pairs={{0,4},{4,0},{8,12},{12,8},{16,20},{20,16},{24,28},{28,24},{1,5},{5... | collective-permute-start | bytes 1572872 | tf_op jit(solution)/shard_map/ppermute | solution.py:41
  34.7 3.9 %collective-permute-start.11 = (f32[128,8,128]{2,1,0:T(8,128)S(1)}, f32[128,8,128]{2,1,0:T(8,128)S(1)}, u32[]{:S(2)}, u32[]{:S(2)}) collective-permute-start(f32[128,8,128]{2,1,0:T(8,128)S(1)} %take.2.refs_0_.own_ref), channel_id=1, source_target_pairs={{0,4},{4,0},{8,12},{12,8},{16,20},{20,16},{24,28},{28,24},{1,5},{5... | collective-permute-start | bytes 1572872 | tf_op jit(solution)/shard_map/ppermute | solution.py:41
  34.8 3.8 %collective-permute-start.9 = (f32[128,8,128]{2,1,0:T(8,128)S(1)}, f32[128,8,128]{2,1,0:T(8,128)S(1)}, u32[]{:S(2)}, u32[]{:S(2)}) collective-permute-start(f32[128,8,128]{2,1,0:T(8,128)S(1)} %collective-permute-done.3.refs_4_.second_ref), channel_id=1, source_target_pairs={{0,4},{4,0},{8,12},{12,8},{16,20},{20,16},{24,28},{28,24},{1,5},{5... | collective-permute-start | bytes 1572872 | tf_op jit(solution)/shard_map/ppermute | solution.py:41
  42.3 10.4 %collective-permute-start.13 = (f32[3,8,1024]{2,1,0:T(8,128)S(1)}, f32[3,8,1024]{2,1,0:T(8,128)S(1)}, u32[]{:S(2)}, u32[]{:S(2)}) collective-permute-start(f32[3,8,1024]{2,1,0:T(8,128)S(1)} %density.1.refs_0_), channel_id=1, source_target_pairs={{0,1},{1,2},{2,3},{3,0},{4,5},{5,6},{6,7},{7,4},{8,9},{9,10},{10,1... | collective-permute-start | bytes 294920 | tf_op jit(solution)/shard_map/ppermute | solution.py:36
  44.9 8.7 %collective-permute-start.14 = (f32[3,8,1024]{2,1,0:T(8,128)S(1)}, f32[3,8,1024]{2,1,0:T(8,128)S(1)}, u32[]{:S(2)}, u32[]{:S(2)}) collective-permute-start(f32[3,8,1024]{2,1,0:T(8,128)S(1)} %density.1.refs_0_), channel_id=1, source_target_pairs={{0,2},{1,3},{2,0},{3,1},{4,6},{5,7},{6,4},{7,5},{8,10},{9,11},{10,... | collective-permute-start | bytes 294920 | tf_op jit(solution)/shard_map/ppermute | solution.py:36
  46.5 7.1 %collective-permute-start.15 = (f32[3,8,1024]{2,1,0:T(8,128)S(1)}, f32[3,8,1024]{2,1,0:T(8,128)S(1)}, u32[]{:S(2)}, u32[]{:S(2)}) collective-permute-start(f32[3,8,1024]{2,1,0:T(8,128)S(1)} %density.1.refs_0_), channel_id=1, source_target_pairs={{0,3},{1,0},{2,1},{3,2},{4,7},{5,4},{6,5},{7,6},{8,11},{9,8},{10,9... | collective-permute-start | bytes 294920 | tf_op jit(solution)/shard_map/ppermute | solution.py:36

commit v3 on v2

--- a/solution.py
+++ b/solution.py
@@ -163,6 +163,21 @@
         compiler_params=params(),
         name="join",
     )(*pieces, *after)
+
+
+def add_kernel(a_ref, b_ref, *refs):
+    refs[-1][...] = a_ref[...] + b_ref[...]
+
+
+def add(a, b, *after):
+    return pl.pallas_call(
+        add_kernel,
+        out_shape=jax.ShapeDtypeStruct(a.shape, a.dtype),
+        in_specs=[VMEM] * 2 + [ANYWHERE] * len(after),
+        out_specs=VMEM,
+        compiler_params=params(),
+        name="add",
+    )(a, b, *after)
 
 
 def total_kernel(count, where_ref, *refs):
@@ -280,12 +295,16 @@
     along = stencil[0] * inner
     for j in range(1, HALO + 1):
         along = along + stencil[j] * (layers[:, HALO - j : HALO - j + count] + layers[:, HALO + j : HALO + j + count])
-    across = transverse(inner.reshape(4 * count, SUBS, LANES), weights).reshape(inner.shape)
+    across = transverse(inner.reshape(-1, SUBS, LANES), weights).reshape(inner.shape)
     return -0.5 * along + (-0.5 / 180.0) * across
 
 
+def turned(u_re, u_im, v_re, v_im, cos, sin):
+    return u_re * cos - u_im * sin, u_re * sin + u_im * cos, v_re * cos + v_im * sin, v_im * cos - v_re * sin
+
+
 def gather_kernel(depth, planes, mine, starts, where_ref, shift_ref, wave_ref, weights_ref, far_ref, second_ref, next_ref, own_ref, *refs):
-    boosted_ref, base_ref, turns, window = refs[-4:]
+    windows, boosted_ref, base_ref, turns = refs[-4:]
     slab = where_ref[0]
     odd = lax.rem(slab, 2)
     cloud = odd if mine else 1 - odd
@@ -298,19 +317,16 @@
         for n, part in enumerate(phase(wave_ref[cloud], first_layer(cloud, slot, slab, planes, shift_ref), depth)):
             for z in range(planes):
                 turns[n, slot * planes + z] = jnp.broadcast_to(part[z : z + 1], (SUBS, LANES))
-    start = window_start(cloud, planes, REACH, shift_ref)
-
-    def one_state(s, _):
+    start = window_start(cloud, planes, HALO, shift_ref)
+
+    for s in range(states):
         def fill(place, ref, row, pitch, number):
             for n in range(number):
-                cos, sin = turns[0, place + n], turns[1, place + n]
-                u_re, u_im, v_re, v_im = [ref[row + k * pitch + n] for k in range(4)]
-                window[0, place + n] = u_re * cos - u_im * sin
-                window[1, place + n] = u_re * sin + u_im * cos
-                window[2, place + n] = v_re * cos + v_im * sin
-                window[3, place + n] = v_im * cos - v_re * sin
-
-        rows = [(start + s) * 4 * planes for start in starts]
+                parts = [ref[row + k * pitch + n] for k in range(4)]
+                for k, value in enumerate(turned(*parts, turns[0, place + n], turns[1, place + n])):
+                    windows[s, k, place + n] = value
+
+        rows = [(start_state + s) * 4 * planes for start_state in starts]
         if mine:
             fill(slots[0] * planes + far_edge, far_ref, (starts[0] + s) * 4 * layers, layers, layers)
         else:
@@ -319,7 +335,7 @@
         fill(slots[2] * planes, next_ref, rows[2], planes, planes)
         fill(slots[3] * planes + own_edge, own_ref, rows[3] + own_edge, planes, layers)
 
-        whole = window[:, pl.ds(start, count + 2 * HALO)]
+        whole = windows[s, :, pl.ds(start, count + 2 * HALO)]
         values = whole[:, HALO : HALO + count]
         kin = kinetic(whole, weights_ref[...])
         boosted_ref[s] = values
@@ -327,20 +343,17 @@
         base_ref[s, 1] = values[1] - time_step * kin[0]
         base_ref[s, 2] = values[2] - time_step * kin[3]
         base_ref[s, 3] = values[3] + time_step * kin[2]
-        return 0
-
-    lax.fori_loop(0, states, one_state, 0)
 
 
 def gather(where, shift, wave, weights, mine, pieces, count, planes, depth, *after):
     arrays, starts = zip(*pieces)
-    shape = jax.ShapeDtypeStruct((count, 4, planes + 2 * HALO, SUBS, LANES), jnp.float32)
+    shapes = [(count, 4, 4 * planes, SUBS, LANES)] + [(count, 4, planes, SUBS, LANES)] * 2
     return pl.pallas_call(
         functools.partial(gather_kernel, depth, planes, mine, starts),
-        out_shape=[shape] * 2,
+        out_shape=[jax.ShapeDtypeStruct(shape, jnp.float32) for shape in shapes],
         in_specs=[SMEM] * 3 + [VMEM] * 5 + [ANYWHERE] * len(after),
-        out_specs=[VMEM] * 2,
-        scratch_shapes=[pltpu.VMEM((2, 4 * planes, SUBS, LANES), jnp.float32), pltpu.VMEM((4, 4 * planes, SUBS, LANES), jnp.float32)],
+        out_specs=[VMEM] * 3,
+        scratch_shapes=[pltpu.VMEM((2, 4 * planes, SUBS, LANES), jnp.float32)],
         compiler_params=params(),
         name="gather",
     )(where, shift, wave, weights, *arrays, *after)
@@ -355,11 +368,11 @@
         total = [jnp.zeros((SUBS, LANES), jnp.float32)] * 3
         for boosted, base in zip(boosted_refs, base_refs):
             for s in range(boosted.shape[0]):
-                part = local_part(field, *[boosted[s, k, HALO + z] for k in range(4)])
-                pr = base[s, 0, HALO + z] + time_step * part[1]
-                pi = base[s, 1, HALO + z] - time_step * part[0]
-                hr = base[s, 2, HALO + z] + time_step * part[3]
-                hi = base[s, 3, HALO + z] - time_step * part[2]
+                part = local_part(field, *[boosted[s, k, z] for k in range(4)])
+                pr = base[s, 0, z] + time_step * part[1]
+                pi = base[s, 1, z] - time_step * part[0]
+                hr = base[s, 2, z] + time_step * part[3]
+                hi = base[s, 3, z] - time_step * part[2]
                 total = [a + b for a, b in zip(total, densities(pr, pi, hr, hi))]
         for f in range(3):
             sums[f, z] = total[f]
@@ -381,48 +394,69 @@
     )(fields, *boosted, *base)
 
 
-def free_kernel(places, where_ref, weights_ref, fields, *refs):
+def free_kernel(places, where_ref, shift_ref, weights_ref, fields, *refs):
     pieces = len(places)
-    boosted_refs, base_refs = refs[:pieces], refs[pieces : 2 * pieces]
-    free_ref, predicted_ref, window, turned = refs[2 * pieces :]
+    windows, boosted_refs, base_refs = refs[:pieces], refs[pieces : 2 * pieces], refs[2 * pieces : 3 * pieces]
+    free_ref, predicted_ref, window, combined = refs[3 * pieces :]
     planes = free_ref.shape[3]
     inner = pl.ds(HALO, planes)
-    odd = lax.rem(where_ref[0], 2)
-    for (mine, first, count), boosted, base in zip(places, boosted_refs, base_refs):
+    slab = where_ref[0]
+    odd = lax.rem(slab, 2)
+    edge = HALO + planes
+
+    def predict(layer, field, boosted, base):
+        part = local_part(field, *boosted)
+        window[0, layer] = base[0] + time_step * part[1]
+        window[1, layer] = base[1] - time_step * part[0]
+        window[2, layer] = base[2] + time_step * part[3]
+        window[3, layer] = base[3] - time_step * part[2]
+
+    for (mine, first, count), boosted_window, boosted, base in zip(places, windows, boosted_refs, base_refs):
         j = odd if mine else 1 - odd
+        start = window_start(j, planes, REACH, shift_ref)
 
         def one_state(s, _):
-            for z in range(planes + 2 * HALO):
-                field = [fields[f, z] for f in range(3)]
-                part = local_part(field, *[boosted[s, k, z] for k in range(4)])
-                window[0, z] = base[s, 0, z] + time_step * part[1]
-                window[1, z] = base[s, 1, z] - time_step * part[0]
-                window[2, z] = base[s, 2, z] + time_step * part[3]
-                window[3, z] = base[s, 3, z] - time_step * part[2]
+            sides = [boosted_window[s, :, pl.ds(start + first_side, 3 * HALO)] for first_side in (0, planes + HALO)]
+            sides = jnp.concatenate(sides, axis=0)
+            kin = kinetic(sides, weights_ref[...])
+            for side, offset in ((0, 0), (1, edge)):
+                for n in range(HALO):
+                    value = [sides[4 * side + k, HALO + n] for k in range(4)]
+                    turn = [kin[4 * side + k, n] for k in range(4)]
+                    moved_on = [
+                        value[0] + time_step * turn[1],
+                        value[1] - time_step * turn[0],
+                        value[2] - time_step * turn[3],
+                        value[3] + time_step * turn[2],
+                    ]
+                    predict(offset + n, [fields[f, offset + n] for f in range(3)], value, moved_on)
+            for z in range(planes):
+                field = [fields[f, HALO + z] for f in range(3)]
+                predict(HALO + z, field, [boosted[s, k, z] for k in range(4)], [base[s, k, z] for k in range(4)])
             kin = kinetic(window[...], weights_ref[...])
-            mean = [0.5 * (boosted[s, k, inner] + window[k, inner]) for k in range(4)]
+            mean = [0.5 * (boosted[s, k] + window[k, inner]) for k in range(4)]
             half = 0.5 * time_step
-            turned[0] = mean[0] + half * kin[1]
-            turned[1] = mean[1] - half * kin[0]
-            turned[2] = mean[2] - half * kin[3]
-            turned[3] = mean[3] + half * kin[2]
+            combined[0] = mean[0] + half * kin[1]
+            combined[1] = mean[1] - half * kin[0]
+            combined[2] = mean[2] - half * kin[3]
+            combined[3] = mean[3] + half * kin[2]
             for k in range(4):
                 for t in range(SUBS):
                     lanes = pl.ds(t * LANES, LANES)
-                    free_ref[j, first + s, k, :, lanes] = turned[k, :, t, :]
-                    predicted_ref[j, first + s, k, :, lanes] = window[k, inner, t, :]
+                    free_ref[0, first + s, k, :, lanes] = combined[k, :, t, :]
+                    predicted_ref[0, first + s, k, :, lanes] = window[k, inner, t, :]
             return 0
 
         lax.fori_loop(0, count, one_state, 0)
 
 
-def free_part(where, weights, fields, boosted, base, places, shape, planes):
+def free_part(where, shift, weights, fields, windows, boosted, base, places, shape, planes):
     pieces = len(places)
     out = jax.ShapeDtypeStruct(shape, jnp.float32)
     return pl.pallas_call(
-        functools.partial(free_kernel, places),
+        functools.partial(free_kernel, tuple(places)),
         out_shape=[out] * 2,
-        in_specs=[SMEM] + [VMEM] * (2 + 2 * pieces),
+        in_specs=[SMEM] * 2 + [VMEM] * (2 + 3 * pieces),
         out_specs=[VMEM] * 2,
         scratch_shapes=[
             pltpu.VMEM((4, planes + 2 * HALO, SUBS, LANES), jnp.float32),
@@ -430,12 +464,12 @@
         ],
         compiler_params=params(),
         name="free_part",
-    )(where, weights, fields, *boosted, *base)
-
-
-def last_kernel(scale, *refs):
-    partial_refs = refs[:-4]
-    free_ref, predicted_ref, out_ref, fields = refs[-4:]
+    )(where, shift, weights, fields, *windows, *boosted, *base)
+
+
+def last_kernel(scale, where_ref, *refs):
+    partial_refs, pieces = refs[:-6], refs[-6:-2]
+    out_ref, fields = refs[-2:]
 
     @pl.when(pl.program_id(0) == 0)
     def _():
@@ -449,31 +483,42 @@
             fields[f] = field
 
     half = 0.5 * time_step
-    for t in range(free_ref.shape[-1] // LANES):
-        lanes = pl.ds(t * LANES, LANES)
-        field = [fields[f, :, lanes] for f in range(3)]
-        for s in range(free_ref.shape[1]):
-            part = local_part(field, *[predicted_ref[0, s, k, :, lanes] for k in range(4)])
-            out_ref[0, s, 0, :, lanes] = free_ref[0, s, 0, :, lanes] + half * part[1]
-            out_ref[0, s, 1, :, lanes] = free_ref[0, s, 1, :, lanes] - half * part[0]
-            out_ref[0, s, 2, :, lanes] = free_ref[0, s, 2, :, lanes] + half * part[3]
-            out_ref[0, s, 3, :, lanes] = free_ref[0, s, 3, :, lanes] - half * part[2]
-
-
-def last_part(partials, free, predicted, scale):
-    shape = free.shape
-    whole = pl.BlockSpec(partials[0].shape, lambda i: (0, 0, 0))
-    block = pl.BlockSpec((1, *shape[1:]), lambda i: (i, 0, 0, 0, 0))
+
+    def write(free_ref, predicted_ref):
+        for t in range(out_ref.shape[-1] // LANES):
+            lanes = pl.ds(t * LANES, LANES)
+            field = [fields[f, :, lanes] for f in range(3)]
+            for s in range(out_ref.shape[1]):
+                part = local_part(field, *[predicted_ref[0, s, k, :, lanes] for k in range(4)])
+                out_ref[0, s, 0, :, lanes] = free_ref[0, s, 0, :, lanes] + half * part[1]
+                out_ref[0, s, 1, :, lanes] = free_ref[0, s, 1, :, lanes] - half * part[0]
+                out_ref[0, s, 2, :, lanes] = free_ref[0, s, 2, :, lanes] + half * part[3]
+                out_ref[0, s, 3, :, lanes] = free_ref[0, s, 3, :, lanes] - half * part[2]
+
+    mine = pl.program_id(0) == lax.rem(where_ref[0], 2)
+
+    @pl.when(jnp.logical_not(mine))
+    def _():
+        write(pieces[0], pieces[2])
+
+    @pl.when(mine)
+    def _():
+        write(pieces[1], pieces[3])
+
+
+def last_part(where, partials, free, predicted, scale):
+    shape = (2, *free[0].shape[1:])
+    whole = lambda a: pl.BlockSpec(a.shape, lambda i: (0,) * a.ndim)
     return pl.pallas_call(
         functools.partial(last_kernel, scale),
         out_shape=jax.ShapeDtypeStruct(shape, jnp.float32),
-        grid=(shape[0],),
-        in_specs=[whole] * len(partials) + [block] * 2,
-        out_specs=block,
+        grid=(2,),
+        in_specs=[SMEM] + [whole(a) for a in (*partials, *free, *predicted)],
+        out_specs=pl.BlockSpec((1, *shape[1:]), lambda i: (i, 0, 0, 0, 0)),
         scratch_shapes=[pltpu.VMEM(partials[0].shape, jnp.float32)],
         compiler_params=params(),
         name="last_part",
-    )(*partials, free, predicted)
+    )(where, *partials, *free, *predicted)
 
 
 def local(weights, cloud_states, cloud_shift, boost_wave):
@@ -487,6 +532,16 @@
     odd_on = lambda a: lax.ppermute(a, "slab", [(i, (i + 2 if i % 2 else i - 2) % slab_count) for i in range(slab_count)])
     across = lambda a: lax.ppermute(a, "slab", [(i, (i + 3 if i % 2 else i - 3) % slab_count) for i in range(slab_count)])
 
+    def paired(a, bit):
+        return lax.ppermute(a, "grp", [(i, i ^ bit) for i in range(group_count)])
+
+    def two_terms(a, *after):
+        if group_count != 4:
+            a = lax.psum(a, "grp")
+            return [a, jnp.zeros_like(a)]
+        a = add(a, paired(a, 1), *after)
+        return [a, paired(a, 2)]
+
     def group_terms(a):
         if group_count > 4:
             return [lax.psum(a, "grp")]
@@ -497,33 +552,40 @@
     mine_second = [even_on(piece) for piece in mine]
     other = [take(where, cloud_states, False, *chunk) for chunk in chunks]
     other_second = [odd_on(piece) for piece in other]
-    terms = group_terms(raw_density(cloud_states, *mine, *other))
-    mine_sums, other_sums = total_of(where, terms, *mine_second)
+    terms = two_terms(raw_density(cloud_states, *mine, *other))
     extra = across(take_extra(where, cloud_states, mine[0]))
+    mine_sums, other_sums = total_of(where, terms, *mine_second, extra)
 
     mine_sums_second, other_sums_second, far_sums = even_on(mine_sums), odd_on(other_sums), across(other_sums)
     other_next = swapped(mine[0])
-    other_far = swapped(mine_second[0])
-    joined = join([mine_sums_second, other_sums_second, mine_sums], extra, far_sums)
-    swapped_sums = swapped(joined)
-    swapped_sums = [swapped_sums[3 * n : 3 * n + 3] for n in range(3)]
-    mine_next = [swapped(piece) for piece in other_second]
+    other_far = swapped(join(mine_second, mine_sums))
     work = lambda *a: gather(where, cloud_shift, boost_wave, weights, *a, planes, depth)
     places, worked = [], []
     for n, (first, count) in enumerate(chunks):
         worked.append(work(False, [(other_far, first), (other_second[n], 0), (other_next, first), (other[n], 0)], count))
         places.append((False, first, count))
+    joined = join([mine_sums_second, other_sums_second, mine_sums], far_sums, *[piece[1] for piece in worked])
+    swapped_sums = swapped(joined)
+    swapped_sums = [swapped_sums[3 * n : 3 * n + 3] for n in range(3)]
+    mine_next = [swapped(join([piece], joined)) for piece in other_second]
     fields = placed_fields(
         where, cloud_shift, boost_wave, [far_sums, mine_sums_second, swapped_sums[1], mine_sums],
-        [swapped_sums[0], other_sums_second, swapped_sums[2], other_sums], depth, scale, *[piece[0] for piece in worked],
+        [swapped_sums[0], other_sums_second, swapped_sums[2], other_sums], depth, scale,
     )
     for n, (first, count) in enumerate(chunks):
         worked.append(work(True, [(extra, first), (mine_second[n], 0), (mine_next[n], 0), (mine[n], 0)], count))
         places.append((True, first, count))
-    boosted, base = [list(part) for part in zip(*worked)]
-    partials = group_terms(density(fields, boosted, base, planes))
-    free, predicted = free_part(where, weights, fields, boosted, base, tuple(places), cloud_states.shape, planes)
-    return last_part(partials, free, predicted, scale)
+    windows, boosted, base = [list(part) for part in zip(*worked)]
+    def free_of(n):
+        return free_part(
+            where, cloud_shift, weights, fields, windows[n : n + 1], boosted[n : n + 1], base[n : n + 1], places[n : n + 1],
+            (1, *cloud_states.shape[1:]), planes,
+        )
+
+    first_parts = free_of(0)
+    partials = two_terms(density(fields, boosted, base, planes), first_parts[0])
+    free, predicted = zip(first_parts, free_of(1))
+    return last_part(where, partials, free, predicted, scale)
 
 
 def solution(mesh):

time: 55 us -> 52.3 us (0.951)
  starting transfers between devices: 23.7 us -> 18.2 us
  waiting for transfers between devices: 18.4 us -> 20.5 us
  Pallas kernels: 11.2 us -> 11.9 us
    ppermute x2, waiting for transfers between devices: 0.25 us -> 10.5 us  [local(): lax.ppermute(a, 'slab', [(i, (i + 3 if i % 2 else i - 3) % slab_count) fo...]
    ppermute x6 -> x4, starting transfers between devices: 14.1 us -> 8.6 us  [paired(): return lax.ppermute(a, 'grp', [(i, i ^ bit) for i in range(group_count)])]
    ppermute x6 -> x4, waiting for transfers between devices: 11.6 us -> 7.51 us  [paired(): return lax.ppermute(a, 'grp', [(i, i ^ bit) for i in range(group_count)])]
    ppermute x2, starting transfers between devices: 0.14 us -> 2.89 us  [local(): lax.ppermute(a, 'slab', [(i, (i + 3 if i % 2 else i - 3) % slab_count) fo...]
    ppermute x2, waiting for transfers between devices: 2.01 us -> 0.01 us  [local(): lax.ppermute(a, 'slab', [(i, (i + 2 if i % 2 else i - 2) % slab_count) fo...]
    pallas_call x1 -> x4, Pallas kernels: 3.33 us -> 5.19 us  [the longest x2 5.16 us: free_part(): pl.pallas_call(functools.partial(free_kernel, tuple(places)), out_shape=[...]
    ppermute x2, waiting for transfers between devices: 3.2 us -> 1.49 us  [local(): lax.ppermute(a, 'slab', [(i, (i - 2 if i % 2 else i + 2) % slab_count) fo...]
    ppermute x2, starting transfers between devices: 6.33 us -> 4.79 us  [local(): lax.ppermute(a, 'slab', [(i, (i - 2 if i % 2 else i + 2) % slab_count) fo...]
  transfers between devices with their start and end apart: 16 -> 14, of which waited for: 9 -> 7; matrix products, arithmetic and copies ran while one was open for 0% -> 0% of each run, Pallas kernels for 11% -> 17%
where the time goes in v3:
time: 52.3 us; the launch traced here: 52.1 us
  waiting for transfers between devices  20.5 us (39%)
  starting transfers between devices  18.2 us (35%)
  Pallas kernels  11.9 us (23%)
  local copies, waits for them, and re-layouts  1.27 us (2%)
    ppermute x2, waiting for transfers between devices, local(): lax.ppermute(a, 'slab', [(i, (i + 3 if i % 2 else i - 3) % slab_count) fo...  10.5 us
    ppermute x4, starting transfers between devices, paired(): return lax.ppermute(a, 'grp', [(i, i ^ bit) for i in range(group_count)])  8.6 us
    ppermute x4, waiting for transfers between devices, paired(): return lax.ppermute(a, 'grp', [(i, i ^ bit) for i in range(group_count)])  7.51 us
    pallas_call x2, Pallas kernels, free_part(): pl.pallas_call(functools.partial(free_kernel, tuple(places)), out_shape=[...  5.16 us
    ppermute x2, starting transfers between devices, local(): lax.ppermute(a, 'slab', [(i, (i - 2 if i % 2 else i + 2) % slab_count) fo...  4.79 us
    ppermute x2, starting transfers between devices, local(): lax.ppermute(a, 'slab', [(i, (i + 3 if i % 2 else i - 3) % slab_count) fo...  2.89 us
    pallas_call x2, Pallas kernels, gather(): pl.pallas_call(functools.partial(gather_kernel, depth, planes, mine, star...  2.86 us
    ppermute x2, waiting for transfers between devices, local(): lax.ppermute(a, 'slab', [(i, (i - 2 if i % 2 else i + 2) % slab_count) fo...  1.49 us
  transfers between devices with their start and end apart: 14, of which 7 were waited for; matrix products, arithmetic and copies ran while one was open for 0% of the time, Pallas kernels for 17%

profile of v3, /device:TPU:0, one launch (start us, length us, event | category | flops | bytes accessed | tf_op | source)
XLA Modules:
  0.0 52.1 jit_solution(524588740199852983)
XLA Ops:
  0.0 1.2 %copy-done = f32[2,4,4,8,1024]{4,3,2,1,0:T(8,128)S(1)} copy-done((f32[2,4,4,8,1024]{4,3,2,1,0:T(8,128)S(1)}, f32[2,4,4,8,1024]{4,3,2,1,0:T(8,128)}, u32[]{:S(2)}) %copy-start) | copy-done | bytes 1048600
  1.5 3.0 %collective-permute-start.2 = (f32[128,8,128]{2,1,0:T(8,128)S(1)}, f32[128,8,128]{2,1,0:T(8,128)S(1)}, u32[]{:S(2)}, u32[]{:S(2)}) collective-permute-start(f32[128,8,128]{2,1,0:T(8,128)S(1)} %take.2.refs_0_.own_ref), channel_id=1, source_target_pairs={{0,8},{4,28},{8,16},{12,4},{16,24},{20,12},{24,0},{28,20},{1,9},{5... | collective-permute-start | bytes 1572872 | tf_op jit(solution)/shard_map/ppermute | solution.py:531
  5.0 1.6 %collective-permute-start = (f32[2,3,8,1024]{3,2,1,0:T(8,128)S(1)}, f32[2,3,8,1024]{3,2,1,0:T(8,128)S(1)}, u32[]{:S(2)}, u32[]{:S(2)}) collective-permute-start(f32[2,3,8,1024]{3,2,1,0:T(8,128)S(1)} %raw_density.1.a_ref), channel_id=1, source_target_pairs={{0,1},{1,0},{2,3},{3,2},{4,5},{5,4},{6,7},{7,6},{8,9},{9,8},{10,11... | collective-permute-start | bytes 589832 | tf_op jit(solution)/shard_map/ppermute | solution.py:536
  7.3 5.0 %collective-permute-done.b_ref = f32[2,3,8,1024]{3,2,1,0:T(8,128)S(1)} collective-permute-done((f32[2,3,8,1024]{3,2,1,0:T(8,128)S(1)}, f32[2,3,8,1024]{3,2,1,0:T(8,128)S(1)}, u32[]{:S(2)}, u32[]{:S(2)}) %collective-permute-start) | collective-permute-done | bytes 196640 | tf_op jit(solution)/shard_map/ppermute | solution.py:536
  12.4 2.7 %collective-permute-start.1 = (f32[2,3,8,1024]{3,2,1,0:T(8,128)S(1)}, f32[2,3,8,1024]{3,2,1,0:T(8,128)S(1)}, u32[]{:S(2)}, u32[]{:S(2)}) collective-permute-start(f32[2,3,8,1024]{3,2,1,0:T(8,128)S(1)} %add.2.refs_0_), channel_id=1, source_target_pairs={{0,2},{1,3},{2,0},{3,1},{4,6},{5,7},{6,4},{7,5},{8,10},{9,11},{10,... | collective-permute-start | bytes 589832 | tf_op jit(solution)/shard_map/ppermute | solution.py:536
  15.0 0.8 %collective-permute-start.8 = (f32[128,8,128]{2,1,0:T(8,128)S(1)}, f32[128,8,128]{2,1,0:T(8,128)S(1)}, u32[]{:S(2)}, u32[]{:S(2)}) collective-permute-start(f32[128,8,128]{2,1,0:T(8,128)S(1)} %take.3.refs_1_.own_ref), channel_id=1, source_target_pairs={{0,24},{4,12},{8,0},{12,20},{16,8},{20,28},{24,16},{28,4},{1,25},{... | collective-permute-start | bytes 1572872 | tf_op jit(solution)/shard_map/ppermute | solution.py:532
  15.9 9.6 %collective-permute-done.3.refs_3_.far_ref = f32[80,8,128]{2,1,0:T(8,128)S(1)} collective-permute-done((f32[80,8,128]{2,1,0:T(8,128)S(1)}, f32[80,8,128]{2,1,0:T(8,128)S(1)}, u32[]{:S(2)}, u32[]{:S(2)}) %collective-permute-start.3) | collective-permute-done | bytes 327712 | tf_op jit(solution)/shard_map/ppermute | solution.py:533
  25.5 0.5 collective-permute-start.7
  26.0 2.5 %collective-permute-start.4 = (f32[3,8,1024]{2,1,0:T(8,128)S(1)}, f32[3,8,1024]{2,1,0:T(8,128)S(1)}, u32[]{:S(2)}, u32[]{:S(2)}) collective-permute-start(f32[3,8,1024]{2,1,0:T(8,128)S(1)} %get-tuple-element.17.refs_7_), channel_id=1, source_target_pairs={{0,20},{4,16},{8,28},{12,24},{16,4},{20,0},{24,12},{28,8},{1,21},{... | collective-permute-start | bytes 294920 | tf_op jit(solution)/shard_map/ppermute | solution.py:533
  28.5 1.8 %collective-permute-start.5 = (f32[3,8,1024]{2,1,0:T(8,128)S(1)}, f32[3,8,1024]{2,1,0:T(8,128)S(1)}, u32[]{:S(2)}, u32[]{:S(2)}) collective-permute-start(f32[3,8,1024]{2,1,0:T(8,128)S(1)} %get-tuple-element.18.refs_1_.refs_2_.refs_3_), channel_id=1, source_target_pairs={{0,8},{4,28},{8,16},{12,4},{16,24},{20,12},{24,0},{28,20},{1,9},{5... | collective-permute-start | bytes 294920 | tf_op jit(solution)/shard_map/ppermute | solution.py:531
  30.3 1.4 %gather.2 = (f32[4,4,32,8,128]{4,3,2,1,0:T(8,128)S(1)}, f32[4,4,8,8,128]{4,3,2,1,0:T(8,128)S(1)}, f32[4,4,8,8,128]{4,3,2,1,0:T(8,128)S(1)}) custom-call(s32[1]{0:T(128)} %bitcast.where_ref, s32[2]{0:T(128)S(1)} %copy-done.3, s32[2]{0:T(128)S(1)} %copy-done.4, bf16[256,384]{1,0:T(8,128)(2,1)S(1)} %copy-done.2, ...), custom_call_target="tpu_custom_call" | custom-call | tf_op jit(solution)/shard_map/gather/pallas_call | solution.py:351
  31.8 1.0 %collective-permute-done.4.refs_3_.refs_0_ = f32[3,8,1024]{2,1,0:T(8,128)S(1)} collective-permute-done((f32[3,8,1024]{2,1,0:T(8,128)S(1)}, f32[3,8,1024]{2,1,0:T(8,128)S(1)}, u32[]{:S(2)}, u32[]{:S(2)}) %collective-permute-start.4) | collective-permute-done | bytes 98336 | tf_op jit(solution)/shard_map/ppermute | solution.py:533
  32.7 1.5 %collective-permute-done.5.refs_0_.refs_1_ = f32[3,8,1024]{2,1,0:T(8,128)S(1)} collective-permute-done((f32[3,8,1024]{2,1,0:T(8,128)S(1)}, f32[3,8,1024]{2,1,0:T(8,128)S(1)}, u32[]{:S(2)}, u32[]{:S(2)}) %collective-permute-start.5) | collective-permute-done | bytes 98336 | tf_op jit(solution)/shard_map/ppermute | solution.py:531
  34.4 0.6 %collective-permute-start.11 = (f32[128,8,128]{2,1,0:T(8,128)S(1)}, f32[128,8,128]{2,1,0:T(8,128)S(1)}, u32[]{:S(2)}, u32[]{:S(2)}) collective-permute-start(f32[128,8,128]{2,1,0:T(8,128)S(1)} %join.5), channel_id=1, source_target_pairs={{0,4},{4,0},{8,12},{12,8},{16,20},{20,16},{24,28},{28,24},{1,5},{5... | collective-permute-start | bytes 1572872 | tf_op jit(solution)/shard_map/ppermute | solution.py:41
  34.9 1.0 %collective-permute-done.10 = f32[9,8,1024]{2,1,0:T(8,128)S(1)} collective-permute-done((f32[9,8,1024]{2,1,0:T(8,128)S(1)}, f32[9,8,1024]{2,1,0:T(8,128)S(1)}, u32[]{:S(2)}, u32[]{:S(2)}) %collective-permute-start.10) | collective-permute-done | bytes 294944 | tf_op jit(solution)/shard_map/ppermute | solution.py:41
  35.9 1.2 %placed_fields.1.fields = f32[3,14,8,128]{3,2,1,0:T(8,128)S(1)} custom-call(s32[1]{0:T(128)} %bitcast.where_ref, s32[2]{0:T(128)S(1)} %copy-done.3, s32[2]{0:T(128)S(1)} %copy-done.4, f32[3,8,1024]{2,1,0:T(8,128)S(1)} %collective-permute-done.4.refs_3_.refs_0_, f32[3,8,1024]{2,1,0:T(8,128)S(1)} %collective-permute-done.5.refs_0_.refs_1_, ...), custom_call_target="tpu_custom_call" | custom-call | tf_op jit(solution)/shard_map/placed_fields/pallas_call | solution.py:268
  37.1 1.4 %gather.3 = (f32[4,4,32,8,128]{4,3,2,1,0:T(8,128)S(1)}, f32[4,4,8,8,128]{4,3,2,1,0:T(8,128)S(1)}, f32[4,4,8,8,128]{4,3,2,1,0:T(8,128)S(1)}) custom-call(s32[1]{0:T(128)} %bitcast.where_ref, s32[2]{0:T(128)S(1)} %copy-done.3, s32[2]{0:T(128)S(1)} %copy-done.4, bf16[256,384]{1,0:T(8,128)(2,1)S(1)} %copy-done.2, ...), custom_call_target="tpu_custom_call" | custom-call | tf_op jit(solution)/shard_map/gather/pallas_call | solution.py:351
  39.0 1.6 %collective-permute-start.12 = (f32[3,8,1024]{2,1,0:T(8,128)S(1)}, f32[3,8,1024]{2,1,0:T(8,128)S(1)}, u32[]{:S(2)}, u32[]{:S(2)}) collective-permute-start(f32[3,8,1024]{2,1,0:T(8,128)S(1)} %density.1.a_ref), channel_id=1, source_target_pairs={{0,1},{1,0},{2,3},{3,2},{4,5},{5,4},{6,7},{7,6},{8,9},{9,8},{10,11... | collective-permute-start | bytes 294920 | tf_op jit(solution)/shard_map/ppermute | solution.py:536
  40.6 2.6 %free_part.2 = (f32[1,4,4,8,1024]{4,3,2,1,0:T(8,128)S(1)}, f32[1,4,4,8,1024]{4,3,2,1,0:T(8,128)S(1)}) custom-call(s32[1]{0:T(128)} %bitcast.where_ref, s32[2]{0:T(128)S(1)} %copy-done.3, bf16[256,384]{1,0:T(8,128)(2,1)S(1)} %copy-done.2, f32[3,14,8,128]{3,2,1,0:T(8,128)S(1)} %placed_fields.1.fields, f32[4,4,32,8,128]{4,3,2,1,0:T(8,128)S(1)} %get-tuple-element.23.refs_0_, ...), custom_call_target="tpu_custom_call" | custom-call | tf_op jit(solution)/shard_map/free_part/pallas_call | solution.py:456
  43.2 0.7 %collective-permute-done.12.b_ref = f32[3,8,1024]{2,1,0:T(8,128)S(1)} collective-permute-done((f32[3,8,1024]{2,1,0:T(8,128)S(1)}, f32[3,8,1024]{2,1,0:T(8,128)S(1)}, u32[]{:S(2)}, u32[]{:S(2)}) %collective-permute-start.12) | collective-permute-done | bytes 98336 | tf_op jit(solution)/shard_map/ppermute | solution.py:536
  43.9 2.7 %collective-permute-start.13 = (f32[3,8,1024]{2,1,0:T(8,128)S(1)}, f32[3,8,1024]{2,1,0:T(8,128)S(1)}, u32[]{:S(2)}, u32[]{:S(2)}) collective-permute-start(f32[3,8,1024]{2,1,0:T(8,128)S(1)} %add.3.refs_0_), channel_id=1, source_target_pairs={{0,2},{1,3},{2,0},{3,1},{4,6},{5,7},{6,4},{7,5},{8,10},{9,11},{10,... | collective-permute-start | bytes 294920 | tf_op jit(solution)/shard_map/ppermute | solution.py:536
  46.6 2.6 %free_part.3 = (f32[1,4,4,8,1024]{4,3,2,1,0:T(8,128)S(1)}, f32[1,4,4,8,1024]{4,3,2,1,0:T(8,128)S(1)}) custom-call(s32[1]{0:T(128)} %bitcast.where_ref, s32[2]{0:T(128)S(1)} %copy-done.3, bf16[256,384]{1,0:T(8,128)(2,1)S(1)} %copy-done.2, f32[3,14,8,128]{3,2,1,0:T(8,128)S(1)} %placed_fields.1.fields, f32[4,4,32,8,128]{4,3,2,1,0:T(8,128)S(1)} %get-tuple-element.25.refs_0_, ...), custom_call_target="tpu_custom_call" | custom-call | tf_op jit(solution)/shard_map/free_part/pallas_call | solution.py:456
  49.1 1.8 %collective-permute-done.13.refs_1_ = f32[3,8,1024]{2,1,0:T(8,128)S(1)} collective-permute-done((f32[3,8,1024]{2,1,0:T(8,128)S(1)}, f32[3,8,1024]{2,1,0:T(8,128)S(1)}, u32[]{:S(2)}, u32[]{:S(2)}) %collective-permute-start.13) | collective-permute-done | bytes 98336 | tf_op jit(solution)/shard_map/ppermute | solution.py:536
  51.0 1.1 %last_part.1 = f32[2,4,4,8,1024]{4,3,2,1,0:T(8,128)} custom-call(s32[1]{0:T(128)} %bitcast.where_ref, f32[3,8,1024]{2,1,0:T(8,128)S(1)} %add.3.refs_0_, f32[3,8,1024]{2,1,0:T(8,128)S(1)} %collective-permute-done.13.refs_1_, f32[1,4,4,8,1024]{4,3,2,1,0:T(8,128)S(1)} %get-tuple-element.24.refs_0_.refs_2_, f32[1,4,4,8,1024]{4,3,2,1,0:T(8,128)S(1)} %get-tuple-element.26.refs_3_, ...), custom_call_target="tpu_custom_call" | custom-call | tf_op jit(solution)/shard_map/last_part/pallas_call | solution.py:512
  (32 shorter events, 2.1 us)
Async XLA Ops:
  0.0 1.2 %copy-start = (f32[2,4,4,8,1024]{4,3,2,1,0:T(8,128)S(1)}, f32[2,4,4,8,1024]{4,3,2,1,0:T(8,128)}, u32[]{:S(2)}) copy-start(f32[2,4,4,8,1024]{4,3,2,1,0:T(8,128)} %x_ref.7) | copy-start | bytes 3145732
  1.2 3.6 %copy-start.1 = (f32[2,4,4,8,1024]{4,3,2,1,0:T(8,128)S(1)}, f32[2,4,4,8,1024]{4,3,2,1,0:T(8,128)}, u32[]{:S(2)}) copy-start(f32[2,4,4,8,1024]{4,3,2,1,0:T(8,128)} %x_ref.7) | copy-start | bytes 3145732
  1.5 23.9 %collective-permute-start.2 = (f32[128,8,128]{2,1,0:T(8,128)S(1)}, f32[128,8,128]{2,1,0:T(8,128)S(1)}, u32[]{:S(2)}, u32[]{:S(2)}) collective-permute-start(f32[128,8,128]{2,1,0:T(8,128)S(1)} %take.2.refs_0_.own_ref), channel_id=1, source_target_pairs={{0,8},{4,28},{8,16},{12,4},{16,24},{20,12},{24,0},{28,20},{1,9},{5... | collective-permute-start | bytes 1572872 | tf_op jit(solution)/shard_map/ppermute | solution.py:531
  4.9 25.4 %copy-start.2 = (bf16[256,384]{1,0:T(8,128)(2,1)S(1)}, bf16[256,384]{1,0:T(8,128)(2,1)}, u32[]{:S(2)}) copy-start(bf16[256,384]{1,0:T(8,128)(2,1)} %constant.8.clone.weights_ref) | copy-start | bytes 589828
  4.9 25.4 %copy-start.3 = (s32[2]{0:T(128)S(1)}, s32[2]{0:T(128)}, u32[]{:S(2)}) copy-start(s32[2]{0:T(128)} %shift_ref.9) | copy-start | bytes 28
  4.9 25.4 %copy-start.4 = (s32[2]{0:T(128)S(1)}, s32[2]{0:T(128)}, u32[]{:S(2)}) copy-start(s32[2]{0:T(128)} %wave_ref.5) | copy-start | bytes 28
  5.0 7.4 %collective-permute-start = (f32[2,3,8,1024]{3,2,1,0:T(8,128)S(1)}, f32[2,3,8,1024]{3,2,1,0:T(8,128)S(1)}, u32[]{:S(2)}, u32[]{:S(2)}) collective-permute-start(f32[2,3,8,1024]{3,2,1,0:T(8,128)S(1)} %raw_density.1.a_ref), channel_id=1, source_target_pairs={{0,1},{1,0},{2,3},{3,2},{4,5},{5,4},{6,7},{7,6},{8,9},{9,8},{10,11... | collective-permute-start | bytes 589832 | tf_op jit(solution)/shard_map/ppermute | solution.py:536
  6.9 18.5 %collective-permute-start.3 = (f32[80,8,128]{2,1,0:T(8,128)S(1)}, f32[80,8,128]{2,1,0:T(8,128)S(1)}, u32[]{:S(2)}, u32[]{:S(2)}) collective-permute-start(f32[80,8,128]{2,1,0:T(8,128)S(1)} %take_extra.1), channel_id=1, source_target_pairs={{0,20},{4,16},{8,28},{12,24},{16,4},{20,0},{24,12},{28,8},{1,21},{... | collective-permute-start | bytes 983048 | tf_op jit(solution)/shard_map/ppermute | solution.py:533
  12.4 13.1 %collective-permute-start.1 = (f32[2,3,8,1024]{3,2,1,0:T(8,128)S(1)}, f32[2,3,8,1024]{3,2,1,0:T(8,128)S(1)}, u32[]{:S(2)}, u32[]{:S(2)}) collective-permute-start(f32[2,3,8,1024]{3,2,1,0:T(8,128)S(1)} %add.2.refs_0_), channel_id=1, source_target_pairs={{0,2},{1,3},{2,0},{3,1},{4,6},{5,7},{6,4},{7,5},{8,10},{9,11},{10,... | collective-permute-start | bytes 589832 | tf_op jit(solution)/shard_map/ppermute | solution.py:536
  15.0 13.5 %collective-permute-start.8 = (f32[128,8,128]{2,1,0:T(8,128)S(1)}, f32[128,8,128]{2,1,0:T(8,128)S(1)}, u32[]{:S(2)}, u32[]{:S(2)}) collective-permute-start(f32[128,8,128]{2,1,0:T(8,128)S(1)} %take.3.refs_1_.own_ref), channel_id=1, source_target_pairs={{0,24},{4,12},{8,0},{12,20},{16,8},{20,28},{24,16},{28,4},{1,25},{... | collective-permute-start | bytes 1572872 | tf_op jit(solution)/shard_map/ppermute | solution.py:532
  15.9 14.4 %collective-permute-start.9 = (f32[128,8,128]{2,1,0:T(8,128)S(1)}, f32[128,8,128]{2,1,0:T(8,128)S(1)}, u32[]{:S(2)}, u32[]{:S(2)}) collective-permute-start(f32[128,8,128]{2,1,0:T(8,128)S(1)} %take.2.refs_0_.own_ref), channel_id=1, source_target_pairs={{0,4},{4,0},{8,12},{12,8},{16,20},{20,16},{24,28},{28,24},{1,5},{5... | collective-permute-start | bytes 1572872 | tf_op jit(solution)/shard_map/ppermute | solution.py:41
  25.5 4.8 %collective-permute-start.7 = (f32[128,8,128]{2,1,0:T(8,128)S(1)}, f32[128,8,128]{2,1,0:T(8,128)S(1)}, u32[]{:S(2)}, u32[]{:S(2)}) collective-permute-start(f32[128,8,128]{2,1,0:T(8,128)S(1)} %join.3), channel_id=1, source_target_pairs={{0,4},{4,0},{8,12},{12,8},{16,20},{20,16},{24,28},{28,24},{1,5},{5... | collective-permute-start | bytes 1572872 | tf_op jit(solution)/shard_map/ppermute | solution.py:41
  26.0 5.7 %collective-permute-start.6 = (f32[3,8,1024]{2,1,0:T(8,128)S(1)}, f32[3,8,1024]{2,1,0:T(8,128)S(1)}, u32[]{:S(2)}, u32[]{:S(2)}) collective-permute-start(f32[3,8,1024]{2,1,0:T(8,128)S(1)} %get-tuple-element.17.refs_7_), channel_id=1, source_target_pairs={{0,24},{4,12},{8,0},{12,20},{16,8},{20,28},{24,16},{28,4},{1,25},{... | collective-permute-start | bytes 294920 | tf_op jit(solution)/shard_map/ppermute | solution.py:532
  26.0 6.7 %collective-permute-start.4 = (f32[3,8,1024]{2,1,0:T(8,128)S(1)}, f32[3,8,1024]{2,1,0:T(8,128)S(1)}, u32[]{:S(2)}, u32[]{:S(2)}) collective-permute-start(f32[3,8,1024]{2,1,0:T(8,128)S(1)} %get-tuple-element.17.refs_7_), channel_id=1, source_target_pairs={{0,20},{4,16},{8,28},{12,24},{16,4},{20,0},{24,12},{28,8},{1,21},{... | collective-permute-start | bytes 294920 | tf_op jit(solution)/shard_map/ppermute | solution.py:533
  28.5 5.7 %collective-permute-start.5 = (f32[3,8,1024]{2,1,0:T(8,128)S(1)}, f32[3,8,1024]{2,1,0:T(8,128)S(1)}, u32[]{:S(2)}, u32[]{:S(2)}) collective-permute-start(f32[3,8,1024]{2,1,0:T(8,128)S(1)} %get-tuple-element.18.refs_1_.refs_2_.refs_3_), channel_id=1, source_target_pairs={{0,8},{4,28},{8,16},{12,4},{16,24},{20,12},{24,0},{28,20},{1,9},{5... | collective-permute-start | bytes 294920 | tf_op jit(solution)/shard_map/ppermute | solution.py:531
  34.3 1.6 %collective-permute-start.10 = (f32[9,8,1024]{2,1,0:T(8,128)S(1)}, f32[9,8,1024]{2,1,0:T(8,128)S(1)}, u32[]{:S(2)}, u32[]{:S(2)}) collective-permute-start(f32[9,8,1024]{2,1,0:T(8,128)S(1)} %join.4.refs_1_), channel_id=1, source_target_pairs={{0,4},{4,0},{8,12},{12,8},{16,20},{20,16},{24,28},{28,24},{1,5},{5... | collective-permute-start | bytes 884744 | tf_op jit(solution)/shard_map/ppermute | solution.py:41
  34.4 2.8 %collective-permute-start.11 = (f32[128,8,128]{2,1,0:T(8,128)S(1)}, f32[128,8,128]{2,1,0:T(8,128)S(1)}, u32[]{:S(2)}, u32[]{:S(2)}) collective-permute-start(f32[128,8,128]{2,1,0:T(8,128)S(1)} %join.5), channel_id=1, source_target_pairs={{0,4},{4,0},{8,12},{12,8},{16,20},{20,16},{24,28},{28,24},{1,5},{5... | collective-permute-start | bytes 1572872 | tf_op jit(solution)/shard_map/ppermute | solution.py:41
  39.0 4.9 %collective-permute-start.12 = (f32[3,8,1024]{2,1,0:T(8,128)S(1)}, f32[3,8,1024]{2,1,0:T(8,128)S(1)}, u32[]{:S(2)}, u32[]{:S(2)}) collective-permute-start(f32[3,8,1024]{2,1,0:T(8,128)S(1)} %density.1.a_ref), channel_id=1, source_target_pairs={{0,1},{1,0},{2,3},{3,2},{4,5},{5,4},{6,7},{7,6},{8,9},{9,8},{10,11... | collective-permute-start | bytes 294920 | tf_op jit(solution)/shard_map/ppermute | solution.py:536
  43.9 7.1 %collective-permute-start.13 = (f32[3,8,1024]{2,1,0:T(8,128)S(1)}, f32[3,8,1024]{2,1,0:T(8,128)S(1)}, u32[]{:S(2)}, u32[]{:S(2)}) collective-permute-start(f32[3,8,1024]{2,1,0:T(8,128)S(1)} %add.3.refs_0_), channel_id=1, source_target_pairs={{0,2},{1,3},{2,0},{3,1},{4,6},{5,7},{6,4},{7,5},{8,10},{9,11},{10,... | collective-permute-start | bytes 294920 | tf_op jit(solution)/shard_map/ppermute | solution.py:536

commit v4 on v3

--- a/solution.py
+++ b/solution.py
@@ -552,8 +552,9 @@
     mine_second = [even_on(piece) for piece in mine]
     other = [take(where, cloud_states, False, *chunk) for chunk in chunks]
     other_second = [odd_on(piece) for piece in other]
-    terms = two_terms(raw_density(cloud_states, *mine, *other))
-    extra = across(take_extra(where, cloud_states, mine[0]))
+    leaving = take_extra(where, cloud_states, mine[0])
+    extra = across(leaving)
+    terms = two_terms(raw_density(cloud_states, leaving))
     mine_sums, other_sums = total_of(where, terms, *mine_second, extra)
 
     mine_sums_second, other_sums_second, far_sums = even_on(mine_sums), odd_on(other_sums), across(other_sums)

time: 52.3 us -> 52.6 us (level)
  waiting for transfers between devices: 20.5 us -> 21.5 us
  starting transfers between devices: 18.2 us -> 17.6 us
    ppermute x4, waiting for transfers between devices: 7.51 us -> 8.44 us  [paired(): return lax.ppermute(a, 'grp', [(i, i ^ bit) for i in range(group_count)])]
    ppermute x2, waiting for transfers between devices: 10.5 us -> 9.84 us  [local(): lax.ppermute(a, 'slab', [(i, (i + 3 if i % 2 else i - 3) % slab_count) fo...]
    ppermute x4, starting transfers between devices: 8.6 us -> 8.06 us  [paired(): return lax.ppermute(a, 'grp', [(i, i ^ bit) for i in range(group_count)])]
  transfers between devices with their start and end apart: 14 -> 14, of which waited for: 7 -> 8; matrix products, arithmetic and copies ran while one was open for 0% -> 0% of each run, Pallas kernels for 17% -> 16%
where the time goes in v4:
time: 52.6 us; the launch traced here: 52.5 us
  waiting for transfers between devices  21.5 us (41%)
  starting transfers between devices  17.6 us (33%)
  Pallas kernels  11.9 us (23%)
  local copies, waits for them, and re-layouts  1.27 us (2%)
    ppermute x2, waiting for transfers between devices, local(): lax.ppermute(a, 'slab', [(i, (i + 3 if i % 2 else i - 3) % slab_count) fo...  9.84 us
    ppermute x4, waiting for transfers between devices, paired(): return lax.ppermute(a, 'grp', [(i, i ^ bit) for i in range(group_count)])  8.44 us
    ppermute x4, starting transfers between devices, paired(): return lax.ppermute(a, 'grp', [(i, i ^ bit) for i in range(group_count)])  8.06 us
    pallas_call x2, Pallas kernels, free_part(): pl.pallas_call(functools.partial(free_kernel, tuple(places)), out_shape=[...  5.17 us
    ppermute x2, starting transfers between devices, local(): lax.ppermute(a, 'slab', [(i, (i - 2 if i % 2 else i + 2) % slab_count) fo...  4.7 us
    pallas_call x2, Pallas kernels, gather(): pl.pallas_call(functools.partial(gather_kernel, depth, planes, mine, star...  2.88 us
    ppermute x2, starting transfers between devices, local(): lax.ppermute(a, 'slab', [(i, (i + 3 if i % 2 else i - 3) % slab_count) fo...  2.82 us
    ppermute x2, waiting for transfers between devices, local(): lax.ppermute(a, 'slab', [(i, (i - 2 if i % 2 else i + 2) % slab_count) fo...  1.99 us
  transfers between devices with their start and end apart: 14, of which 8 were waited for; matrix products, arithmetic and copies ran while one was open for 0% of the time, Pallas kernels for 16%

profile of v4, /device:TPU:0, one launch (start us, length us, event | category | flops | bytes accessed | tf_op | source)
XLA Modules:
  0.0 52.5 jit_solution(5845012482800739965)
XLA Ops:
  0.0 1.2 %copy-done = f32[2,4,4,8,1024]{4,3,2,1,0:T(8,128)S(1)} copy-done((f32[2,4,4,8,1024]{4,3,2,1,0:T(8,128)S(1)}, f32[2,4,4,8,1024]{4,3,2,1,0:T(8,128)}, u32[]{:S(2)}) %copy-start) | copy-done | bytes 1048600
  1.5 3.0 %collective-permute-start.2 = (f32[128,8,128]{2,1,0:T(8,128)S(1)}, f32[128,8,128]{2,1,0:T(8,128)S(1)}, u32[]{:S(2)}, u32[]{:S(2)}) collective-permute-start(f32[128,8,128]{2,1,0:T(8,128)S(1)} %take.2.refs_0_.own_ref), channel_id=1, source_target_pairs={{0,8},{4,28},{8,16},{12,4},{16,24},{20,12},{24,0},{28,20},{1,9},{5... | collective-permute-start | bytes 1572872 | tf_op jit(solution)/shard_map/ppermute | solution.py:531
  5.0 1.6 %collective-permute-start = (f32[2,3,8,1024]{3,2,1,0:T(8,128)S(1)}, f32[2,3,8,1024]{3,2,1,0:T(8,128)S(1)}, u32[]{:S(2)}, u32[]{:S(2)}) collective-permute-start(f32[2,3,8,1024]{3,2,1,0:T(8,128)S(1)} %raw_density.1.a_ref), channel_id=1, source_target_pairs={{0,1},{1,0},{2,3},{3,2},{4,5},{5,4},{6,7},{7,6},{8,9},{9,8},{10,11... | collective-permute-start | bytes 589832 | tf_op jit(solution)/shard_map/ppermute | solution.py:536
  7.0 5.4 %collective-permute-done.b_ref = f32[2,3,8,1024]{3,2,1,0:T(8,128)S(1)} collective-permute-done((f32[2,3,8,1024]{3,2,1,0:T(8,128)S(1)}, f32[2,3,8,1024]{3,2,1,0:T(8,128)S(1)}, u32[]{:S(2)}, u32[]{:S(2)}) %collective-permute-start) | collective-permute-done | bytes 196640 | tf_op jit(solution)/shard_map/ppermute | solution.py:536
  12.4 2.7 %collective-permute-start.1 = (f32[2,3,8,1024]{3,2,1,0:T(8,128)S(1)}, f32[2,3,8,1024]{3,2,1,0:T(8,128)S(1)}, u32[]{:S(2)}, u32[]{:S(2)}) collective-permute-start(f32[2,3,8,1024]{3,2,1,0:T(8,128)S(1)} %add.2.refs_0_), channel_id=1, source_target_pairs={{0,2},{1,3},{2,0},{3,1},{4,6},{5,7},{6,4},{7,5},{8,10},{9,11},{10,... | collective-permute-start | bytes 589832 | tf_op jit(solution)/shard_map/ppermute | solution.py:536
  15.4 0.9 %collective-permute-start.8 = (f32[128,8,128]{2,1,0:T(8,128)S(1)}, f32[128,8,128]{2,1,0:T(8,128)S(1)}, u32[]{:S(2)}, u32[]{:S(2)}) collective-permute-start(f32[128,8,128]{2,1,0:T(8,128)S(1)} %take.3.own_ref), channel_id=1, source_target_pairs={{0,24},{4,12},{8,0},{12,20},{16,8},{20,28},{24,16},{28,4},{1,25},{... | collective-permute-start | bytes 1572872 | tf_op jit(solution)/shard_map/ppermute | solution.py:532
  16.2 9.0 %collective-permute-done.3.refs_3_.far_ref = f32[80,8,128]{2,1,0:T(8,128)S(1)} collective-permute-done((f32[80,8,128]{2,1,0:T(8,128)S(1)}, f32[80,8,128]{2,1,0:T(8,128)S(1)}, u32[]{:S(2)}, u32[]{:S(2)}) %collective-permute-start.3) | collective-permute-done | bytes 327712 | tf_op jit(solution)/shard_map/ppermute | solution.py:533
  25.3 0.5 collective-permute-start.7
  25.8 2.5 %collective-permute-start.4 = (f32[3,8,1024]{2,1,0:T(8,128)S(1)}, f32[3,8,1024]{2,1,0:T(8,128)S(1)}, u32[]{:S(2)}, u32[]{:S(2)}) collective-permute-start(f32[3,8,1024]{2,1,0:T(8,128)S(1)} %get-tuple-element.17.refs_7_), channel_id=1, source_target_pairs={{0,20},{4,16},{8,28},{12,24},{16,4},{20,0},{24,12},{28,8},{1,21},{... | collective-permute-start | bytes 294920 | tf_op jit(solution)/shard_map/ppermute | solution.py:533
  28.6 1.7 %collective-permute-start.5 = (f32[3,8,1024]{2,1,0:T(8,128)S(1)}, f32[3,8,1024]{2,1,0:T(8,128)S(1)}, u32[]{:S(2)}, u32[]{:S(2)}) collective-permute-start(f32[3,8,1024]{2,1,0:T(8,128)S(1)} %get-tuple-element.18.refs_1_.refs_2_.refs_3_), channel_id=1, source_target_pairs={{0,8},{4,28},{8,16},{12,4},{16,24},{20,12},{24,0},{28,20},{1,9},{5... | collective-permute-start | bytes 294920 | tf_op jit(solution)/shard_map/ppermute | solution.py:531
  30.3 1.4 %gather.2 = (f32[4,4,32,8,128]{4,3,2,1,0:T(8,128)S(1)}, f32[4,4,8,8,128]{4,3,2,1,0:T(8,128)S(1)}, f32[4,4,8,8,128]{4,3,2,1,0:T(8,128)S(1)}) custom-call(s32[1]{0:T(128)} %bitcast.where_ref, s32[2]{0:T(128)S(1)} %copy-done.3, s32[2]{0:T(128)S(1)} %copy-done.4, bf16[256,384]{1,0:T(8,128)(2,1)S(1)} %copy-done.2, ...), custom_call_target="tpu_custom_call" | custom-call | tf_op jit(solution)/shard_map/gather/pallas_call | solution.py:351
  31.8 0.8 %collective-permute-done.4.refs_3_.refs_0_ = f32[3,8,1024]{2,1,0:T(8,128)S(1)} collective-permute-done((f32[3,8,1024]{2,1,0:T(8,128)S(1)}, f32[3,8,1024]{2,1,0:T(8,128)S(1)}, u32[]{:S(2)}, u32[]{:S(2)}) %collective-permute-start.4) | collective-permute-done | bytes 98336 | tf_op jit(solution)/shard_map/ppermute | solution.py:533
  32.6 2.0 %collective-permute-done.5.refs_0_.refs_1_ = f32[3,8,1024]{2,1,0:T(8,128)S(1)} collective-permute-done((f32[3,8,1024]{2,1,0:T(8,128)S(1)}, f32[3,8,1024]{2,1,0:T(8,128)S(1)}, u32[]{:S(2)}, u32[]{:S(2)}) %collective-permute-start.5) | collective-permute-done | bytes 98336 | tf_op jit(solution)/shard_map/ppermute | solution.py:531
  34.7 0.6 %collective-permute-start.11 = (f32[128,8,128]{2,1,0:T(8,128)S(1)}, f32[128,8,128]{2,1,0:T(8,128)S(1)}, u32[]{:S(2)}, u32[]{:S(2)}) collective-permute-start(f32[128,8,128]{2,1,0:T(8,128)S(1)} %join.5), channel_id=1, source_target_pairs={{0,4},{4,0},{8,12},{12,8},{16,20},{20,16},{24,28},{28,24},{1,5},{5... | collective-permute-start | bytes 1572872 | tf_op jit(solution)/shard_map/ppermute | solution.py:41
  35.3 1.0 %collective-permute-done.10 = f32[9,8,1024]{2,1,0:T(8,128)S(1)} collective-permute-done((f32[9,8,1024]{2,1,0:T(8,128)S(1)}, f32[9,8,1024]{2,1,0:T(8,128)S(1)}, u32[]{:S(2)}, u32[]{:S(2)}) %collective-permute-start.10) | collective-permute-done | bytes 294944 | tf_op jit(solution)/shard_map/ppermute | solution.py:41
  36.3 1.2 %placed_fields.1.fields = f32[3,14,8,128]{3,2,1,0:T(8,128)S(1)} custom-call(s32[1]{0:T(128)} %bitcast.where_ref, s32[2]{0:T(128)S(1)} %copy-done.3, s32[2]{0:T(128)S(1)} %copy-done.4, f32[3,8,1024]{2,1,0:T(8,128)S(1)} %collective-permute-done.4.refs_3_.refs_0_, f32[3,8,1024]{2,1,0:T(8,128)S(1)} %collective-permute-done.5.refs_0_.refs_1_, ...), custom_call_target="tpu_custom_call" | custom-call | tf_op jit(solution)/shard_map/placed_fields/pallas_call | solution.py:268
  37.5 1.4 %gather.3 = (f32[4,4,32,8,128]{4,3,2,1,0:T(8,128)S(1)}, f32[4,4,8,8,128]{4,3,2,1,0:T(8,128)S(1)}, f32[4,4,8,8,128]{4,3,2,1,0:T(8,128)S(1)}) custom-call(s32[1]{0:T(128)} %bitcast.where_ref, s32[2]{0:T(128)S(1)} %copy-done.3, s32[2]{0:T(128)S(1)} %copy-done.4, bf16[256,384]{1,0:T(8,128)(2,1)S(1)} %copy-done.2, ...), custom_call_target="tpu_custom_call" | custom-call | tf_op jit(solution)/shard_map/gather/pallas_call | solution.py:351
  39.3 1.6 %collective-permute-start.12 = (f32[3,8,1024]{2,1,0:T(8,128)S(1)}, f32[3,8,1024]{2,1,0:T(8,128)S(1)}, u32[]{:S(2)}, u32[]{:S(2)}) collective-permute-start(f32[3,8,1024]{2,1,0:T(8,128)S(1)} %density.1.a_ref), channel_id=1, source_target_pairs={{0,1},{1,0},{2,3},{3,2},{4,5},{5,4},{6,7},{7,6},{8,9},{9,8},{10,11... | collective-permute-start | bytes 294920 | tf_op jit(solution)/shard_map/ppermute | solution.py:536
  41.0 2.6 %free_part.2 = (f32[1,4,4,8,1024]{4,3,2,1,0:T(8,128)S(1)}, f32[1,4,4,8,1024]{4,3,2,1,0:T(8,128)S(1)}) custom-call(s32[1]{0:T(128)} %bitcast.where_ref, s32[2]{0:T(128)S(1)} %copy-done.3, bf16[256,384]{1,0:T(8,128)(2,1)S(1)} %copy-done.2, f32[3,14,8,128]{3,2,1,0:T(8,128)S(1)} %placed_fields.1.fields, f32[4,4,32,8,128]{4,3,2,1,0:T(8,128)S(1)} %get-tuple-element.23.refs_0_, ...), custom_call_target="tpu_custom_call" | custom-call | tf_op jit(solution)/shard_map/free_part/pallas_call | solution.py:456
  43.6 0.7 %collective-permute-done.12.b_ref = f32[3,8,1024]{2,1,0:T(8,128)S(1)} collective-permute-done((f32[3,8,1024]{2,1,0:T(8,128)S(1)}, f32[3,8,1024]{2,1,0:T(8,128)S(1)}, u32[]{:S(2)}, u32[]{:S(2)}) %collective-permute-start.12) | collective-permute-done | bytes 98336 | tf_op jit(solution)/shard_map/ppermute | solution.py:536
  44.2 2.1 %collective-permute-start.13 = (f32[3,8,1024]{2,1,0:T(8,128)S(1)}, f32[3,8,1024]{2,1,0:T(8,128)S(1)}, u32[]{:S(2)}, u32[]{:S(2)}) collective-permute-start(f32[3,8,1024]{2,1,0:T(8,128)S(1)} %add.3.refs_0_), channel_id=1, source_target_pairs={{0,2},{1,3},{2,0},{3,1},{4,6},{5,7},{6,4},{7,5},{8,10},{9,11},{10,... | collective-permute-start | bytes 294920 | tf_op jit(solution)/shard_map/ppermute | solution.py:536
  46.4 2.6 %free_part.3 = (f32[1,4,4,8,1024]{4,3,2,1,0:T(8,128)S(1)}, f32[1,4,4,8,1024]{4,3,2,1,0:T(8,128)S(1)}) custom-call(s32[1]{0:T(128)} %bitcast.where_ref, s32[2]{0:T(128)S(1)} %copy-done.3, bf16[256,384]{1,0:T(8,128)(2,1)S(1)} %copy-done.2, f32[3,14,8,128]{3,2,1,0:T(8,128)S(1)} %placed_fields.1.fields, f32[4,4,32,8,128]{4,3,2,1,0:T(8,128)S(1)} %get-tuple-element.25.refs_0_, ...), custom_call_target="tpu_custom_call" | custom-call | tf_op jit(solution)/shard_map/free_part/pallas_call | solution.py:456
  48.9 2.4 %collective-permute-done.13.refs_1_ = f32[3,8,1024]{2,1,0:T(8,128)S(1)} collective-permute-done((f32[3,8,1024]{2,1,0:T(8,128)S(1)}, f32[3,8,1024]{2,1,0:T(8,128)S(1)}, u32[]{:S(2)}, u32[]{:S(2)}) %collective-permute-start.13) | collective-permute-done | bytes 98336 | tf_op jit(solution)/shard_map/ppermute | solution.py:536
  51.3 1.1 %last_part.1 = f32[2,4,4,8,1024]{4,3,2,1,0:T(8,128)} custom-call(s32[1]{0:T(128)} %bitcast.where_ref, f32[3,8,1024]{2,1,0:T(8,128)S(1)} %add.3.refs_0_, f32[3,8,1024]{2,1,0:T(8,128)S(1)} %collective-permute-done.13.refs_1_, f32[1,4,4,8,1024]{4,3,2,1,0:T(8,128)S(1)} %get-tuple-element.24.refs_0_.refs_2_, f32[1,4,4,8,1024]{4,3,2,1,0:T(8,128)S(1)} %get-tuple-element.26.refs_3_, ...), custom_call_target="tpu_custom_call" | custom-call | tf_op jit(solution)/shard_map/last_part/pallas_call | solution.py:512
  (32 shorter events, 2.3 us)
Async XLA Ops:
  0.0 1.2 %copy-start = (f32[2,4,4,8,1024]{4,3,2,1,0:T(8,128)S(1)}, f32[2,4,4,8,1024]{4,3,2,1,0:T(8,128)}, u32[]{:S(2)}) copy-start(f32[2,4,4,8,1024]{4,3,2,1,0:T(8,128)} %x_ref.7) | copy-start | bytes 3145732
  1.2 3.6 %copy-start.1 = (f32[2,4,4,8,1024]{4,3,2,1,0:T(8,128)S(1)}, f32[2,4,4,8,1024]{4,3,2,1,0:T(8,128)}, u32[]{:S(2)}) copy-start(f32[2,4,4,8,1024]{4,3,2,1,0:T(8,128)} %x_ref.7) | copy-start | bytes 3145732
  1.5 23.8 %collective-permute-start.2 = (f32[128,8,128]{2,1,0:T(8,128)S(1)}, f32[128,8,128]{2,1,0:T(8,128)S(1)}, u32[]{:S(2)}, u32[]{:S(2)}) collective-permute-start(f32[128,8,128]{2,1,0:T(8,128)S(1)} %take.2.refs_0_.own_ref), channel_id=1, source_target_pairs={{0,8},{4,28},{8,16},{12,4},{16,24},{20,12},{24,0},{28,20},{1,9},{5... | collective-permute-start | bytes 1572872 | tf_op jit(solution)/shard_map/ppermute | solution.py:531
  5.0 7.4 %collective-permute-start = (f32[2,3,8,1024]{3,2,1,0:T(8,128)S(1)}, f32[2,3,8,1024]{3,2,1,0:T(8,128)S(1)}, u32[]{:S(2)}, u32[]{:S(2)}) collective-permute-start(f32[2,3,8,1024]{3,2,1,0:T(8,128)S(1)} %raw_density.1.a_ref), channel_id=1, source_target_pairs={{0,1},{1,0},{2,3},{3,2},{4,5},{5,4},{6,7},{7,6},{8,9},{9,8},{10,11... | collective-permute-start | bytes 589832 | tf_op jit(solution)/shard_map/ppermute | solution.py:536
  6.6 18.7 %collective-permute-start.3 = (f32[80,8,128]{2,1,0:T(8,128)S(1)}, f32[80,8,128]{2,1,0:T(8,128)S(1)}, u32[]{:S(2)}, u32[]{:S(2)}) collective-permute-start(f32[80,8,128]{2,1,0:T(8,128)S(1)} %take_extra.1.refs_0_), channel_id=1, source_target_pairs={{0,20},{4,16},{8,28},{12,24},{16,4},{20,0},{24,12},{28,8},{1,21},{... | collective-permute-start | bytes 983048 | tf_op jit(solution)/shard_map/ppermute | solution.py:533
  12.4 17.9 %copy-start.2 = (bf16[256,384]{1,0:T(8,128)(2,1)S(1)}, bf16[256,384]{1,0:T(8,128)(2,1)}, u32[]{:S(2)}) copy-start(bf16[256,384]{1,0:T(8,128)(2,1)} %constant.8.clone.weights_ref) | copy-start | bytes 589828
  12.4 17.9 %copy-start.3 = (s32[2]{0:T(128)S(1)}, s32[2]{0:T(128)}, u32[]{:S(2)}) copy-start(s32[2]{0:T(128)} %shift_ref.9) | copy-start | bytes 28
  12.4 17.9 %copy-start.4 = (s32[2]{0:T(128)S(1)}, s32[2]{0:T(128)}, u32[]{:S(2)}) copy-start(s32[2]{0:T(128)} %wave_ref.5) | copy-start | bytes 28
  12.4 12.9 %collective-permute-start.1 = (f32[2,3,8,1024]{3,2,1,0:T(8,128)S(1)}, f32[2,3,8,1024]{3,2,1,0:T(8,128)S(1)}, u32[]{:S(2)}, u32[]{:S(2)}) collective-permute-start(f32[2,3,8,1024]{3,2,1,0:T(8,128)S(1)} %add.2.refs_0_), channel_id=1, source_target_pairs={{0,2},{1,3},{2,0},{3,1},{4,6},{5,7},{6,4},{7,5},{8,10},{9,11},{10,... | collective-permute-start | bytes 589832 | tf_op jit(solution)/shard_map/ppermute | solution.py:536
  15.4 13.2 %collective-permute-start.8 = (f32[128,8,128]{2,1,0:T(8,128)S(1)}, f32[128,8,128]{2,1,0:T(8,128)S(1)}, u32[]{:S(2)}, u32[]{:S(2)}) collective-permute-start(f32[128,8,128]{2,1,0:T(8,128)S(1)} %take.3.own_ref), channel_id=1, source_target_pairs={{0,24},{4,12},{8,0},{12,20},{16,8},{20,28},{24,16},{28,4},{1,25},{... | collective-permute-start | bytes 1572872 | tf_op jit(solution)/shard_map/ppermute | solution.py:532
  16.2 14.1 %collective-permute-start.9 = (f32[128,8,128]{2,1,0:T(8,128)S(1)}, f32[128,8,128]{2,1,0:T(8,128)S(1)}, u32[]{:S(2)}, u32[]{:S(2)}) collective-permute-start(f32[128,8,128]{2,1,0:T(8,128)S(1)} %take.2.refs_0_.own_ref), channel_id=1, source_target_pairs={{0,4},{4,0},{8,12},{12,8},{16,20},{20,16},{24,28},{28,24},{1,5},{5... | collective-permute-start | bytes 1572872 | tf_op jit(solution)/shard_map/ppermute | solution.py:41
  25.3 5.0 %collective-permute-start.7 = (f32[128,8,128]{2,1,0:T(8,128)S(1)}, f32[128,8,128]{2,1,0:T(8,128)S(1)}, u32[]{:S(2)}, u32[]{:S(2)}) collective-permute-start(f32[128,8,128]{2,1,0:T(8,128)S(1)} %join.3), channel_id=1, source_target_pairs={{0,4},{4,0},{8,12},{12,8},{16,20},{20,16},{24,28},{28,24},{1,5},{5... | collective-permute-start | bytes 1572872 | tf_op jit(solution)/shard_map/ppermute | solution.py:41
  25.8 6.0 %collective-permute-start.6 = (f32[3,8,1024]{2,1,0:T(8,128)S(1)}, f32[3,8,1024]{2,1,0:T(8,128)S(1)}, u32[]{:S(2)}, u32[]{:S(2)}) collective-permute-start(f32[3,8,1024]{2,1,0:T(8,128)S(1)} %get-tuple-element.17.refs_7_), channel_id=1, source_target_pairs={{0,24},{4,12},{8,0},{12,20},{16,8},{20,28},{24,16},{28,4},{1,25},{... | collective-permute-start | bytes 294920 | tf_op jit(solution)/shard_map/ppermute | solution.py:532
  25.8 6.8 %collective-permute-start.4 = (f32[3,8,1024]{2,1,0:T(8,128)S(1)}, f32[3,8,1024]{2,1,0:T(8,128)S(1)}, u32[]{:S(2)}, u32[]{:S(2)}) collective-permute-start(f32[3,8,1024]{2,1,0:T(8,128)S(1)} %get-tuple-element.17.refs_7_), channel_id=1, source_target_pairs={{0,20},{4,16},{8,28},{12,24},{16,4},{20,0},{24,12},{28,8},{1,21},{... | collective-permute-start | bytes 294920 | tf_op jit(solution)/shard_map/ppermute | solution.py:533
  28.6 6.0 %collective-permute-start.5 = (f32[3,8,1024]{2,1,0:T(8,128)S(1)}, f32[3,8,1024]{2,1,0:T(8,128)S(1)}, u32[]{:S(2)}, u32[]{:S(2)}) collective-permute-start(f32[3,8,1024]{2,1,0:T(8,128)S(1)} %get-tuple-element.18.refs_1_.refs_2_.refs_3_), channel_id=1, source_target_pairs={{0,8},{4,28},{8,16},{12,4},{16,24},{20,12},{24,0},{28,20},{1,9},{5... | collective-permute-start | bytes 294920 | tf_op jit(solution)/shard_map/ppermute | solution.py:531
  34.6 1.6 %collective-permute-start.10 = (f32[9,8,1024]{2,1,0:T(8,128)S(1)}, f32[9,8,1024]{2,1,0:T(8,128)S(1)}, u32[]{:S(2)}, u32[]{:S(2)}) collective-permute-start(f32[9,8,1024]{2,1,0:T(8,128)S(1)} %join.4.refs_1_), channel_id=1, source_target_pairs={{0,4},{4,0},{8,12},{12,8},{16,20},{20,16},{24,28},{28,24},{1,5},{5... | collective-permute-start | bytes 884744 | tf_op jit(solution)/shard_map/ppermute | solution.py:41
  34.7 2.8 %collective-permute-start.11 = (f32[128,8,128]{2,1,0:T(8,128)S(1)}, f32[128,8,128]{2,1,0:T(8,128)S(1)}, u32[]{:S(2)}, u32[]{:S(2)}) collective-permute-start(f32[128,8,128]{2,1,0:T(8,128)S(1)} %join.5), channel_id=1, source_target_pairs={{0,4},{4,0},{8,12},{12,8},{16,20},{20,16},{24,28},{28,24},{1,5},{5... | collective-permute-start | bytes 1572872 | tf_op jit(solution)/shard_map/ppermute | solution.py:41
  39.3 4.9 %collective-permute-start.12 = (f32[3,8,1024]{2,1,0:T(8,128)S(1)}, f32[3,8,1024]{2,1,0:T(8,128)S(1)}, u32[]{:S(2)}, u32[]{:S(2)}) collective-permute-start(f32[3,8,1024]{2,1,0:T(8,128)S(1)} %density.1.a_ref), channel_id=1, source_target_pairs={{0,1},{1,0},{2,3},{3,2},{4,5},{5,4},{6,7},{7,6},{8,9},{9,8},{10,11... | collective-permute-start | bytes 294920 | tf_op jit(solution)/shard_map/ppermute | solution.py:536
  44.2 7.1 %collective-permute-start.13 = (f32[3,8,1024]{2,1,0:T(8,128)S(1)}, f32[3,8,1024]{2,1,0:T(8,128)S(1)}, u32[]{:S(2)}, u32[]{:S(2)}) collective-permute-start(f32[3,8,1024]{2,1,0:T(8,128)S(1)} %add.3.refs_0_), channel_id=1, source_target_pairs={{0,2},{1,3},{2,0},{3,1},{4,6},{5,7},{6,4},{7,5},{8,10},{9,11},{10,... | collective-permute-start | bytes 294920 | tf_op jit(solution)/shard_map/ppermute | solution.py:536

commit v5 on v3

--- a/solution.py
+++ b/solution.py
@@ -554,7 +554,7 @@
     other_second = [odd_on(piece) for piece in other]
     terms = two_terms(raw_density(cloud_states, *mine, *other))
     extra = across(take_extra(where, cloud_states, mine[0]))
-    mine_sums, other_sums = total_of(where, terms, *mine_second, extra)
+    mine_sums, other_sums = total_of(where, terms, extra)
 
     mine_sums_second, other_sums_second, far_sums = even_on(mine_sums), odd_on(other_sums), across(other_sums)
     other_next = swapped(mine[0])

time: 52.3 us -> 52.3 us (level)
  no operation moved by 1% of the time
where the time goes in v5:
time: 52.3 us; the launch traced here: 52.1 us
  waiting for transfers between devices  20.5 us (39%)
  starting transfers between devices  18.2 us (35%)
  Pallas kernels  11.9 us (23%)
  local copies, waits for them, and re-layouts  1.27 us (2%)
    ppermute x2, waiting for transfers between devices, local(): lax.ppermute(a, 'slab', [(i, (i + 3 if i % 2 else i - 3) % slab_count) fo...  10.6 us
    ppermute x4, starting transfers between devices, paired(): return lax.ppermute(a, 'grp', [(i, i ^ bit) for i in range(group_count)])  8.61 us
    ppermute x4, waiting for transfers between devices, paired(): return lax.ppermute(a, 'grp', [(i, i ^ bit) for i in range(group_count)])  7.47 us
    pallas_call x2, Pallas kernels, free_part(): pl.pallas_call(functools.partial(free_kernel, tuple(places)), out_shape=[...  5.19 us
    ppermute x2, starting transfers between devices, local(): lax.ppermute(a, 'slab', [(i, (i - 2 if i % 2 else i + 2) % slab_count) fo...  4.78 us
    ppermute x2, starting transfers between devices, local(): lax.ppermute(a, 'slab', [(i, (i + 3 if i % 2 else i - 3) % slab_count) fo...  2.89 us
    pallas_call x2, Pallas kernels, gather(): pl.pallas_call(functools.partial(gather_kernel, depth, planes, mine, star...  2.85 us
    ppermute x2, waiting for transfers between devices, local(): lax.ppermute(a, 'slab', [(i, (i - 2 if i % 2 else i + 2) % slab_count) fo...  1.48 us
  transfers between devices with their start and end apart: 14, of which 7 were waited for; matrix products, arithmetic and copies ran while one was open for 0% of the time, Pallas kernels for 17%

profile of v5, /device:TPU:0, one launch (start us, length us, event | category | flops | bytes accessed | tf_op | source)
XLA Modules:
  0.0 52.1 jit_solution(13724671490484481448)
XLA Ops:
  0.0 1.2 %copy-done = f32[2,4,4,8,1024]{4,3,2,1,0:T(8,128)S(1)} copy-done((f32[2,4,4,8,1024]{4,3,2,1,0:T(8,128)S(1)}, f32[2,4,4,8,1024]{4,3,2,1,0:T(8,128)}, u32[]{:S(2)}) %copy-start) | copy-done | bytes 1048600
  1.5 3.0 %collective-permute-start.6 = (f32[128,8,128]{2,1,0:T(8,128)S(1)}, f32[128,8,128]{2,1,0:T(8,128)S(1)}, u32[]{:S(2)}, u32[]{:S(2)}) collective-permute-start(f32[128,8,128]{2,1,0:T(8,128)S(1)} %take.2.refs_0_.own_ref), channel_id=1, source_target_pairs={{0,8},{4,28},{8,16},{12,4},{16,24},{20,12},{24,0},{28,20},{1,9},{5... | collective-permute-start | bytes 1572872 | tf_op jit(solution)/shard_map/ppermute | solution.py:531
  5.0 1.6 %collective-permute-start = (f32[2,3,8,1024]{3,2,1,0:T(8,128)S(1)}, f32[2,3,8,1024]{3,2,1,0:T(8,128)S(1)}, u32[]{:S(2)}, u32[]{:S(2)}) collective-permute-start(f32[2,3,8,1024]{3,2,1,0:T(8,128)S(1)} %raw_density.1.a_ref), channel_id=1, source_target_pairs={{0,1},{1,0},{2,3},{3,2},{4,5},{5,4},{6,7},{7,6},{8,9},{9,8},{10,11... | collective-permute-start | bytes 589832 | tf_op jit(solution)/shard_map/ppermute | solution.py:536
  7.3 5.0 %collective-permute-done.b_ref = f32[2,3,8,1024]{3,2,1,0:T(8,128)S(1)} collective-permute-done((f32[2,3,8,1024]{3,2,1,0:T(8,128)S(1)}, f32[2,3,8,1024]{3,2,1,0:T(8,128)S(1)}, u32[]{:S(2)}, u32[]{:S(2)}) %collective-permute-start) | collective-permute-done | bytes 196640 | tf_op jit(solution)/shard_map/ppermute | solution.py:536
  12.4 2.7 %collective-permute-start.1 = (f32[2,3,8,1024]{3,2,1,0:T(8,128)S(1)}, f32[2,3,8,1024]{3,2,1,0:T(8,128)S(1)}, u32[]{:S(2)}, u32[]{:S(2)}) collective-permute-start(f32[2,3,8,1024]{3,2,1,0:T(8,128)S(1)} %add.2.refs_0_), channel_id=1, source_target_pairs={{0,2},{1,3},{2,0},{3,1},{4,6},{5,7},{6,4},{7,5},{8,10},{9,11},{10,... | collective-permute-start | bytes 589832 | tf_op jit(solution)/shard_map/ppermute | solution.py:536
  15.0 0.8 %collective-permute-start.8 = (f32[128,8,128]{2,1,0:T(8,128)S(1)}, f32[128,8,128]{2,1,0:T(8,128)S(1)}, u32[]{:S(2)}, u32[]{:S(2)}) collective-permute-start(f32[128,8,128]{2,1,0:T(8,128)S(1)} %take.3.refs_1_.own_ref), channel_id=1, source_target_pairs={{0,24},{4,12},{8,0},{12,20},{16,8},{20,28},{24,16},{28,4},{1,25},{... | collective-permute-start | bytes 1572872 | tf_op jit(solution)/shard_map/ppermute | solution.py:532
  15.9 9.6 %collective-permute-done.2.refs_2_.far_ref = f32[80,8,128]{2,1,0:T(8,128)S(1)} collective-permute-done((f32[80,8,128]{2,1,0:T(8,128)S(1)}, f32[80,8,128]{2,1,0:T(8,128)S(1)}, u32[]{:S(2)}, u32[]{:S(2)}) %collective-permute-start.2) | collective-permute-done | bytes 327712 | tf_op jit(solution)/shard_map/ppermute | solution.py:533
  25.5 0.5 collective-permute-start.7
  26.0 2.5 %collective-permute-start.3 = (f32[3,8,1024]{2,1,0:T(8,128)S(1)}, f32[3,8,1024]{2,1,0:T(8,128)S(1)}, u32[]{:S(2)}, u32[]{:S(2)}) collective-permute-start(f32[3,8,1024]{2,1,0:T(8,128)S(1)} %get-tuple-element.17.refs_7_), channel_id=1, source_target_pairs={{0,20},{4,16},{8,28},{12,24},{16,4},{20,0},{24,12},{28,8},{1,21},{... | collective-permute-start | bytes 294920 | tf_op jit(solution)/shard_map/ppermute | solution.py:533
  28.5 1.8 %collective-permute-start.4 = (f32[3,8,1024]{2,1,0:T(8,128)S(1)}, f32[3,8,1024]{2,1,0:T(8,128)S(1)}, u32[]{:S(2)}, u32[]{:S(2)}) collective-permute-start(f32[3,8,1024]{2,1,0:T(8,128)S(1)} %get-tuple-element.18.refs_1_.refs_2_.refs_3_), channel_id=1, source_target_pairs={{0,8},{4,28},{8,16},{12,4},{16,24},{20,12},{24,0},{28,20},{1,9},{5... | collective-permute-start | bytes 294920 | tf_op jit(solution)/shard_map/ppermute | solution.py:531
  30.3 1.4 %gather.2 = (f32[4,4,32,8,128]{4,3,2,1,0:T(8,128)S(1)}, f32[4,4,8,8,128]{4,3,2,1,0:T(8,128)S(1)}, f32[4,4,8,8,128]{4,3,2,1,0:T(8,128)S(1)}) custom-call(s32[1]{0:T(128)} %bitcast.where_ref, s32[2]{0:T(128)S(1)} %copy-done.3, s32[2]{0:T(128)S(1)} %copy-done.4, bf16[256,384]{1,0:T(8,128)(2,1)S(1)} %copy-done.2, ...), custom_call_target="tpu_custom_call" | custom-call | tf_op jit(solution)/shard_map/gather/pallas_call | solution.py:351
  31.8 1.0 %collective-permute-done.3.refs_3_.refs_0_ = f32[3,8,1024]{2,1,0:T(8,128)S(1)} collective-permute-done((f32[3,8,1024]{2,1,0:T(8,128)S(1)}, f32[3,8,1024]{2,1,0:T(8,128)S(1)}, u32[]{:S(2)}, u32[]{:S(2)}) %collective-permute-start.3) | collective-permute-done | bytes 98336 | tf_op jit(solution)/shard_map/ppermute | solution.py:533
  32.7 1.5 %collective-permute-done.4.refs_0_.refs_1_ = f32[3,8,1024]{2,1,0:T(8,128)S(1)} collective-permute-done((f32[3,8,1024]{2,1,0:T(8,128)S(1)}, f32[3,8,1024]{2,1,0:T(8,128)S(1)}, u32[]{:S(2)}, u32[]{:S(2)}) %collective-permute-start.4) | collective-permute-done | bytes 98336 | tf_op jit(solution)/shard_map/ppermute | solution.py:531
  34.4 0.6 %collective-permute-start.11 = (f32[128,8,128]{2,1,0:T(8,128)S(1)}, f32[128,8,128]{2,1,0:T(8,128)S(1)}, u32[]{:S(2)}, u32[]{:S(2)}) collective-permute-start(f32[128,8,128]{2,1,0:T(8,128)S(1)} %join.5), channel_id=1, source_target_pairs={{0,4},{4,0},{8,12},{12,8},{16,20},{20,16},{24,28},{28,24},{1,5},{5... | collective-permute-start | bytes 1572872 | tf_op jit(solution)/shard_map/ppermute | solution.py:41
  34.9 1.0 %collective-permute-done.10 = f32[9,8,1024]{2,1,0:T(8,128)S(1)} collective-permute-done((f32[9,8,1024]{2,1,0:T(8,128)S(1)}, f32[9,8,1024]{2,1,0:T(8,128)S(1)}, u32[]{:S(2)}, u32[]{:S(2)}) %collective-permute-start.10) | collective-permute-done | bytes 294944 | tf_op jit(solution)/shard_map/ppermute | solution.py:41
  35.9 1.2 %placed_fields.1.fields = f32[3,14,8,128]{3,2,1,0:T(8,128)S(1)} custom-call(s32[1]{0:T(128)} %bitcast.where_ref, s32[2]{0:T(128)S(1)} %copy-done.3, s32[2]{0:T(128)S(1)} %copy-done.4, f32[3,8,1024]{2,1,0:T(8,128)S(1)} %collective-permute-done.3.refs_3_.refs_0_, f32[3,8,1024]{2,1,0:T(8,128)S(1)} %collective-permute-done.4.refs_0_.refs_1_, ...), custom_call_target="tpu_custom_call" | custom-call | tf_op jit(solution)/shard_map/placed_fields/pallas_call | solution.py:268
  37.1 1.4 %gather.3 = (f32[4,4,32,8,128]{4,3,2,1,0:T(8,128)S(1)}, f32[4,4,8,8,128]{4,3,2,1,0:T(8,128)S(1)}, f32[4,4,8,8,128]{4,3,2,1,0:T(8,128)S(1)}) custom-call(s32[1]{0:T(128)} %bitcast.where_ref, s32[2]{0:T(128)S(1)} %copy-done.3, s32[2]{0:T(128)S(1)} %copy-done.4, bf16[256,384]{1,0:T(8,128)(2,1)S(1)} %copy-done.2, ...), custom_call_target="tpu_custom_call" | custom-call | tf_op jit(solution)/shard_map/gather/pallas_call | solution.py:351
  39.0 1.6 %collective-permute-start.12 = (f32[3,8,1024]{2,1,0:T(8,128)S(1)}, f32[3,8,1024]{2,1,0:T(8,128)S(1)}, u32[]{:S(2)}, u32[]{:S(2)}) collective-permute-start(f32[3,8,1024]{2,1,0:T(8,128)S(1)} %density.1.a_ref), channel_id=1, source_target_pairs={{0,1},{1,0},{2,3},{3,2},{4,5},{5,4},{6,7},{7,6},{8,9},{9,8},{10,11... | collective-permute-start | bytes 294920 | tf_op jit(solution)/shard_map/ppermute | solution.py:536
  40.6 2.6 %free_part.2 = (f32[1,4,4,8,1024]{4,3,2,1,0:T(8,128)S(1)}, f32[1,4,4,8,1024]{4,3,2,1,0:T(8,128)S(1)}) custom-call(s32[1]{0:T(128)} %bitcast.where_ref, s32[2]{0:T(128)S(1)} %copy-done.3, bf16[256,384]{1,0:T(8,128)(2,1)S(1)} %copy-done.2, f32[3,14,8,128]{3,2,1,0:T(8,128)S(1)} %placed_fields.1.fields, f32[4,4,32,8,128]{4,3,2,1,0:T(8,128)S(1)} %get-tuple-element.23.refs_0_, ...), custom_call_target="tpu_custom_call" | custom-call | tf_op jit(solution)/shard_map/free_part/pallas_call | solution.py:456
  43.2 0.7 %collective-permute-done.12.b_ref = f32[3,8,1024]{2,1,0:T(8,128)S(1)} collective-permute-done((f32[3,8,1024]{2,1,0:T(8,128)S(1)}, f32[3,8,1024]{2,1,0:T(8,128)S(1)}, u32[]{:S(2)}, u32[]{:S(2)}) %collective-permute-start.12) | collective-permute-done | bytes 98336 | tf_op jit(solution)/shard_map/ppermute | solution.py:536
  43.9 2.7 %collective-permute-start.13 = (f32[3,8,1024]{2,1,0:T(8,128)S(1)}, f32[3,8,1024]{2,1,0:T(8,128)S(1)}, u32[]{:S(2)}, u32[]{:S(2)}) collective-permute-start(f32[3,8,1024]{2,1,0:T(8,128)S(1)} %add.3.refs_0_), channel_id=1, source_target_pairs={{0,2},{1,3},{2,0},{3,1},{4,6},{5,7},{6,4},{7,5},{8,10},{9,11},{10,... | collective-permute-start | bytes 294920 | tf_op jit(solution)/shard_map/ppermute | solution.py:536
  46.6 2.6 %free_part.3 = (f32[1,4,4,8,1024]{4,3,2,1,0:T(8,128)S(1)}, f32[1,4,4,8,1024]{4,3,2,1,0:T(8,128)S(1)}) custom-call(s32[1]{0:T(128)} %bitcast.where_ref, s32[2]{0:T(128)S(1)} %copy-done.3, bf16[256,384]{1,0:T(8,128)(2,1)S(1)} %copy-done.2, f32[3,14,8,128]{3,2,1,0:T(8,128)S(1)} %placed_fields.1.fields, f32[4,4,32,8,128]{4,3,2,1,0:T(8,128)S(1)} %get-tuple-element.25.refs_0_, ...), custom_call_target="tpu_custom_call" | custom-call | tf_op jit(solution)/shard_map/free_part/pallas_call | solution.py:456
  49.2 1.8 %collective-permute-done.13.refs_1_ = f32[3,8,1024]{2,1,0:T(8,128)S(1)} collective-permute-done((f32[3,8,1024]{2,1,0:T(8,128)S(1)}, f32[3,8,1024]{2,1,0:T(8,128)S(1)}, u32[]{:S(2)}, u32[]{:S(2)}) %collective-permute-start.13) | collective-permute-done | bytes 98336 | tf_op jit(solution)/shard_map/ppermute | solution.py:536
  51.0 1.1 %last_part.1 = f32[2,4,4,8,1024]{4,3,2,1,0:T(8,128)} custom-call(s32[1]{0:T(128)} %bitcast.where_ref, f32[3,8,1024]{2,1,0:T(8,128)S(1)} %add.3.refs_0_, f32[3,8,1024]{2,1,0:T(8,128)S(1)} %collective-permute-done.13.refs_1_, f32[1,4,4,8,1024]{4,3,2,1,0:T(8,128)S(1)} %get-tuple-element.24.refs_0_.refs_2_, f32[1,4,4,8,1024]{4,3,2,1,0:T(8,128)S(1)} %get-tuple-element.26.refs_3_, ...), custom_call_target="tpu_custom_call" | custom-call | tf_op jit(solution)/shard_map/last_part/pallas_call | solution.py:512
  (32 shorter events, 2.1 us)
Async XLA Ops:
  0.0 1.2 %copy-start = (f32[2,4,4,8,1024]{4,3,2,1,0:T(8,128)S(1)}, f32[2,4,4,8,1024]{4,3,2,1,0:T(8,128)}, u32[]{:S(2)}) copy-start(f32[2,4,4,8,1024]{4,3,2,1,0:T(8,128)} %x_ref.7) | copy-start | bytes 3145732
  1.2 3.6 %copy-start.1 = (f32[2,4,4,8,1024]{4,3,2,1,0:T(8,128)S(1)}, f32[2,4,4,8,1024]{4,3,2,1,0:T(8,128)}, u32[]{:S(2)}) copy-start(f32[2,4,4,8,1024]{4,3,2,1,0:T(8,128)} %x_ref.7) | copy-start | bytes 3145732
  1.5 24.0 %collective-permute-start.6 = (f32[128,8,128]{2,1,0:T(8,128)S(1)}, f32[128,8,128]{2,1,0:T(8,128)S(1)}, u32[]{:S(2)}, u32[]{:S(2)}) collective-permute-start(f32[128,8,128]{2,1,0:T(8,128)S(1)} %take.2.refs_0_.own_ref), channel_id=1, source_target_pairs={{0,8},{4,28},{8,16},{12,4},{16,24},{20,12},{24,0},{28,20},{1,9},{5... | collective-permute-start | bytes 1572872 | tf_op jit(solution)/shard_map/ppermute | solution.py:531
  4.9 25.4 %copy-start.2 = (bf16[256,384]{1,0:T(8,128)(2,1)S(1)}, bf16[256,384]{1,0:T(8,128)(2,1)}, u32[]{:S(2)}) copy-start(bf16[256,384]{1,0:T(8,128)(2,1)} %constant.8.clone.weights_ref) | copy-start | bytes 589828
  4.9 25.4 %copy-start.3 = (s32[2]{0:T(128)S(1)}, s32[2]{0:T(128)}, u32[]{:S(2)}) copy-start(s32[2]{0:T(128)} %shift_ref.9) | copy-start | bytes 28
  4.9 25.4 %copy-start.4 = (s32[2]{0:T(128)S(1)}, s32[2]{0:T(128)}, u32[]{:S(2)}) copy-start(s32[2]{0:T(128)} %wave_ref.5) | copy-start | bytes 28
  5.0 7.4 %collective-permute-start = (f32[2,3,8,1024]{3,2,1,0:T(8,128)S(1)}, f32[2,3,8,1024]{3,2,1,0:T(8,128)S(1)}, u32[]{:S(2)}, u32[]{:S(2)}) collective-permute-start(f32[2,3,8,1024]{3,2,1,0:T(8,128)S(1)} %raw_density.1.a_ref), channel_id=1, source_target_pairs={{0,1},{1,0},{2,3},{3,2},{4,5},{5,4},{6,7},{7,6},{8,9},{9,8},{10,11... | collective-permute-start | bytes 589832 | tf_op jit(solution)/shard_map/ppermute | solution.py:536
  6.9 18.5 %collective-permute-start.2 = (f32[80,8,128]{2,1,0:T(8,128)S(1)}, f32[80,8,128]{2,1,0:T(8,128)S(1)}, u32[]{:S(2)}, u32[]{:S(2)}) collective-permute-start(f32[80,8,128]{2,1,0:T(8,128)S(1)} %take_extra.1), channel_id=1, source_target_pairs={{0,20},{4,16},{8,28},{12,24},{16,4},{20,0},{24,12},{28,8},{1,21},{... | collective-permute-start | bytes 983048 | tf_op jit(solution)/shard_map/ppermute | solution.py:533
  12.4 13.1 %collective-permute-start.1 = (f32[2,3,8,1024]{3,2,1,0:T(8,128)S(1)}, f32[2,3,8,1024]{3,2,1,0:T(8,128)S(1)}, u32[]{:S(2)}, u32[]{:S(2)}) collective-permute-start(f32[2,3,8,1024]{3,2,1,0:T(8,128)S(1)} %add.2.refs_0_), channel_id=1, source_target_pairs={{0,2},{1,3},{2,0},{3,1},{4,6},{5,7},{6,4},{7,5},{8,10},{9,11},{10,... | collective-permute-start | bytes 589832 | tf_op jit(solution)/shard_map/ppermute | solution.py:536
  15.0 13.5 %collective-permute-start.8 = (f32[128,8,128]{2,1,0:T(8,128)S(1)}, f32[128,8,128]{2,1,0:T(8,128)S(1)}, u32[]{:S(2)}, u32[]{:S(2)}) collective-permute-start(f32[128,8,128]{2,1,0:T(8,128)S(1)} %take.3.refs_1_.own_ref), channel_id=1, source_target_pairs={{0,24},{4,12},{8,0},{12,20},{16,8},{20,28},{24,16},{28,4},{1,25},{... | collective-permute-start | bytes 1572872 | tf_op jit(solution)/shard_map/ppermute | solution.py:532
  15.9 14.4 %collective-permute-start.9 = (f32[128,8,128]{2,1,0:T(8,128)S(1)}, f32[128,8,128]{2,1,0:T(8,128)S(1)}, u32[]{:S(2)}, u32[]{:S(2)}) collective-permute-start(f32[128,8,128]{2,1,0:T(8,128)S(1)} %take.2.refs_0_.own_ref), channel_id=1, source_target_pairs={{0,4},{4,0},{8,12},{12,8},{16,20},{20,16},{24,28},{28,24},{1,5},{5... | collective-permute-start | bytes 1572872 | tf_op jit(solution)/shard_map/ppermute | solution.py:41
  25.5 4.8 %collective-permute-start.7 = (f32[128,8,128]{2,1,0:T(8,128)S(1)}, f32[128,8,128]{2,1,0:T(8,128)S(1)}, u32[]{:S(2)}, u32[]{:S(2)}) collective-permute-start(f32[128,8,128]{2,1,0:T(8,128)S(1)} %join.3), channel_id=1, source_target_pairs={{0,4},{4,0},{8,12},{12,8},{16,20},{20,16},{24,28},{28,24},{1,5},{5... | collective-permute-start | bytes 1572872 | tf_op jit(solution)/shard_map/ppermute | solution.py:41
  26.0 5.7 %collective-permute-start.5 = (f32[3,8,1024]{2,1,0:T(8,128)S(1)}, f32[3,8,1024]{2,1,0:T(8,128)S(1)}, u32[]{:S(2)}, u32[]{:S(2)}) collective-permute-start(f32[3,8,1024]{2,1,0:T(8,128)S(1)} %get-tuple-element.17.refs_7_), channel_id=1, source_target_pairs={{0,24},{4,12},{8,0},{12,20},{16,8},{20,28},{24,16},{28,4},{1,25},{... | collective-permute-start | bytes 294920 | tf_op jit(solution)/shard_map/ppermute | solution.py:532
  26.0 6.7 %collective-permute-start.3 = (f32[3,8,1024]{2,1,0:T(8,128)S(1)}, f32[3,8,1024]{2,1,0:T(8,128)S(1)}, u32[]{:S(2)}, u32[]{:S(2)}) collective-permute-start(f32[3,8,1024]{2,1,0:T(8,128)S(1)} %get-tuple-element.17.refs_7_), channel_id=1, source_target_pairs={{0,20},{4,16},{8,28},{12,24},{16,4},{20,0},{24,12},{28,8},{1,21},{... | collective-permute-start | bytes 294920 | tf_op jit(solution)/shard_map/ppermute | solution.py:533
  28.5 5.7 %collective-permute-start.4 = (f32[3,8,1024]{2,1,0:T(8,128)S(1)}, f32[3,8,1024]{2,1,0:T(8,128)S(1)}, u32[]{:S(2)}, u32[]{:S(2)}) collective-permute-start(f32[3,8,1024]{2,1,0:T(8,128)S(1)} %get-tuple-element.18.refs_1_.refs_2_.refs_3_), channel_id=1, source_target_pairs={{0,8},{4,28},{8,16},{12,4},{16,24},{20,12},{24,0},{28,20},{1,9},{5... | collective-permute-start | bytes 294920 | tf_op jit(solution)/shard_map/ppermute | solution.py:531
  34.3 1.6 %collective-permute-start.10 = (f32[9,8,1024]{2,1,0:T(8,128)S(1)}, f32[9,8,1024]{2,1,0:T(8,128)S(1)}, u32[]{:S(2)}, u32[]{:S(2)}) collective-permute-start(f32[9,8,1024]{2,1,0:T(8,128)S(1)} %join.4.refs_1_), channel_id=1, source_target_pairs={{0,4},{4,0},{8,12},{12,8},{16,20},{20,16},{24,28},{28,24},{1,5},{5... | collective-permute-start | bytes 884744 | tf_op jit(solution)/shard_map/ppermute | solution.py:41
  34.4 2.8 %collective-permute-start.11 = (f32[128,8,128]{2,1,0:T(8,128)S(1)}, f32[128,8,128]{2,1,0:T(8,128)S(1)}, u32[]{:S(2)}, u32[]{:S(2)}) collective-permute-start(f32[128,8,128]{2,1,0:T(8,128)S(1)} %join.5), channel_id=1, source_target_pairs={{0,4},{4,0},{8,12},{12,8},{16,20},{20,16},{24,28},{28,24},{1,5},{5... | collective-permute-start | bytes 1572872 | tf_op jit(solution)/shard_map/ppermute | solution.py:41
  39.0 4.9 %collective-permute-start.12 = (f32[3,8,1024]{2,1,0:T(8,128)S(1)}, f32[3,8,1024]{2,1,0:T(8,128)S(1)}, u32[]{:S(2)}, u32[]{:S(2)}) collective-permute-start(f32[3,8,1024]{2,1,0:T(8,128)S(1)} %density.1.a_ref), channel_id=1, source_target_pairs={{0,1},{1,0},{2,3},{3,2},{4,5},{5,4},{6,7},{7,6},{8,9},{9,8},{10,11... | collective-permute-start | bytes 294920 | tf_op jit(solution)/shard_map/ppermute | solution.py:536
  43.9 7.1 %collective-permute-start.13 = (f32[3,8,1024]{2,1,0:T(8,128)S(1)}, f32[3,8,1024]{2,1,0:T(8,128)S(1)}, u32[]{:S(2)}, u32[]{:S(2)}) collective-permute-start(f32[3,8,1024]{2,1,0:T(8,128)S(1)} %add.3.refs_0_), channel_id=1, source_target_pairs={{0,2},{1,3},{2,0},{3,1},{4,6},{5,7},{6,4},{7,5},{8,10},{9,11},{10,... | collective-permute-start | bytes 294920 | tf_op jit(solution)/shard_map/ppermute | solution.py:536
